TPU v7x, 128 devices: a whole 4x4x4 slice. The times are simulated.
128 devices in a mesh: wide: 16 (over y_hi, x, core), narrow: 8 (over z, y_lo).
Axes of the slice: x: 4, y: 4 (y_hi: 2, y_lo: 2; y = y_hi * 2 + y_lo), z: 4, core: 2. Of those that a mesh axis runs over, the one named last changes fastest.
Arguments:
- right_side: float32 [3, 128, 512, 256], P(None, 'wide', 'narrow'), may hold values from -6 to 6
- start_guess: float32 [3, 128, 512, 256], P(None, 'wide', 'narrow'), may hold values from -6 to 6
- reaction: float32 [128, 512, 256], P('wide', 'narrow'), may hold values from 2.5 to 5
- coarse_reaction: float32 [64, 256, 128], P('wide'), may hold values from 2.5 to 5
- rest_x: float32 [64, 5], replicated, may hold values from 0.1 to 0.8
- rest_y: float32 [256, 5], replicated, may hold values from 0.1 to 0.8
- rest_z: float32 [128, 5], replicated, may hold values from 0.1 to 0.8
- fine_bounds: float32 [2], replicated, may hold values from 3 to 20, as said below
- coarse_bounds: float32 [2], replicated, may hold values from 0.8 to 20, as said below
Outputs:
- solution: float32 [3, 128, 512, 256], P(None, 'wide', 'narrow')
- coarse_correction: float32 [3, 64, 256, 128], P(None, 'wide')
Inputs may be any that keep to these rules, and one draw needn't show every extreme that they name: fine_bounds[1] lies above every eigenvalue of the fine operator and fine_bounds[0] below fine_bounds[1]. coarse_bounds[1] lies above every eigenvalue of the coarse operator and coarse_bounds[0] below coarse_bounds[1].
All inputs are finite; a program needn't handle non-finite values.
Results may differ from a plain program's by a relative error of at most 0.0003.
Values sent between devices are 32-bit elements; how exact they have to be, the bound alone decides.
No kernel may reach another device: no remote copies, remote signals or barrier semaphores. Data moves between devices by JAX's collectives and lax.ppermute only.
A program may use at most 128 MiB of HBM per device.

v0:
```python
import jax
import jax.numpy as jnp
from jax import lax
from jax.experimental import pallas as pl
from jax.experimental.pallas import tpu as pltpu
from jax.sharding import PartitionSpec as P

F32 = jnp.float32
LANES = 128
SUB = 8
RIM = 4
PAD = 8
VMEM_LIMIT = 48 * 1024 * 1024


def params():
    return pltpu.CompilerParams(vmem_limit_bytes=VMEM_LIMIT)


def swap_near(x, axis):
    count = lax.axis_size(axis)
    return lax.ppermute(x, axis, [(i, i ^ 1) for i in range(count)])


def swap_far(x, axis):
    count = lax.axis_size(axis)
    up = [(i, i + 1) for i in range(1, count - 1, 2)]
    return lax.ppermute(x, axis, up + [(j, i) for i, j in up])


def is_even(axis):
    return lax.rem(lax.axis_index(axis), 2) == 0


def lane_index():
    return lax.broadcasted_iota(jnp.int32, (SUB, LANES), 1)


def z_next(parts, last):
    rolled = [pltpu.roll(part, LANES - 1, 1) for part in parts]
    beyond = rolled[1:] + [jnp.zeros_like(parts[0])]
    return [jnp.where(last, b, r) for r, b in zip(rolled, beyond)]


def z_before(parts, first):
    rolled = [pltpu.roll(part, 1, 1) for part in parts]
    beyond = [jnp.zeros_like(parts[0])] + rolled[:-1]
    return [jnp.where(first, b, r) for r, b in zip(rolled, beyond)]


def each(fn, *lists):
    return [fn(*items) for items in zip(*lists)]


def add(a, b):
    return each(lambda p, q: p + q, a, b)


def sub(a, b):
    return each(lambda p, q: p - q, a, b)


def eighth(a):
    return each(lambda p: 0.125 * p, a)


class Plane:
    def __init__(self, load, edges):
        first, last = edges
        v = [load(c, 0) for c in range(3)]
        above = [load(c, 1) for c in range(3)]
        below = [load(c, -1) for c in range(3)]
        dy = [eighth(sub(above[c], below[c])) for c in range(3)]
        next_0, before_0 = z_next(v[0], last), z_before(v[0], first)
        next_2, before_2 = z_next(v[2], last), z_before(v[2], first)
        slope = [
            add(dy[1], eighth(sub(next_2, before_2))),
            dy[0],
            eighth(sub(next_0, before_0)),
        ]
        self.v = v
        self.ahead = [add(v[c], slope[c]) for c in range(3)]
        self.behind = [sub(v[c], slope[c]) for c in range(3)]
        self.parts = (above, below, dy, next_0, before_0, edges)

    def inner(self, diagonal):
        above, below, dy, next_0, before_0, (first, last) = self.parts
        v = self.v
        out = []
        for c in range(3):
            if c == 0:
                along_z = add(next_0, before_0)
            else:
                other = dy[2] if c == 1 else dy[1]
                along_z = add(
                    z_next(sub(v[c], other), last), z_before(add(v[c], other), first)
                )
            total = add(add(above[c], below[c]), along_z)
            out.append(each(lambda d, p, q: d * p - q, diagonal, v[c], total))
        return out


def applied(before, plane, after, diagonal):
    out = plane.inner(diagonal)
    for c in range(3):
        if after is not None:
            out[c] = sub(out[c], after.behind[c])
        if before is not None:
            out[c] = sub(out[c], before.ahead[c])
    return out


def edge_masks():
    lane = lane_index()
    return lane == 0, lane == LANES - 1


def inside_rows(start, own, axis):
    row = start + lax.broadcasted_iota(jnp.int32, (SUB, LANES), 0)
    place = lax.axis_index(axis)
    low = jnp.where(place == 0, RIM, 0)
    high = jnp.where(place == lax.axis_size(axis) - 1, RIM + own, own + 2 * RIM)
    return (row >= low) & (row < high)


def pack_y_kernel(u_lo, u_hi, b_lo, b_hi, s_lo, s_hi, near, far):
    width = u_lo.shape[1]

    def pack(out, u, b, s, low):
        u_rows = slice(0, 3) if low else slice(5, 8)
        two = slice(0, 2) if low else slice(6, 8)
        for h in range(2):
            lanes = slice(h * LANES, (h + 1) * LANES)
            for x in range(width):
                for c in range(3):
                    k = c * width + x
                    out[h, 3 * k : 3 * k + 3, :] = u[c, x, u_rows, lanes]
                    base = 9 * width + 2 * k
                    out[h, base : base + 2, :] = b[c, x, two, lanes]
                base = 15 * width + 2 * x
                out[h, base : base + 2, :] = s[x, two, lanes]

    even = is_even("narrow")

    @pl.when(even)
    def _():
        pack(near, u_hi, b_hi, s_hi, False)
        pack(far, u_lo, b_lo, s_lo, True)

    @pl.when(jnp.logical_not(even))
    def _():
        pack(near, u_lo, b_lo, s_lo, True)
        pack(far, u_hi, b_hi, s_hi, False)


def pack_y(u, b, s):
    _, width, height, depth = u.shape
    last = height // SUB - 1
    block = pl.BlockSpec((3, width, SUB, depth), lambda i: (0, 0, 0, 0))
    block_last = pl.BlockSpec((3, width, SUB, depth), lambda i: (0, 0, last, 0))
    plane = pl.BlockSpec((width, SUB, depth), lambda i: (0, 0, 0))
    plane_last = pl.BlockSpec((width, SUB, depth), lambda i: (0, last, 0))
    rows = 17 * width
    out = jax.ShapeDtypeStruct((2, rows, LANES), F32)
    whole = pl.BlockSpec((2, rows, LANES), lambda i: (0, 0, 0))
    return pl.pallas_call(
        pack_y_kernel,
        grid=(1,),
        in_specs=[block, block_last, block, block_last, plane, plane_last],
        out_specs=[whole, whole],
        out_shape=[out, out],
        compiler_params=params(),
        name="pack_y",
    )(u, u, b, b, s, s)


def residual_kernel(u, b, s, got_near, got_far, r0, s_ext, near, far, ue, be):
    _, width, height, _ = u.shape
    own = PAD + RIM
    tiles = (height + 2 * RIM) // SUB
    for h in range(2):
        lanes = slice(h * LANES, (h + 1) * LANES)

        def fill(t, carry, h=h, lanes=lanes):
            rows = pl.ds(pl.multiple_of(t * SUB, SUB), SUB)
            to = pl.ds(own + t * SUB, SUB)
            for x in range(width):
                for c in range(3):
                    ue[c, x, h, to, :] = u[c, x, rows, lanes]
                    be[c, x, h, to, :] = b[c, x, rows, lanes]
                s_ext[x, h, to, :] = s[x, rows, lanes]
            return carry

        lax.fori_loop(0, height // SUB, fill, 0)

    def place(low, high):
        for h in range(2):
            for x in range(width):
                for c in range(3):
                    k = c * width + x
                    ue[c, x, h, own - 3 : own, :] = low[h, 3 * k : 3 * k + 3, :]
                    ue[c, x, h, own + height : own + height + 3, :] = high[h, 3 * k : 3 * k + 3, :]
                    base = 9 * width + 2 * k
                    be[c, x, h, own - 2 : own, :] = low[h, base : base + 2, :]
                    be[c, x, h, own + height : own + height + 2, :] = high[h, base : base + 2, :]
                base = 15 * width + 2 * x
                s_ext[x, h, own - 2 : own, :] = low[h, base : base + 2, :]
                s_ext[x, h, own + height : own + height + 2, :] = high[h, base : base + 2, :]

    even = is_even("narrow")

    @pl.when(even)
    def _():
        place(got_far, got_near)

    @pl.when(jnp.logical_not(even))
    def _():
        place(got_near, got_far)

    edges = edge_masks()

    def step(t, carry):
        start = PAD + t * SUB
        inside = inside_rows(t * SUB, height, "narrow")

        def plane(x):
            return Plane(
                lambda c, dy: [ue[c, x, h, pl.ds(start + dy, SUB), :] for h in range(2)],
                edges,
            )

        before, here = None, plane(0)
        rows = pl.ds(start, SUB)
        for x in range(width):
            after = plane(x + 1) if x + 1 < width else None
            diagonal = [6.0 + s_ext[x, h, rows, :] for h in range(2)]
            au = applied(before, here, after, diagonal)
            for c in range(3):
                for h in range(2):
                    r0[c, x, h, rows, :] = jnp.where(inside, be[c, x, h, rows, :] - au[c][h], 0.0)
            before, here = here, after
        return carry

    lax.fori_loop(0, tiles, step, 0)

    window = slice(PAD, PAD + height + 2 * RIM)

    def pack(out, edge, second):
        for c in range(3):
            out[c] = r0[c, edge, :, window, :]
            out[3 + c] = r0[c, second, :, window, :]
            out[6 + c] = ue[c, edge, :, window, :]
        out[9] = s_ext[edge, :, window, :]

    even_x = is_even("wide")

    @pl.when(even_x)
    def _():
        pack(near, width - 1, width - 2)
        pack(far, 0, 1)

    @pl.when(jnp.logical_not(even_x))
    def _():
        pack(near, 0, 1)
        pack(far, width - 1, width - 2)


def residual(u, b, s, got_near, got_far):
    _, width, height, _ = u.shape
    padded = height + 2 * (RIM + PAD)
    side = jax.ShapeDtypeStruct((10, 2, height + 2 * RIM, LANES), F32)
    return pl.pallas_call(
        residual_kernel,
        out_shape=[
            jax.ShapeDtypeStruct((3, width, 2, padded, LANES), F32),
            jax.ShapeDtypeStruct((width, 2, padded, LANES), F32),
            side,
            side,
        ],
        scratch_shapes=[
            pltpu.VMEM((3, width, 2, padded, LANES), F32),
            pltpu.VMEM((3, width, 2, padded, LANES), F32),
        ],
        compiler_params=params(),
        name="residual",
    )(u, b, s, got_near, got_far)


def full(value):
    return jnp.full((SUB, LANES), value, F32)


def chebyshev_numbers(bounds, steps):
    low, high = full(bounds[0]), full(bounds[1])
    middle = (high + low) / 2.0
    radius = (high - low) / 2.0
    stretch = middle / radius
    rho = 1.0 / stretch
    factors = []
    for _ in range(steps - 1):
        rho_next = 1.0 / (2.0 * stretch - rho)
        factors.append((rho_next * rho, 2.0 * rho_next / radius))
        rho = rho_next
    return 1.0 / middle, factors


def z_matrix(rest_zt):
    shape = (2 * LANES, LANES)
    offset = lax.broadcasted_iota(jnp.int32, shape, 0) - 2 * lax.broadcasted_iota(jnp.int32, shape, 1) + 2
    out = jnp.zeros(shape, F32)
    for a in range(5):
        out = out + jnp.where(offset == a, rest_zt[a : a + 1, :], 0.0)
    return out


def y_weights(rest_y, a, rows, own):
    start = pl.multiple_of(lax.axis_index("narrow") * own, SUB)
    return jnp.broadcast_to(rest_y[pl.ds(start, rows), a : a + 1], (rows, LANES))


def smooth_kernel(
    bounds, rest_x, r0p, s_ext, got_near, got_far, sent_near, sent_far, u, rest_y, rest_zt,
    smooth, partial, near, far, left, right, u_left, u_right, r0, d1, r1, r2, t_pad, zr,
):
    _, width, height, _ = u.shape
    window = slice(PAD, PAD + height + 2 * RIM)
    tiles = (height + 2 * RIM) // SUB
    even_x = is_even("wide")
    zr[...] = z_matrix(rest_zt)

    def place(from_left, from_right, mine_left, mine_right):
        for k in range(10):
            left[k, :, window, :] = from_left[k]
            right[k, :, window, :] = from_right[k]
        for c in range(3):
            u_left[c, :, window, :] = mine_left[6 + c]
            u_right[c, :, window, :] = mine_right[6 + c]

    @pl.when(even_x)
    def _():
        place(got_far, got_near, sent_far, sent_near)

    @pl.when(jnp.logical_not(even_x))
    def _():
        place(got_near, got_far, sent_near, sent_far)

    edges = edge_masks()
    place_x = lax.axis_index("wide")
    has_left = place_x > 0
    has_right = place_x < lax.axis_size("wide") - 1
    inverse, factors = chebyshev_numbers(bounds, 2)
    factor_d = factors[0][0] * inverse
    factor_r = factors[0][1]

    def fix(t, carry):
        start = PAD + t * SUB
        rows = pl.ds(start, SUB)
        inside = inside_rows(t * SUB, height, "narrow")

        def plane(ref, first):
            return Plane(
                lambda c, dy: [ref[first + c, h, pl.ds(start + dy, SUB), :] for h in range(2)],
                edges,
            )

        out_left = plane(left, 6)
        in_left = plane(u_left, 0)
        in_right = plane(u_right, 0)
        out_right = plane(right, 6)
        inside_left = inside & has_left
        inside_right = inside & has_right
        for c in range(3):
            for h in range(2):
                for x in range(1, width - 1):
                    r0[c, 2 + x, h, rows, :] = r0p[c, x, h, rows, :]
                r0[c, 0, h, rows, :] = left[3 + c, h, rows, :]
                r0[c, 1, h, rows, :] = jnp.where(
                    inside_left, left[c, h, rows, :] + in_left.behind[c][h], 0.0
                )
                r0[c, 2, h, rows, :] = jnp.where(
                    inside, r0p[c, 0, h, rows, :] + out_left.ahead[c][h], 0.0
                )
                r0[c, width + 1, h, rows, :] = jnp.where(
                    inside, r0p[c, width - 1, h, rows, :] + out_right.behind[c][h], 0.0
                )
                r0[c, width + 2, h, rows, :] = jnp.where(
                    inside_right, right[c, h, rows, :] + in_right.ahead[c][h], 0.0
                )
                r0[c, width + 3, h, rows, :] = right[3 + c, h, rows, :]
        return carry

    lax.fori_loop(0, tiles, fix, 0)

    def first_step(t, carry):
        start = PAD + t * SUB
        rows = pl.ds(start, SUB)
        inside = inside_rows(t * SUB, height, "narrow")

        def plane(x):
            return Plane(
                lambda c, dy: [r0[c, x + 2, h, pl.ds(start + dy, SUB), :] for h in range(2)],
                edges,
            )

        before, here = plane(-2), plane(-1)
        for x in range(-1, width + 1):
            after = plane(x + 1)
            keep = inside & has_left if x < 0 else inside & has_right if x == width else inside
            source = left.at[9] if x < 0 else right.at[9] if x == width else s_ext.at[x]
            diagonal = [6.0 + source[h, rows, :] for h in range(2)]
            ar = applied(before, here, after, diagonal)
            for c in range(3):
                for h in range(2):
                    old = here.v[c][h]
                    new = old - inverse * ar[c][h]
                    d1[c, x + 1, h, rows, :] = jnp.where(keep, factor_d * old + factor_r * new, 0.0)
                    if 0 <= x < width:
                        r1[c, x, h, rows, :] = new
            before, here = here, after
        return carry

    lax.fori_loop(0, tiles, first_step, 0)

    def second_step(t, carry):
        start = PAD + RIM + t * SUB
        rows = pl.ds(start, SUB)
        to = pl.ds(pl.multiple_of(t * SUB, SUB), SUB)

        def plane(x):
            return Plane(
                lambda c, dy: [d1[c, x + 1, h, pl.ds(start + dy, SUB), :] for h in range(2)],
                edges,
            )

        before, here = plane(-1), plane(0)
        for x in range(width):
            after = plane(x + 1)
            diagonal = [6.0 + s_ext[x, h, rows, :] for h in range(2)]
            ad = applied(before, here, after, diagonal)
            for c in range(3):
                for h in range(2):
                    lanes = slice(h * LANES, (h + 1) * LANES)
                    r2[c, x, h, to, :] = r1[c, x, h, rows, :] - ad[c][h]
                    step = inverse * r0[c, x + 2, h, rows, :] + here.v[c][h]
                    smooth[c, x, to, lanes] = u[c, x, to, lanes] + step
            before, here = here, after
        return carry

    lax.fori_loop(0, height // SUB, second_step, 0)

    coarse_width = width // 2
    coarse_height = height // 2
    coarse_rows = coarse_height + 2 * RIM
    first_weight = place_x * coarse_width
    lead = 2 * RIM + 2
    for c in range(3):
        for i in range(-1, coarse_width + 1):
            k = c * (coarse_width + 2) + i + 1
            terms = [(a, 2 * i - 2 + a) for a in range(5) if 0 <= 2 * i - 2 + a < width]
            halves = []
            for h in range(2):
                total = None
                for a, x in terms:
                    piece = rest_x[first_weight + i + 1, a] * r2[c, x, h]
                    total = piece if total is None else total + piece
                halves.append(total)
            joined = jnp.concatenate(halves, axis=1)
            t_pad[k, 0:lead, :] = jnp.zeros((lead, LANES), F32)
            t_pad[k, lead + height :, :] = jnp.zeros((t_pad.shape[1] - lead - height, LANES), F32)
            t_pad[k, lead : lead + height, :] = jnp.dot(
                joined, zr[...], precision=lax.Precision.HIGHEST, preferred_element_type=F32
            )
    weights = [y_weights(rest_y, a, coarse_rows, coarse_height) for a in range(5)]
    even_y = is_even("narrow")
    for c in range(3):
        for i in range(coarse_width + 2):
            k = c * (coarse_width + 2) + i
            total = None
            for a in range(5):
                piece = weights[a] * t_pad[k, pl.ds(a, coarse_rows, stride=2), :]
                total = piece if total is None else total + piece
            partial[c, i] = total

    def send(out, first):
        for c in range(3):
            for i in range(coarse_width + 2):
                out[c * (coarse_width + 2) + i] = partial[c, i, first : first + SUB, :]

    @pl.when(even_y)
    def _():
        send(near, coarse_rows - SUB)
        send(far, 0)

    @pl.when(jnp.logical_not(even_y))
    def _():
        send(near, 0)
        send(far, coarse_rows - SUB)


SMEM = pl.BlockSpec(memory_space=pltpu.SMEM)
VMEM = pl.BlockSpec(memory_space=pltpu.VMEM)


def smoothing(bounds, rest_x, r0p, s_ext, got_near, got_far, sent_near, sent_far, u, rest_y, rest_zt):
    _, width, height, depth = u.shape
    padded = height + 2 * (RIM + PAD)
    planes = 3 * (width // 2 + 2)
    coarse_rows = height // 2 + 2 * RIM
    tile = jax.ShapeDtypeStruct((planes, SUB, LANES), F32)

    def field(*lead):
        return pltpu.VMEM((*lead, 2, padded, LANES), F32)

    return pl.pallas_call(
        smooth_kernel,
        in_specs=[SMEM, SMEM] + [VMEM] * 9,
        out_shape=[
            jax.ShapeDtypeStruct((3, width, height, depth), F32),
            jax.ShapeDtypeStruct((3, width // 2 + 2, coarse_rows, LANES), F32),
            tile,
            tile,
        ],
        scratch_shapes=[
            field(10),
            field(10),
            field(3),
            field(3),
            field(3, width + 4),
            field(3, width + 2),
            field(3, width),
            pltpu.VMEM((3, width, 2, height, LANES), F32),
            pltpu.VMEM((planes, 2 * coarse_rows + 2 * SUB, LANES), F32),
            pltpu.VMEM((2 * LANES, LANES), F32),
        ],
        compiler_params=params(),
        name="smoothing",
    )(bounds, rest_x, r0p, s_ext, got_near, got_far, sent_near, sent_far, u, rest_y, rest_zt)


def rows_kernel(partial, got_near, got_far, s, q, s_win, near, far):
    _, planes, rows, _ = partial.shape
    own = rows - 2 * RIM
    coarse_width = planes - 2
    n = lax.axis_index("narrow")
    even_y = is_even("narrow")
    q[:, :, SUB : rows - SUB, :] = partial[:, :, SUB : rows - SUB, :]

    def join(low, high):
        for c in range(3):
            for i in range(planes):
                k = c * planes + i
                q[c, i, 0:SUB, :] = partial[c, i, 0:SUB, :] + low[k]
                q[c, i, rows - SUB :, :] = partial[c, i, rows - SUB :, :] + high[k]

    @pl.when(even_y)
    def _():
        join(got_far, got_near)

    @pl.when(jnp.logical_not(even_y))
    def _():
        join(got_near, got_far)

    total = s.shape[1]
    start = pl.multiple_of(n * own, SUB)
    before = pl.multiple_of(jnp.maximum(start - SUB, 0), SUB)
    after = pl.multiple_of(jnp.minimum(start + own, total - SUB), SUB)
    for x in range(coarse_width):
        s_win[x, RIM : RIM + own, :] = s[x, pl.ds(start, own), :]
        s_win[x, 0:RIM, :] = s[x, pl.ds(before, SUB), :][SUB - RIM :, :]
        s_win[x, RIM + own :, :] = s[x, pl.ds(after, SUB), :][0:RIM, :]

    def pack(out, to_left):
        first = 0 if to_left else 2
        for c in range(3):
            for k in range(coarse_width):
                out[c * coarse_width + k] = q[c, first + k]
        edge = 0 if to_left else coarse_width - 2
        for k in range(2):
            out[3 * coarse_width + k] = s_win[edge + k]

    even_x = is_even("wide")

    @pl.when(even_x)
    def _():
        pack(near, False)
        pack(far, True)

    @pl.when(jnp.logical_not(even_x))
    def _():
        pack(near, True)
        pack(far, False)


def rows(partial, got_near, got_far, s):
    _, planes, height, _ = partial.shape
    width = planes - 2
    side = jax.ShapeDtypeStruct((3 * width + 2, height, LANES), F32)
    return pl.pallas_call(
        rows_kernel,
        out_shape=[
            jax.ShapeDtypeStruct(partial.shape, F32),
            jax.ShapeDtypeStruct((width, height, LANES), F32),
            side,
            side,
        ],
        compiler_params=params(),
        name="coarse_rows",
    )(partial, got_near, got_far, s)


def coarse_kernel(bounds, q, s_win, got_near, got_far, out, own_out, near, far, left, right, r, d, total, sc):
    _, planes, height, _ = q.shape
    width = planes - 2
    own = height - 2 * RIM
    tiles = height // SUB
    window = slice(PAD, PAD + height)
    even_x = is_even("wide")
    place_x = lax.axis_index("wide")
    has_left = place_x > 0
    has_right = place_x < lax.axis_size("wide") - 1
    inverse, factors = chebyshev_numbers(bounds, 4)
    edges = edge_masks()
    reach = 3

    def place(from_left, from_right):
        left[...] = from_left[...]
        right[...] = from_right[...]

    @pl.when(even_x)
    def _():
        place(got_far, got_near)

    @pl.when(jnp.logical_not(even_x))
    def _():
        place(got_near, got_far)

    for k in range(2):
        sc[k] = left[3 * width + k]
        sc[width + 2 + k] = right[3 * width + k]
    for x in range(width):
        sc[x + 2] = s_win[x]

    def start_rows(t, carry):
        rows = pl.ds(pl.multiple_of(t * SUB, SUB), SUB)
        to = pl.ds(pl.multiple_of(PAD + t * SUB, SUB), SUB)
        for c in range(3):
            for i in range(-reach, width + reach):
                value = None
                if -1 <= i <= width:
                    value = q[c, i + 1, rows, :]
                if i <= 0:
                    other = left[c * width + i + reach, rows, :]
                    value = other if value is None else value + other
                if i >= width - 1:
                    other = right[c * width + i - width + 1, rows, :]
                    value = other if value is None else value + other
                r[c, i + reach, to, :] = value
                first = inverse * value
                d[c, i + reach, to, :] = first
                if 0 <= i < width:
                    total[c, i, to, :] = first
        return carry

    lax.fori_loop(0, tiles, start_rows, 0)

    for k in range(3):
        factor_d, factor_r = factors[k]
        rim = reach - 1 - k

        def residual_step(t, carry, rim=rim):
            start = PAD + t * SUB
            rows = pl.ds(start, SUB)
            inside = inside_rows(t * SUB, own, "narrow")

            def plane(x):
                return Plane(lambda c, dy: [d[c, x + reach, pl.ds(start + dy, SUB), :]], edges)

            before, here = plane(-rim - 1), plane(-rim)
            for x in range(-rim, width + rim):
                after = plane(x + 1)
                keep = inside & has_left if x < 0 else inside & has_right if x >= width else inside
                ad = applied(before, here, after, [6.0 + sc[x + 2, pl.ds(t * SUB, SUB), :]])
                for c in range(3):
                    new = r[c, x + reach, rows, :] - ad[c][0]
                    r[c, x + reach, rows, :] = jnp.where(keep, new, 0.0)
                before, here = here, after
            return carry

        lax.fori_loop(0, tiles, residual_step, 0)

        def direction_step(t, carry, rim=rim, factor_d=factor_d, factor_r=factor_r):
            rows = pl.ds(pl.multiple_of(PAD + t * SUB, SUB), SUB)
            for c in range(3):
                for x in range(-rim, width + rim):
                    new = factor_d * d[c, x + reach, rows, :] + factor_r * r[c, x + reach, rows, :]
                    d[c, x + reach, rows, :] = new
                    if 0 <= x < width:
                        total[c, x, rows, :] = total[c, x, rows, :] + new
            return carry

        lax.fori_loop(0, tiles, direction_step, 0)

    for c in range(3):
        for x in range(width):
            out[c, x] = total[c, x, window, :]
            own_out[c, x] = total[c, x, PAD + RIM : PAD + RIM + own, :]

    def send(ref, x):
        for c in range(3):
            ref[c] = total[c, x, window, :]

    @pl.when(even_x)
    def _():
        send(near, width - 1)
        send(far, 0)

    @pl.when(jnp.logical_not(even_x))
    def _():
        send(near, 0)
        send(far, width - 1)


def coarse_solve(bounds, q, s_win, got_near, got_far):
    _, planes, height, _ = q.shape
    width = planes - 2
    side = (3 * width + 2, height, LANES)
    edge = jax.ShapeDtypeStruct((3, height, LANES), F32)

    def field(count):
        return pltpu.VMEM((3, count, height + 2 * PAD, LANES), F32)

    return pl.pallas_call(
        coarse_kernel,
        in_specs=[SMEM] + [VMEM] * 4,
        out_shape=[
            jax.ShapeDtypeStruct((3, width, height, LANES), F32),
            jax.ShapeDtypeStruct((3, width, height - 2 * RIM, LANES), F32),
            edge,
            edge,
        ],
        scratch_shapes=[
            pltpu.VMEM(side, F32),
            pltpu.VMEM(side, F32),
            field(width + 6),
            field(width + 6),
            field(width),
            pltpu.VMEM((width + 4, height, LANES), F32),
        ],
        compiler_params=params(),
        name="coarse_solve",
    )(bounds, q, s_win, got_near, got_far)


def prolong_kernel(rest_x, corr, got_near, got_far, smooth, rest_y, rest_zt, out, left, right, wy, col, grown):
    _, width, height, _ = corr.shape
    own = height - 2 * RIM
    fine_width = 2 * width
    even_x = is_even("wide")
    first_weight = lax.axis_index("wide") * width
    zr = z_matrix(rest_zt)
    for a in range(5):
        wy[a] = y_weights(rest_y, a, height, own)

    def place(from_left, from_right):
        left[...] = from_left[...]
        right[...] = from_right[...]

    @pl.when(even_x)
    def _():
        place(got_far, got_near)

    @pl.when(jnp.logical_not(even_x))
    def _():
        place(got_near, got_far)

    def row(c, i):
        return left[c] if i < 0 else right[c] if i == width else corr[c, i]

    for c in range(3):
        for x in range(fine_width):
            total = None
            for a in range(x % 2, 5, 2):
                i = (x + 2 - a) // 2
                piece = rest_x[first_weight + i + 1, a] * row(c, i)
                total = piece if total is None else total + piece
            col[...] = total

            def at(a, shift):
                rows = pl.ds(RIM + shift, own)
                return wy[a, rows, :] * col[rows, :]

            grown[x, pl.ds(0, own, stride=2), :] = at(0, 1) + at(2, 0) + at(4, -1)
            grown[x, pl.ds(1, own, stride=2), :] = at(1, 1) + at(3, 0)
        flat = grown[...].reshape(fine_width * 2 * own, LANES)
        wide = lax.dot_general(
            flat, zr, (((1,), (1,)), ((), ())), precision=lax.Precision.HIGHEST, preferred_element_type=F32
        )
        out[c] = smooth[c] + wide.reshape(fine_width, 2 * own, 2 * LANES)


def prolong(rest_x, corr, got_near, got_far, smooth, rest_y, rest_zt):
    _, width, height, _ = corr.shape
    own = height - 2 * RIM
    return pl.pallas_call(
        prolong_kernel,
        in_specs=[SMEM] + [VMEM] * 6,
        out_shape=jax.ShapeDtypeStruct(smooth.shape, F32),
        scratch_shapes=[
            pltpu.VMEM((3, height, LANES), F32),
            pltpu.VMEM((3, height, LANES), F32),
            pltpu.VMEM((5, height, LANES), F32),
            pltpu.VMEM((height, LANES), F32),
            pltpu.VMEM((2 * width, 2 * own, LANES), F32),
        ],
        compiler_params=params(),
        name="prolong",
    )(rest_x, corr, got_near, got_far, smooth, rest_y, rest_zt)


def gather(own):
    count = lax.axis_size("narrow")
    n = lax.axis_index("narrow")

    def ring(x, by):
        return lax.ppermute(x, "narrow", [(i, (i + by) % count) for i in range(count)])

    pair = swap_near(own, "narrow")
    low, high = ring(own, 2), ring(own, -2)
    pair_low, pair_high = ring(pair, 2), ring(pair, -2)
    far_own, far_pair = ring(low, 2), ring(pair_high, -2)
    blocks = [own, pair, low, high, pair_low, pair_high, far_own, far_pair]
    return blocks


def assemble_kernel(*refs):
    blocks, out = refs[:-1], refs[-1]
    count = len(blocks)
    n = lax.axis_index("narrow")
    m = n + 1 - 2 * lax.rem(n, 2)
    own = blocks[0].shape[2]
    sources = [n, m, n - 2, n + 2, m - 2, m + 2, n - 4, m + 4]
    for block, source in zip(blocks, sources):
        start = pl.multiple_of(lax.rem(source + count, count) * own, SUB)
        out[:, :, pl.ds(start, own), :] = block[...]


def assemble(blocks):
    three, width, own, lanes = blocks[0].shape
    return pl.pallas_call(
        assemble_kernel,
        out_shape=jax.ShapeDtypeStruct((three, width, own * len(blocks), lanes), F32),
        compiler_params=params(),
        name="assemble",
    )(*blocks)


def body(
    right_side,
    start_guess,
    reaction,
    coarse_reaction,
    rest_x,
    rest_y,
    rest_z,
    fine_bounds,
    coarse_bounds,
):
    x_weights = jnp.pad(rest_x, ((1, 1), (0, 0)))
    y_padded = jnp.pad(rest_y, ((RIM, RIM), (0, 0)))
    z_weights = rest_z.T
    near, far = pack_y(start_guess, right_side, reaction)
    got_far, got_near = swap_far(far, "narrow"), swap_near(near, "narrow")
    r0p, s_ext, near, far = residual(start_guess, right_side, reaction, got_near, got_far)
    got_far, got_near = swap_far(far, "wide"), swap_near(near, "wide")
    smooth, partial, near, far = smoothing(
        fine_bounds, x_weights, r0p, s_ext, got_near, got_far, near, far, start_guess, y_padded, z_weights
    )
    got_far, got_near = swap_far(far, "narrow"), swap_near(near, "narrow")
    q, s_win, near, far = rows(partial, got_near, got_far, coarse_reaction)
    got_far, got_near = swap_far(far, "wide"), swap_near(near, "wide")
    corr, own, near, far = coarse_solve(coarse_bounds, q, s_win, got_near, got_far)
    got_far, got_near = swap_far(far, "wide"), swap_near(near, "wide")
    solution_block = prolong(x_weights, corr, got_near, got_far, smooth, y_padded, z_weights)
    return solution_block, assemble(gather(own))


def solution(mesh):
    return jax.shard_map(
        body,
        mesh=mesh,
        in_specs=(
            P(None, "wide", "narrow", None),
            P(None, "wide", "narrow", None),
            P("wide", "narrow", None),
            P("wide", None, None),
            P(),
            P(),
            P(),
            P(),
            P(),
        ),
        out_specs=(P(None, "wide", "narrow", None), P(None, "wide", None, None)),
        check_vma=False,
    )
```

profile of v0, /device:TPU:16, one launch (start us, length us, event | category | flops | bytes accessed | tf_op | source)
XLA Modules:
  0.0 102.4 jit_solution(10861387902568181574)
XLA Ops:
  0.6 1.4 %copy-done = f32[3,8,64,256]{3,2,1,0:T(8,128)S(1)} copy-done((f32[3,8,64,256]{3,2,1,0:T(8,128)S(1)}, f32[3,8,64,256]{3,2,1,0:T(8,128)}, u32[]{:S(2)}) %copy-start) | copy-done | bytes 1572888
  2.0 1.4 %copy-done.1 = f32[3,8,64,256]{3,2,1,0:T(8,128)S(1)} copy-done((f32[3,8,64,256]{3,2,1,0:T(8,128)S(1)}, f32[3,8,64,256]{3,2,1,0:T(8,128)}, u32[]{:S(2)}) %copy-start.1) | copy-done | bytes 1572888
  4.6 1.4 %collective-permute-start = (f32[2,136,128]{2,1,0:T(8,128)S(1)}, f32[2,136,128]{2,1,0:T(8,128)S(1)}, u32[]{:S(2)}, u32[]{:S(2)}) collective-permute-start(f32[2,136,128]{2,1,0:T(8,128)S(1)} %get-tuple-element.20), channel_id=1, source_target_pairs={{0,1},{1,0},{2,3},{3,2},{4,5},{5,4},{6,7},{7,6},{8,9},{9,8},{10,11... | collective-permute-start | bytes 417800 | tf_op jit(solution)/shard_map/ppermute | solution.py:22
  6.8 3.3 %collective-permute-done.got_near = f32[2,136,128]{2,1,0:T(8,128)S(1)} collective-permute-done((f32[2,136,128]{2,1,0:T(8,128)S(1)}, f32[2,136,128]{2,1,0:T(8,128)S(1)}, u32[]{:S(2)}, u32[]{:S(2)}) %collective-permute-start) | collective-permute-done | bytes 139296 | tf_op jit(solution)/shard_map/ppermute | solution.py:22
  10.1 4.0 %residual.1 = (f32[3,8,2,88,128]{4,3,2,1,0:T(8,128)}, f32[8,2,88,128]{3,2,1,0:T(8,128)S(1)}, f32[10,2,72,128]{3,2,1,0:T(8,128)S(1)}, f32[10,2,72,128]{3,2,1,0:T(8,128)S(1)}) custom-call(f32[3,8,64,256]{3,2,1,0:T(8,128)S(1)} %copy-done, f32[3,8,64,256]{3,2,1,0:T(8,128)S(1)} %copy-done.1, f32[8,64,256]{2,1,0:T(8,128)S(1)} %copy-done.2, ...), custom_call_target="tpu_custom_call" | custom-call | tf_op jit(solution)/shard_map/residual/pallas_call | solution.py:272
  15.0 4.5 %collective-permute-start.3 = (f32[10,2,72,128]{3,2,1,0:T(8,128)S(1)}, f32[10,2,72,128]{3,2,1,0:T(8,128)S(1)}, u32[]{:S(2)}, u32[]{:S(2)}) collective-permute-start(f32[10,2,72,128]{3,2,1,0:T(8,128)S(1)} %get-tuple-element.25.sent_far), channel_id=1, source_target_pairs={{8,16},{24,32},{40,48},{56,64},{72,80},{88,96},{104,112},{16,8},{3... | collective-permute-start | bytes 2211848 | tf_op jit(solution)/shard_map/ppermute | solution.py:28
  19.9 11.5 %collective-permute-done.3.got_far = f32[10,2,72,128]{3,2,1,0:T(8,128)S(1)} collective-permute-done((f32[10,2,72,128]{3,2,1,0:T(8,128)S(1)}, f32[10,2,72,128]{3,2,1,0:T(8,128)S(1)}, u32[]{:S(2)}, u32[]{:S(2)}) %collective-permute-start.3) | collective-permute-done | bytes 737312 | tf_op jit(solution)/shard_map/ppermute | solution.py:28
  32.5 9.9 %smoothing.1 = (f32[3,8,64,256]{3,2,1,0:T(8,128)S(1)}, f32[3,6,40,128]{3,2,1,0:T(8,128)S(1)}, f32[18,8,128]{2,1,0:T(8,128)S(1)}, f32[18,8,128]{2,1,0:T(8,128)S(1)}) custom-call(f32[2]{0:T(128)S(1)} %copy-done.8, f32[66,5]{1,0:T(8,128)S(1)} %pad.8.rest_x, f32[3,8,2,88,128]{4,3,2,1,0:T(8,128)} %get-tuple-element.22.r0p, f32[8,2,88,128]{3,2,1,0:T(8,128)S(1)} %copy-done.4, ...), custom_call_target="tpu_custom_call" | custom-call | tf_op jit(solution)/shard_map/smoothing/pallas_call | solution.py:514
  42.4 5.7 %collective-permute-start.4 = (f32[18,8,128]{2,1,0:T(8,128)S(1)}, f32[18,8,128]{2,1,0:T(8,128)S(1)}, u32[]{:S(2)}, u32[]{:S(2)}) collective-permute-start(f32[18,8,128]{2,1,0:T(8,128)S(1)} %get-tuple-element.27), channel_id=1, source_target_pairs={{0,1},{1,0},{2,3},{3,2},{4,5},{5,4},{6,7},{7,6},{8,9},{9,8},{10,11... | collective-permute-start | bytes 221192 | tf_op jit(solution)/shard_map/ppermute | solution.py:22
  48.8 1.7 %collective-permute-done.4.got_near = f32[18,8,128]{2,1,0:T(8,128)S(1)} collective-permute-done((f32[18,8,128]{2,1,0:T(8,128)S(1)}, f32[18,8,128]{2,1,0:T(8,128)S(1)}, u32[]{:S(2)}, u32[]{:S(2)}) %collective-permute-start.4) | collective-permute-done | bytes 73760 | tf_op jit(solution)/shard_map/ppermute | solution.py:22
  50.7 4.0 %collective-permute-start.7 = (f32[14,40,128]{2,1,0:T(8,128)S(1)}, f32[14,40,128]{2,1,0:T(8,128)S(1)}, u32[]{:S(2)}, u32[]{:S(2)}) collective-permute-start(f32[14,40,128]{2,1,0:T(8,128)S(1)} %get-tuple-element.32), channel_id=1, source_target_pairs={{8,16},{24,32},{40,48},{56,64},{72,80},{88,96},{104,112},{16,8},{3... | collective-permute-start | bytes 860168 | tf_op jit(solution)/shard_map/ppermute | solution.py:28
  54.7 7.6 %collective-permute-done.7.got_far = f32[14,40,128]{2,1,0:T(8,128)S(1)} collective-permute-done((f32[14,40,128]{2,1,0:T(8,128)S(1)}, f32[14,40,128]{2,1,0:T(8,128)S(1)}, u32[]{:S(2)}, u32[]{:S(2)}) %collective-permute-start.7) | collective-permute-done | bytes 286752 | tf_op jit(solution)/shard_map/ppermute | solution.py:28
  62.3 3.1 %coarse_solve.1 = (f32[3,4,40,128]{3,2,1,0:T(8,128)S(1)}, f32[3,4,32,128]{3,2,1,0:T(8,128)S(1)}, f32[3,40,128]{2,1,0:T(8,128)S(1)}, f32[3,40,128]{2,1,0:T(8,128)S(1)}) custom-call(f32[2]{0:T(128)S(1)} %copy-done.7, f32[3,6,40,128]{3,2,1,0:T(8,128)S(1)} %get-tuple-element.29.q, f32[4,40,128]{2,1,0:T(8,128)S(1)} %get-tuple-element.30.s_win, ...), custom_call_target="tpu_custom_call" | custom-call | tf_op jit(solution)/shard_map/coarse_solve/pallas_call | solution.py:732
  65.4 5.3 %collective-permute-start.10 = (f32[3,4,32,128]{3,2,1,0:T(8,128)S(1)}, f32[3,4,32,128]{3,2,1,0:T(8,128)S(1)}, u32[]{:S(2)}, u32[]{:S(2)}) collective-permute-start(f32[3,4,32,128]{3,2,1,0:T(8,128)S(1)} %get-tuple-element.37.refs_0_), channel_id=1, source_target_pairs={{0,1},{1,0},{2,3},{3,2},{4,5},{5,4},{6,7},{7,6},{8,9},{9,8},{10,11... | collective-permute-start | bytes 589832 | tf_op jit(solution)/shard_map/ppermute | solution.py:22
  70.7 1.7 %collective-permute-start.11 = (f32[3,4,32,128]{3,2,1,0:T(8,128)S(1)}, f32[3,4,32,128]{3,2,1,0:T(8,128)S(1)}, u32[]{:S(2)}, u32[]{:S(2)}) collective-permute-start(f32[3,4,32,128]{3,2,1,0:T(8,128)S(1)} %get-tuple-element.37.refs_0_), channel_id=1, source_target_pairs={{0,2},{1,3},{2,4},{3,5},{4,6},{5,7},{6,0},{7,1},{8,10},{9,11},{10,... | collective-permute-start | bytes 589832 | tf_op jit(solution)/shard_map/ppermute | solution.py:825
  72.4 1.9 %collective-permute-done.10.refs_1_ = f32[3,4,32,128]{3,2,1,0:T(8,128)S(1)} collective-permute-done((f32[3,4,32,128]{3,2,1,0:T(8,128)S(1)}, f32[3,4,32,128]{3,2,1,0:T(8,128)S(1)}, u32[]{:S(2)}, u32[]{:S(2)}) %collective-permute-start.10) | collective-permute-done | bytes 196640 | tf_op jit(solution)/shard_map/ppermute | solution.py:22
  74.4 4.0 %collective-permute-start.14 = (f32[3,4,32,128]{3,2,1,0:T(8,128)S(1)}, f32[3,4,32,128]{3,2,1,0:T(8,128)S(1)}, u32[]{:S(2)}, u32[]{:S(2)}) collective-permute-start(f32[3,4,32,128]{3,2,1,0:T(8,128)S(1)} %collective-permute-done.10.refs_1_), channel_id=1, source_target_pairs={{0,6},{1,7},{2,0},{3,1},{4,2},{5,3},{6,4},{7,5},{8,14},{9,15},{10,... | collective-permute-start | bytes 589832 | tf_op jit(solution)/shard_map/ppermute | solution.py:825
  78.4 1.7 %collective-permute-start.12 = (f32[3,4,32,128]{3,2,1,0:T(8,128)S(1)}, f32[3,4,32,128]{3,2,1,0:T(8,128)S(1)}, u32[]{:S(2)}, u32[]{:S(2)}) collective-permute-start(f32[3,4,32,128]{3,2,1,0:T(8,128)S(1)} %get-tuple-element.37.refs_0_), channel_id=1, source_target_pairs={{0,6},{1,7},{2,0},{3,1},{4,2},{5,3},{6,4},{7,5},{8,14},{9,15},{10,... | collective-permute-start | bytes 589832 | tf_op jit(solution)/shard_map/ppermute | solution.py:825
  80.5 3.1 %collective-permute-done.14.refs_5_ = f32[3,4,32,128]{3,2,1,0:T(8,128)S(1)} collective-permute-done((f32[3,4,32,128]{3,2,1,0:T(8,128)S(1)}, f32[3,4,32,128]{3,2,1,0:T(8,128)S(1)}, u32[]{:S(2)}, u32[]{:S(2)}) %collective-permute-start.14) | collective-permute-done | bytes 196640 | tf_op jit(solution)/shard_map/ppermute | solution.py:825
  83.5 3.2 %collective-permute-start.16 = (f32[3,4,32,128]{3,2,1,0:T(8,128)S(1)}, f32[3,4,32,128]{3,2,1,0:T(8,128)S(1)}, u32[]{:S(2)}, u32[]{:S(2)}) collective-permute-start(f32[3,4,32,128]{3,2,1,0:T(8,128)S(1)} %collective-permute-done.14.refs_5_), channel_id=1, source_target_pairs={{0,6},{1,7},{2,0},{3,1},{4,2},{5,3},{6,4},{7,5},{8,14},{9,15},{10,... | collective-permute-start | bytes 589832 | tf_op jit(solution)/shard_map/ppermute | solution.py:825
  88.0 1.9 %collective-permute-start.9 = (f32[3,40,128]{2,1,0:T(8,128)S(1)}, f32[3,40,128]{2,1,0:T(8,128)S(1)}, u32[]{:S(2)}, u32[]{:S(2)}) collective-permute-start(f32[3,40,128]{2,1,0:T(8,128)S(1)} %get-tuple-element.35), channel_id=1, source_target_pairs={{8,16},{24,32},{40,48},{56,64},{72,80},{88,96},{104,112},{16,8},{3... | collective-permute-start | bytes 184328 | tf_op jit(solution)/shard_map/ppermute | solution.py:28
  89.9 7.2 %collective-permute-done.9.got_far = f32[3,40,128]{2,1,0:T(8,128)S(1)} collective-permute-done((f32[3,40,128]{2,1,0:T(8,128)S(1)}, f32[3,40,128]{2,1,0:T(8,128)S(1)}, u32[]{:S(2)}, u32[]{:S(2)}) %collective-permute-start.9) | collective-permute-done | bytes 61472 | tf_op jit(solution)/shard_map/ppermute | solution.py:28
  97.1 4.0 %prolong.1 = f32[3,8,64,256]{3,2,1,0:T(8,128)} custom-call(f32[66,5]{1,0:T(8,128)S(1)} %pad.8.rest_x, f32[3,4,40,128]{3,2,1,0:T(8,128)S(1)} %get-tuple-element.33.corr, f32[3,40,128]{2,1,0:T(8,128)S(1)} %collective-permute-done.8.got_near, f32[3,40,128]{2,1,0:T(8,128)S(1)} %collective-permute-done.9.got_far, f32[3,8,64,256]{3,2,1,0:T(8,128)S(1)} %get-tuple-element.36.smooth, ...), custom_call_target="tpu_custom_call" | custom-call | tf_op jit(solution)/shard_map/prolong/pallas_call | solution.py:804
  101.2 1.3 %assemble.1 = f32[3,4,256,128]{3,2,1,0:T(8,128)} custom-call(f32[3,4,32,128]{3,2,1,0:T(8,128)S(1)} %get-tuple-element.37.refs_0_, f32[3,4,32,128]{3,2,1,0:T(8,128)S(1)} %collective-permute-done.10.refs_1_, f32[3,4,32,128]{3,2,1,0:T(8,128)S(1)} %collective-permute-done.11.refs_2_, f32[3,4,32,128]{3,2,1,0:T(8,128)S(1)} %collective-permute-done.12.refs_3_, ...), custom_call_target="tpu_custom_call" | custom-call | tf_op jit(solution)/shard_map/assemble/pallas_call | solution.py:849
  (43 shorter events, 6.7 us)
Async XLA Ops:
  0.6 1.4 %copy-start = (f32[3,8,64,256]{3,2,1,0:T(8,128)S(1)}, f32[3,8,64,256]{3,2,1,0:T(8,128)}, u32[]{:S(2)}) copy-start(f32[3,8,64,256]{3,2,1,0:T(8,128)} %u.3) | copy-start | bytes 4718596
  4.6 5.5 %collective-permute-start = (f32[2,136,128]{2,1,0:T(8,128)S(1)}, f32[2,136,128]{2,1,0:T(8,128)S(1)}, u32[]{:S(2)}, u32[]{:S(2)}) collective-permute-start(f32[2,136,128]{2,1,0:T(8,128)S(1)} %get-tuple-element.20), channel_id=1, source_target_pairs={{0,1},{1,0},{2,3},{3,2},{4,5},{5,4},{6,7},{7,6},{8,9},{9,8},{10,11... | collective-permute-start | bytes 417800 | tf_op jit(solution)/shard_map/ppermute | solution.py:22
  6.0 13.6 %copy-start.10 = (f32[64,5]{0,1:T(8,128)S(1)}, f32[64,5]{0,1:T(8,128)}, u32[]{:S(2)}) copy-start(f32[64,5]{0,1:T(8,128)} %param.13) | copy-start | bytes 3844
  6.0 13.7 %copy-start.9 = (f32[256,5]{0,1:T(8,128)S(1)}, f32[256,5]{0,1:T(8,128)}, u32[]{:S(2)}) copy-start(f32[256,5]{0,1:T(8,128)} %param.14) | copy-start | bytes 15364
  6.0 25.4 %copy-start.6 = (f32[128,5]{0,1:T(8,128)S(1)}, f32[128,5]{0,1:T(8,128)}, u32[]{:S(2)}) copy-start(f32[128,5]{0,1:T(8,128)} %param.15) | copy-start | bytes 7684
  6.0 25.4 %copy-start.8 = (f32[2]{0:T(128)S(1)}, f32[2]{0:T(128)}, u32[]{:S(2)}) copy-start(f32[2]{0:T(128)} %bounds.2) | copy-start | bytes 28
  6.0 4.1 %collective-permute-start.1 = (f32[2,136,128]{2,1,0:T(8,128)S(1)}, f32[2,136,128]{2,1,0:T(8,128)S(1)}, u32[]{:S(2)}, u32[]{:S(2)}) collective-permute-start(f32[2,136,128]{2,1,0:T(8,128)S(1)} %get-tuple-element.21), channel_id=1, source_target_pairs={{1,2},{3,4},{5,6},{2,1},{4,3},{6,5},{9,10},{11,12},{13,14},{10,9},... | collective-permute-start | bytes 417800 | tf_op jit(solution)/shard_map/ppermute | solution.py:28
  15.0 4.8 %collective-permute-start.2 = (f32[10,2,72,128]{3,2,1,0:T(8,128)S(1)}, f32[10,2,72,128]{3,2,1,0:T(8,128)S(1)}, u32[]{:S(2)}, u32[]{:S(2)}) collective-permute-start(f32[10,2,72,128]{3,2,1,0:T(8,128)S(1)} %get-tuple-element.24.sent_near), channel_id=1, source_target_pairs={{0,8},{8,0},{16,24},{24,16},{32,40},{40,32},{48,56},{56,48},{64,72... | collective-permute-start | bytes 2211848 | tf_op jit(solution)/shard_map/ppermute | solution.py:22
  15.0 16.4 %collective-permute-start.3 = (f32[10,2,72,128]{3,2,1,0:T(8,128)S(1)}, f32[10,2,72,128]{3,2,1,0:T(8,128)S(1)}, u32[]{:S(2)}, u32[]{:S(2)}) collective-permute-start(f32[10,2,72,128]{3,2,1,0:T(8,128)S(1)} %get-tuple-element.25.sent_far), channel_id=1, source_target_pairs={{8,16},{24,32},{40,48},{56,64},{72,80},{88,96},{104,112},{16,8},{3... | collective-permute-start | bytes 2211848 | tf_op jit(solution)/shard_map/ppermute | solution.py:28
  32.5 18.0 %copy-start.5 = (f32[4,256,128]{2,1,0:T(8,128)S(1)}, f32[4,256,128]{2,1,0:T(8,128)}, u32[]{:S(2)}) copy-start(f32[4,256,128]{2,1,0:T(8,128)} %s.3) | copy-start | bytes 1572868
  32.5 29.8 %copy-start.7 = (f32[2]{0:T(128)S(1)}, f32[2]{0:T(128)}, u32[]{:S(2)}) copy-start(f32[2]{0:T(128)} %bounds.3) | copy-start | bytes 28
  42.4 8.1 %collective-permute-start.4 = (f32[18,8,128]{2,1,0:T(8,128)S(1)}, f32[18,8,128]{2,1,0:T(8,128)S(1)}, u32[]{:S(2)}, u32[]{:S(2)}) collective-permute-start(f32[18,8,128]{2,1,0:T(8,128)S(1)} %get-tuple-element.27), channel_id=1, source_target_pairs={{0,1},{1,0},{2,3},{3,2},{4,5},{5,4},{6,7},{7,6},{8,9},{9,8},{10,11... | collective-permute-start | bytes 221192 | tf_op jit(solution)/shard_map/ppermute | solution.py:22
  48.1 2.3 %collective-permute-start.5 = (f32[18,8,128]{2,1,0:T(8,128)S(1)}, f32[18,8,128]{2,1,0:T(8,128)S(1)}, u32[]{:S(2)}, u32[]{:S(2)}) collective-permute-start(f32[18,8,128]{2,1,0:T(8,128)S(1)} %get-tuple-element.28), channel_id=1, source_target_pairs={{1,2},{3,4},{5,6},{2,1},{4,3},{6,5},{9,10},{11,12},{13,14},{10,9},... | collective-permute-start | bytes 221192 | tf_op jit(solution)/shard_map/ppermute | solution.py:28
  50.6 4.1 %collective-permute-start.6 = (f32[14,40,128]{2,1,0:T(8,128)S(1)}, f32[14,40,128]{2,1,0:T(8,128)S(1)}, u32[]{:S(2)}, u32[]{:S(2)}) collective-permute-start(f32[14,40,128]{2,1,0:T(8,128)S(1)} %get-tuple-element.31), channel_id=1, source_target_pairs={{0,8},{8,0},{16,24},{24,16},{32,40},{40,32},{48,56},{56,48},{64,72... | collective-permute-start | bytes 860168 | tf_op jit(solution)/shard_map/ppermute | solution.py:22
  50.7 11.7 %collective-permute-start.7 = (f32[14,40,128]{2,1,0:T(8,128)S(1)}, f32[14,40,128]{2,1,0:T(8,128)S(1)}, u32[]{:S(2)}, u32[]{:S(2)}) collective-permute-start(f32[14,40,128]{2,1,0:T(8,128)S(1)} %get-tuple-element.32), channel_id=1, source_target_pairs={{8,16},{24,32},{40,48},{56,64},{72,80},{88,96},{104,112},{16,8},{3... | collective-permute-start | bytes 860168 | tf_op jit(solution)/shard_map/ppermute | solution.py:28
  65.4 9.0 %collective-permute-start.10 = (f32[3,4,32,128]{3,2,1,0:T(8,128)S(1)}, f32[3,4,32,128]{3,2,1,0:T(8,128)S(1)}, u32[]{:S(2)}, u32[]{:S(2)}) collective-permute-start(f32[3,4,32,128]{3,2,1,0:T(8,128)S(1)} %get-tuple-element.37.refs_0_), channel_id=1, source_target_pairs={{0,1},{1,0},{2,3},{3,2},{4,5},{5,4},{6,7},{7,6},{8,9},{9,8},{10,11... | collective-permute-start | bytes 589832 | tf_op jit(solution)/shard_map/ppermute | solution.py:22
  70.7 9.7 %collective-permute-start.11 = (f32[3,4,32,128]{3,2,1,0:T(8,128)S(1)}, f32[3,4,32,128]{3,2,1,0:T(8,128)S(1)}, u32[]{:S(2)}, u32[]{:S(2)}) collective-permute-start(f32[3,4,32,128]{3,2,1,0:T(8,128)S(1)} %get-tuple-element.37.refs_0_), channel_id=1, source_target_pairs={{0,2},{1,3},{2,4},{3,5},{4,6},{5,7},{6,0},{7,1},{8,10},{9,11},{10,... | collective-permute-start | bytes 589832 | tf_op jit(solution)/shard_map/ppermute | solution.py:825
  74.4 9.2 %collective-permute-start.14 = (f32[3,4,32,128]{3,2,1,0:T(8,128)S(1)}, f32[3,4,32,128]{3,2,1,0:T(8,128)S(1)}, u32[]{:S(2)}, u32[]{:S(2)}) collective-permute-start(f32[3,4,32,128]{3,2,1,0:T(8,128)S(1)} %collective-permute-done.10.refs_1_), channel_id=1, source_target_pairs={{0,6},{1,7},{2,0},{3,1},{4,2},{5,3},{6,4},{7,5},{8,14},{9,15},{10,... | collective-permute-start | bytes 589832 | tf_op jit(solution)/shard_map/ppermute | solution.py:825
  78.4 22.7 %collective-permute-start.12 = (f32[3,4,32,128]{3,2,1,0:T(8,128)S(1)}, f32[3,4,32,128]{3,2,1,0:T(8,128)S(1)}, u32[]{:S(2)}, u32[]{:S(2)}) collective-permute-start(f32[3,4,32,128]{3,2,1,0:T(8,128)S(1)} %get-tuple-element.37.refs_0_), channel_id=1, source_target_pairs={{0,6},{1,7},{2,0},{3,1},{4,2},{5,3},{6,4},{7,5},{8,14},{9,15},{10,... | collective-permute-start | bytes 589832 | tf_op jit(solution)/shard_map/ppermute | solution.py:825
  80.1 21.1 %collective-permute-start.13 = (f32[3,4,32,128]{3,2,1,0:T(8,128)S(1)}, f32[3,4,32,128]{3,2,1,0:T(8,128)S(1)}, u32[]{:S(2)}, u32[]{:S(2)}) collective-permute-start(f32[3,4,32,128]{3,2,1,0:T(8,128)S(1)} %collective-permute-done.10.refs_1_), channel_id=1, source_target_pairs={{0,2},{1,3},{2,4},{3,5},{4,6},{5,7},{6,0},{7,1},{8,10},{9,11},{10,... | collective-permute-start | bytes 589832 | tf_op jit(solution)/shard_map/ppermute | solution.py:825
  80.4 20.7 %collective-permute-start.15 = (f32[3,4,32,128]{3,2,1,0:T(8,128)S(1)}, f32[3,4,32,128]{3,2,1,0:T(8,128)S(1)}, u32[]{:S(2)}, u32[]{:S(2)}) collective-permute-start(f32[3,4,32,128]{3,2,1,0:T(8,128)S(1)} %collective-permute-done.11.refs_2_), channel_id=1, source_target_pairs={{0,2},{1,3},{2,4},{3,5},{4,6},{5,7},{6,0},{7,1},{8,10},{9,11},{10,... | collective-permute-start | bytes 589832 | tf_op jit(solution)/shard_map/ppermute | solution.py:825
  83.5 17.6 %collective-permute-start.16 = (f32[3,4,32,128]{3,2,1,0:T(8,128)S(1)}, f32[3,4,32,128]{3,2,1,0:T(8,128)S(1)}, u32[]{:S(2)}, u32[]{:S(2)}) collective-permute-start(f32[3,4,32,128]{3,2,1,0:T(8,128)S(1)} %collective-permute-done.14.refs_5_), channel_id=1, source_target_pairs={{0,6},{1,7},{2,0},{3,1},{4,2},{5,3},{6,4},{7,5},{8,14},{9,15},{10,... | collective-permute-start | bytes 589832 | tf_op jit(solution)/shard_map/ppermute | solution.py:825
  86.7 1.2 %collective-permute-start.8 = (f32[3,40,128]{2,1,0:T(8,128)S(1)}, f32[3,40,128]{2,1,0:T(8,128)S(1)}, u32[]{:S(2)}, u32[]{:S(2)}) collective-permute-start(f32[3,40,128]{2,1,0:T(8,128)S(1)} %get-tuple-element.34), channel_id=1, source_target_pairs={{0,8},{8,0},{16,24},{24,16},{32,40},{40,32},{48,56},{56,48},{64,72... | collective-permute-start | bytes 184328 | tf_op jit(solution)/shard_map/ppermute | solution.py:22
  88.0 9.1 %collective-permute-start.9 = (f32[3,40,128]{2,1,0:T(8,128)S(1)}, f32[3,40,128]{2,1,0:T(8,128)S(1)}, u32[]{:S(2)}, u32[]{:S(2)}) collective-permute-start(f32[3,40,128]{2,1,0:T(8,128)S(1)} %get-tuple-element.35), channel_id=1, source_target_pairs={{8,16},{24,32},{40,48},{56,64},{72,80},{88,96},{104,112},{16,8},{3... | collective-permute-start | bytes 184328 | tf_op jit(solution)/shard_map/ppermute | solution.py:28
  (4 other events, 4.4 us)
where the time goes:
time: 103 us; the launch traced here: 102 us
  waiting for transfers between devices  37.6 us (37%)
  starting transfers between devices  35.4 us (34%)
  Pallas kernels  22.5 us (22%)
  local copies, waits for them, and re-layouts  6.1 us (6%)
    ppermute x5, waiting for transfers between devices, swap_far(): return lax.ppermute(x, axis, up + [(j, i) for i, j in up])  26.4 us
    ppermute x6, starting transfers between devices, swap_near(): return lax.ppermute(x, axis, [(i, i ^ 1) for i in range(count)])  12.5 us
    ppermute x5, starting transfers between devices, swap_far(): return lax.ppermute(x, axis, up + [(j, i) for i, j in up])  11.9 us
    ppermute x6, starting transfers between devices, ring(): lax.ppermute(x, 'narrow', [(i, (i + by) % count) for i in range(count)])  11 us
    pallas_call x1, Pallas kernels, smoothing(): pl.pallas_call(smooth_kernel, in_specs=[SMEM, SMEM] + [VMEM] * 9, out_sha...  9.88 us
    ppermute x6, waiting for transfers between devices, swap_near(): return lax.ppermute(x, axis, [(i, i ^ 1) for i in range(count)])  8.17 us
    unnamed x24, local copies, waits for them, and re-layouts  6.07 us
    pallas_call x1, Pallas kernels, residual(): pl.pallas_call(residual_kernel, out_shape=[jax.ShapeDtypeStruct((3, width...  4.02 us
  transfers between devices with their start and end apart: 17, of which 8 were waited for; matrix products, arithmetic and copies ran while one was open for 0% of the time, Pallas kernels for 4%

commit v1 on v0

--- a/solution.py
+++ b/solution.py
@@ -10,11 +10,16 @@
 SUB = 8
 RIM = 4
 PAD = 8
-VMEM_LIMIT = 48 * 1024 * 1024
-
-
-def params():
-    return pltpu.CompilerParams(vmem_limit_bytes=VMEM_LIMIT)
+MIB = 1024 * 1024
+BYTES_PER_US = 3_690_000
+
+
+def params(mib=24):
+    return pltpu.CompilerParams(vmem_limit_bytes=mib * MIB)
+
+
+def cost(us):
+    return pl.CostEstimate(flops=0, bytes_accessed=int(us * BYTES_PER_US), transcendentals=0)
 
 
 def swap_near(x, axis):
@@ -26,6 +31,10 @@
     count = lax.axis_size(axis)
     up = [(i, i + 1) for i in range(1, count - 1, 2)]
     return lax.ppermute(x, axis, up + [(j, i) for i, j in up])
+
+
+def swap_both(pair, axis):
+    return [swap_near(pair[0], axis), swap_far(pair[1], axis)]
 
 
 def is_even(axis):
@@ -170,58 +179,35 @@
         out_specs=[whole, whole],
         out_shape=[out, out],
         compiler_params=params(),
+        cost_estimate=cost(1),
         name="pack_y",
     )(u, u, b, b, s, s)
 
 
-def residual_kernel(u, b, s, got_near, got_far, r0, s_ext, near, far, ue, be):
+def residual_kernel(u, b, s, r0, near, far, ue):
     _, width, height, _ = u.shape
-    own = PAD + RIM
-    tiles = (height + 2 * RIM) // SUB
     for h in range(2):
         lanes = slice(h * LANES, (h + 1) * LANES)
+        for x in range(width):
+            for c in range(3):
+                ue[c, x, h, 0:PAD, :] = jnp.zeros((PAD, LANES), F32)
+                ue[c, x, h, PAD + height :, :] = jnp.zeros((PAD, LANES), F32)
 
         def fill(t, carry, h=h, lanes=lanes):
             rows = pl.ds(pl.multiple_of(t * SUB, SUB), SUB)
-            to = pl.ds(own + t * SUB, SUB)
+            to = pl.ds(pl.multiple_of(PAD + t * SUB, SUB), SUB)
             for x in range(width):
                 for c in range(3):
                     ue[c, x, h, to, :] = u[c, x, rows, lanes]
-                    be[c, x, h, to, :] = b[c, x, rows, lanes]
-                s_ext[x, h, to, :] = s[x, rows, lanes]
             return carry
 
         lax.fori_loop(0, height // SUB, fill, 0)
-
-    def place(low, high):
-        for h in range(2):
-            for x in range(width):
-                for c in range(3):
-                    k = c * width + x
-                    ue[c, x, h, own - 3 : own, :] = low[h, 3 * k : 3 * k + 3, :]
-                    ue[c, x, h, own + height : own + height + 3, :] = high[h, 3 * k : 3 * k + 3, :]
-                    base = 9 * width + 2 * k
-                    be[c, x, h, own - 2 : own, :] = low[h, base : base + 2, :]
-                    be[c, x, h, own + height : own + height + 2, :] = high[h, base : base + 2, :]
-                base = 15 * width + 2 * x
-                s_ext[x, h, own - 2 : own, :] = low[h, base : base + 2, :]
-                s_ext[x, h, own + height : own + height + 2, :] = high[h, base : base + 2, :]
-
-    even = is_even("narrow")
-
-    @pl.when(even)
-    def _():
-        place(got_far, got_near)
-
-    @pl.when(jnp.logical_not(even))
-    def _():
-        place(got_near, got_far)
 
     edges = edge_masks()
 
     def step(t, carry):
         start = PAD + t * SUB
-        inside = inside_rows(t * SUB, height, "narrow")
+        rows = pl.ds(pl.multiple_of(t * SUB, SUB), SUB)
 
         def plane(x):
             return Plane(
@@ -230,27 +216,24 @@
             )
 
         before, here = None, plane(0)
-        rows = pl.ds(start, SUB)
         for x in range(width):
             after = plane(x + 1) if x + 1 < width else None
-            diagonal = [6.0 + s_ext[x, h, rows, :] for h in range(2)]
-            au = applied(before, here, after, diagonal)
+            au = applied(before, here, after, [6.0 + s[x, rows, h * LANES : (h + 1) * LANES] for h in range(2)])
             for c in range(3):
                 for h in range(2):
-                    r0[c, x, h, rows, :] = jnp.where(inside, be[c, x, h, rows, :] - au[c][h], 0.0)
+                    r0[c, x, h, rows, :] = b[c, x, rows, h * LANES : (h + 1) * LANES] - au[c][h]
             before, here = here, after
         return carry
 
-    lax.fori_loop(0, tiles, step, 0)
-
-    window = slice(PAD, PAD + height + 2 * RIM)
+    lax.fori_loop(0, height // SUB, step, 0)
 
     def pack(out, edge, second):
         for c in range(3):
-            out[c] = r0[c, edge, :, window, :]
-            out[3 + c] = r0[c, second, :, window, :]
-            out[6 + c] = ue[c, edge, :, window, :]
-        out[9] = s_ext[edge, :, window, :]
+            out[c] = r0[c, edge]
+            out[3 + c] = r0[c, second]
+            out[6 + c] = ue[c, edge, :, PAD : PAD + height, :]
+        for h in range(2):
+            out[9, h] = s[edge, :, h * LANES : (h + 1) * LANES]
 
     even_x = is_even("wide")
 
@@ -265,25 +248,138 @@
         pack(far, width - 1, width - 2)
 
 
-def residual(u, b, s, got_near, got_far):
+def residual(u, b, s):
     _, width, height, _ = u.shape
-    padded = height + 2 * (RIM + PAD)
-    side = jax.ShapeDtypeStruct((10, 2, height + 2 * RIM, LANES), F32)
+    side = jax.ShapeDtypeStruct((10, 2, height, LANES), F32)
     return pl.pallas_call(
         residual_kernel,
-        out_shape=[
-            jax.ShapeDtypeStruct((3, width, 2, padded, LANES), F32),
-            jax.ShapeDtypeStruct((width, 2, padded, LANES), F32),
-            side,
-            side,
-        ],
-        scratch_shapes=[
-            pltpu.VMEM((3, width, 2, padded, LANES), F32),
-            pltpu.VMEM((3, width, 2, padded, LANES), F32),
-        ],
+        out_shape=[pltpu.HBM((3, width, 2, height, LANES), F32), side, side],
+        scratch_shapes=[pltpu.VMEM((3, width, 2, height + 2 * PAD, LANES), F32)],
         compiler_params=params(),
+        cost_estimate=cost(3),
         name="residual",
-    )(u, b, s, got_near, got_far)
+    )(u, b, s)
+
+
+def ends_kernel(
+    u_lo, u_hi, b_lo, b_hi, s_lo, s_hi, got_near, got_far, main_near, main_far,
+    r_end, s_end, near, far, ue, be, se, own,
+):
+    width = u_lo.shape[1]
+    begin = (PAD + RIM, PAD - RIM)
+
+    def place(e, u, b, s, halo):
+        at = begin[e]
+        low = e == 0
+        three = slice(at - 3, at) if low else slice(at + SUB, at + SUB + 3)
+        two = slice(at - 2, at) if low else slice(at + SUB, at + SUB + 2)
+        for h in range(2):
+            lanes = slice(h * LANES, (h + 1) * LANES)
+            for x in range(width):
+                for c in range(3):
+                    k = c * width + x
+                    ue[e, c, x, h, at : at + SUB, :] = u[c, x, :, lanes]
+                    be[e, c, x, h, at : at + SUB, :] = b[c, x, :, lanes]
+                    ue[e, c, x, h, three, :] = halo[h, 3 * k : 3 * k + 3, :]
+                    base = 9 * width + 2 * k
+                    be[e, c, x, h, two, :] = halo[h, base : base + 2, :]
+                se[e, x, h, at : at + SUB, :] = s[x, :, lanes]
+                base = 15 * width + 2 * x
+                se[e, x, h, two, :] = halo[h, base : base + 2, :]
+
+    even = is_even("narrow")
+
+    @pl.when(even)
+    def _():
+        place(0, u_lo, b_lo, s_lo, got_far)
+        place(1, u_hi, b_hi, s_hi, got_near)
+
+    @pl.when(jnp.logical_not(even))
+    def _():
+        place(0, u_lo, b_lo, s_lo, got_near)
+        place(1, u_hi, b_hi, s_hi, got_far)
+
+    edges = edge_masks()
+
+    def step(e, carry):
+        inside = inside_rows(e * own + 2 * RIM * e - SUB * e, own, "narrow")
+
+        def plane(x):
+            return Plane(
+                lambda c, dy: [ue[e, c, x, h, pl.ds(PAD + dy, SUB), :] for h in range(2)],
+                edges,
+            )
+
+        before, here = None, plane(0)
+        tile = pl.ds(PAD, SUB)
+        for x in range(width):
+            after = plane(x + 1) if x + 1 < width else None
+            au = applied(before, here, after, [6.0 + se[e, x, h, tile, :] for h in range(2)])
+            for c in range(3):
+                for h in range(2):
+                    r_end[e, c, x, h] = jnp.where(inside, be[e, c, x, h, tile, :] - au[c][h], 0.0)
+            for h in range(2):
+                s_end[e, x, h] = se[e, x, h, tile, :]
+            before, here = here, after
+        return carry
+
+    lax.fori_loop(0, 2, step, 0)
+
+    def pack(out, main, edge, second):
+        for k in range(10):
+            out[k, :, SUB:own, :] = main[k, :, RIM : own - RIM, :]
+        for e in range(2):
+            tile = slice(e * own, e * own + SUB)
+            for h in range(2):
+                for c in range(3):
+                    out[c, h, tile, :] = r_end[e, c, edge, h]
+                    out[3 + c, h, tile, :] = r_end[e, c, second, h]
+                    out[6 + c, h, tile, :] = ue[e, c, edge, h, PAD : PAD + SUB, :]
+                out[9, h, tile, :] = s_end[e, edge, h]
+
+    even_x = is_even("wide")
+
+    @pl.when(even_x)
+    def _():
+        pack(near, main_near, width - 1, width - 2)
+        pack(far, main_far, 0, 1)
+
+    @pl.when(jnp.logical_not(even_x))
+    def _():
+        pack(near, main_near, 0, 1)
+        pack(far, main_far, width - 1, width - 2)
+
+
+def ends(u, b, s, got, main):
+    _, width, height, depth = u.shape
+    last = height // SUB - 1
+    block = pl.BlockSpec((3, width, SUB, depth), lambda i: (0, 0, 0, 0))
+    block_last = pl.BlockSpec((3, width, SUB, depth), lambda i: (0, 0, last, 0))
+    plane = pl.BlockSpec((width, SUB, depth), lambda i: (0, 0, 0))
+    plane_last = pl.BlockSpec((width, SUB, depth), lambda i: (0, last, 0))
+    shapes = [(2, 3, width, 2, SUB, LANES), (2, width, 2, SUB, LANES)] + [(10, 2, height + 2 * RIM, LANES)] * 2
+
+    def whole(shape):
+        return pl.BlockSpec(shape, lambda i: (0,) * len(shape))
+
+    def field(*lead):
+        return pltpu.VMEM((2, *lead, 2, 3 * SUB, LANES), F32)
+
+    def kernel(*refs):
+        return ends_kernel(*refs, height)
+
+    return pl.pallas_call(
+        kernel,
+        grid=(1,),
+        in_specs=[block, block_last, block, block_last, plane, plane_last] + [whole(x.shape) for x in (*got, *main)],
+        out_specs=[whole(shape) for shape in shapes],
+        out_shape=[pltpu.HBM(shape, F32) for shape in shapes[:2]]
+        + [jax.ShapeDtypeStruct(shape, F32) for shape in shapes[2:]],
+        scratch_shapes=[field(3, width), field(3, width), field(width)],
+        compiler_params=params(),
+        cost_estimate=cost(40),
+        name="ends",
+    )(u, u, b, b, s, s, *got, *main)
 
 
 def full(value):
@@ -319,12 +415,14 @@
 
 
 def smooth_kernel(
-    bounds, rest_x, r0p, s_ext, got_near, got_far, sent_near, sent_far, u, rest_y, rest_zt,
-    smooth, partial, near, far, left, right, u_left, u_right, r0, d1, r1, r2, t_pad, zr,
+    bounds, rest_x, r0p, r_end, s_end, got_near, got_far, sent_near, sent_far, u, s, rest_y, rest_zt,
+    smooth, partial, near, far, left, right, u_left, u_right, s_ext, r0, d1, r1, r2, t_pad, zr,
 ):
     _, width, height, _ = u.shape
+    tiles = (height + 2 * RIM) // SUB
     window = slice(PAD, PAD + height + 2 * RIM)
-    tiles = (height + 2 * RIM) // SUB
+    middle = slice(PAD + SUB, PAD + height)
+    tile_rows = [slice(PAD, PAD + SUB), slice(PAD + height, PAD + height + SUB)]
     even_x = is_even("wide")
     zr[...] = z_matrix(rest_zt)
 
@@ -343,6 +441,16 @@
     @pl.when(jnp.logical_not(even_x))
     def _():
         place(got_near, got_far, sent_near, sent_far)
+
+    for x in range(width):
+        for h in range(2):
+            s_ext[x, h, middle, :] = s[x, RIM : height - RIM, h * LANES : (h + 1) * LANES]
+        for e in range(2):
+            s_ext[x, :, tile_rows[e], :] = s_end[e, x]
+            for c in range(3):
+                r0[c, x + 2, :, tile_rows[e], :] = r_end[e, c, x]
+        for c in range(3):
+            r0[c, x + 2, :, middle, :] = r0p[c, x, :, RIM : height - RIM, :]
 
     edges = edge_masks()
     place_x = lax.axis_index("wide")
@@ -371,17 +479,15 @@
         inside_right = inside & has_right
         for c in range(3):
             for h in range(2):
-                for x in range(1, width - 1):
-                    r0[c, 2 + x, h, rows, :] = r0p[c, x, h, rows, :]
                 r0[c, 0, h, rows, :] = left[3 + c, h, rows, :]
                 r0[c, 1, h, rows, :] = jnp.where(
                     inside_left, left[c, h, rows, :] + in_left.behind[c][h], 0.0
                 )
                 r0[c, 2, h, rows, :] = jnp.where(
-                    inside, r0p[c, 0, h, rows, :] + out_left.ahead[c][h], 0.0
+                    inside, r0[c, 2, h, rows, :] + out_left.ahead[c][h], 0.0
                 )
                 r0[c, width + 1, h, rows, :] = jnp.where(
-                    inside, r0p[c, width - 1, h, rows, :] + out_right.behind[c][h], 0.0
+                    inside, r0[c, width + 1, h, rows, :] + out_right.behind[c][h], 0.0
                 )
                 r0[c, width + 2, h, rows, :] = jnp.where(
                     inside_right, right[c, h, rows, :] + in_right.ahead[c][h], 0.0
@@ -501,7 +607,7 @@
 VMEM = pl.BlockSpec(memory_space=pltpu.VMEM)
 
 
-def smoothing(bounds, rest_x, r0p, s_ext, got_near, got_far, sent_near, sent_far, u, rest_y, rest_zt):
+def smoothing(bounds, rest_x, r0p, r_end, s_end, got, sent, u, s, rest_y, rest_zt):
     _, width, height, depth = u.shape
     padded = height + 2 * (RIM + PAD)
     planes = 3 * (width // 2 + 2)
@@ -513,7 +619,7 @@
 
     return pl.pallas_call(
         smooth_kernel,
-        in_specs=[SMEM, SMEM] + [VMEM] * 9,
+        in_specs=[SMEM, SMEM] + [VMEM] * 11,
         out_shape=[
             jax.ShapeDtypeStruct((3, width, height, depth), F32),
             jax.ShapeDtypeStruct((3, width // 2 + 2, coarse_rows, LANES), F32),
@@ -525,6 +631,7 @@
             field(10),
             field(3),
             field(3),
+            field(width),
             field(3, width + 4),
             field(3, width + 2),
             field(3, width),
@@ -533,8 +640,9 @@
             pltpu.VMEM((2 * LANES, LANES), F32),
         ],
         compiler_params=params(),
+        cost_estimate=cost(10),
         name="smoothing",
-    )(bounds, rest_x, r0p, s_ext, got_near, got_far, sent_near, sent_far, u, rest_y, rest_zt)
+    )(bounds, rest_x, r0p, r_end, s_end, *got, *sent, u, s, rest_y, rest_zt)
 
 
 def rows_kernel(partial, got_near, got_far, s, q, s_win, near, far):
@@ -604,6 +712,7 @@
             side,
         ],
         compiler_params=params(),
+        cost_estimate=cost(1),
         name="coarse_rows",
     )(partial, got_near, got_far, s)
 
@@ -747,6 +856,7 @@
             pltpu.VMEM((width + 4, height, LANES), F32),
         ],
         compiler_params=params(),
+        cost_estimate=cost(3),
         name="coarse_solve",
     )(bounds, q, s_win, got_near, got_far)
 
@@ -813,11 +923,12 @@
             pltpu.VMEM((2 * width, 2 * own, LANES), F32),
         ],
         compiler_params=params(),
+        cost_estimate=cost(12),
         name="prolong",
     )(rest_x, corr, got_near, got_far, smooth, rest_y, rest_zt)
 
 
-def gather(own):
+def gather(own, edges):
     count = lax.axis_size("narrow")
     n = lax.axis_index("narrow")
 
@@ -826,10 +937,12 @@
 
     pair = swap_near(own, "narrow")
     low, high = ring(own, 2), ring(own, -2)
+    pair, low, high = lax.optimization_barrier((pair, low, high))
     pair_low, pair_high = ring(pair, 2), ring(pair, -2)
+    pair_high, edges = lax.optimization_barrier((pair_high, edges))
     far_own, far_pair = ring(low, 2), ring(pair_high, -2)
     blocks = [own, pair, low, high, pair_low, pair_high, far_own, far_pair]
-    return blocks
+    return blocks, edges
 
 
 def assemble_kernel(*refs):
@@ -850,6 +963,7 @@
         assemble_kernel,
         out_shape=jax.ShapeDtypeStruct((three, width, own * len(blocks), lanes), F32),
         compiler_params=params(),
+        cost_estimate=cost(1),
         name="assemble",
     )(*blocks)
 
@@ -868,20 +982,23 @@
     x_weights = jnp.pad(rest_x, ((1, 1), (0, 0)))
     y_padded = jnp.pad(rest_y, ((RIM, RIM), (0, 0)))
     z_weights = rest_z.T
-    near, far = pack_y(start_guess, right_side, reaction)
-    got_far, got_near = swap_far(far, "narrow"), swap_near(near, "narrow")
-    r0p, s_ext, near, far = residual(start_guess, right_side, reaction, got_near, got_far)
-    got_far, got_near = swap_far(far, "wide"), swap_near(near, "wide")
-    smooth, partial, near, far = smoothing(
-        fine_bounds, x_weights, r0p, s_ext, got_near, got_far, near, far, start_guess, y_padded, z_weights
+    from_hbm = [pltpu.with_memory_space_constraint(x, pltpu.HBM) for x in (start_guess, right_side, reaction)]
+    got = swap_both(pack_y(*from_hbm), "narrow")
+    r0p, *main = residual(start_guess, right_side, reaction)
+    r_end, s_end, *sent = ends(start_guess, right_side, reaction, got, main)
+    got = swap_both(sent, "wide")
+    r0p, r_end, s_end = (pltpu.with_memory_space_constraint(x, pltpu.HBM) for x in (r0p, r_end, s_end))
+    smooth, partial, *sent = smoothing(
+        fine_bounds, x_weights, r0p, r_end, s_end, got, sent, start_guess, reaction, y_padded, z_weights
     )
-    got_far, got_near = swap_far(far, "narrow"), swap_near(near, "narrow")
-    q, s_win, near, far = rows(partial, got_near, got_far, coarse_reaction)
-    got_far, got_near = swap_far(far, "wide"), swap_near(near, "wide")
-    corr, own, near, far = coarse_solve(coarse_bounds, q, s_win, got_near, got_far)
-    got_far, got_near = swap_far(far, "wide"), swap_near(near, "wide")
+    got = swap_both(sent, "narrow")
+    q, s_win, *sent = rows(partial, *got, coarse_reaction)
+    got = swap_both(sent, "wide")
+    corr, own, *sent = coarse_solve(coarse_bounds, q, s_win, *got)
+    got_near, got_far = swap_both(sent, "wide")
+    blocks, (got_near, got_far) = gather(own, (got_near, got_far))
     solution_block = prolong(x_weights, corr, got_near, got_far, smooth, y_padded, z_weights)
-    return solution_block, assemble(gather(own))
+    return solution_block, assemble(blocks)
 
 
 def solution(mesh):

time: 103 us -> 91.4 us (0.89)
  local copies, waits for them, and re-layouts: 6.1 us -> 0.3 us
  starting transfers between devices: 35.4 us -> 30 us
  Pallas kernels: 22.5 us -> 24.9 us
  waiting for transfers between devices: 37.6 us -> 35.2 us
    ppermute x6, waiting for transfers between devices: 8.17 us -> 1.86 us  [swap_near(): return lax.ppermute(x, axis, [(i, i ^ 1) for i in range(count)])]
    unnamed x24 -> x20, local copies, waits for them, and re-layouts: 6.07 us -> 0.27 us
    ppermute x6, starting transfers between devices: 12.5 us -> 7.61 us  [swap_near(): return lax.ppermute(x, axis, [(i, i ^ 1) for i in range(count)])]
    ppermute x6, waiting for transfers between devices: 3.09 us -> 7.36 us  [ring(): lax.ppermute(x, 'narrow', [(i, (i + by) % count) for i in range(count)])]
    pallas_call x1, Pallas kernels: 0.15 us -> 1.45 us  [pack_y(): pl.pallas_call(pack_y_kernel, grid=(1,), in_specs=[block, block_last, blo...]
    pallas_call x2 -> x3, Pallas kernels: 13.9 us -> 15 us  [the longest x1 9.98 us: smoothing(): pl.pallas_call(smooth_kernel, in_specs=[SMEM, SMEM] + [VMEM] * 11, out_sh...]
  transfers between devices with their start and end apart: 17 -> 17, of which waited for: 8 -> 9; matrix products, arithmetic and copies ran while one was open for 0% -> 0% of each run, Pallas kernels for 4% -> 8%
where the time goes in v1:
time: 91.4 us; the launch traced here: 91.2 us
  waiting for transfers between devices  35.2 us (39%)
  starting transfers between devices  30 us (33%)
  Pallas kernels  24.9 us (27%)
    ppermute x5, waiting for transfers between devices, swap_far(): return lax.ppermute(x, axis, up + [(j, i) for i, j in up])  25.9 us
    ppermute x5, starting transfers between devices, swap_far(): return lax.ppermute(x, axis, up + [(j, i) for i, j in up])  11.9 us
    ppermute x6, starting transfers between devices, ring(): lax.ppermute(x, 'narrow', [(i, (i + by) % count) for i in range(count)])  10.5 us
    pallas_call x1, Pallas kernels, smoothing(): pl.pallas_call(smooth_kernel, in_specs=[SMEM, SMEM] + [VMEM] * 11, out_sh...  9.98 us
    ppermute x6, starting transfers between devices, swap_near(): return lax.ppermute(x, axis, [(i, i ^ 1) for i in range(count)])  7.61 us
    ppermute x6, waiting for transfers between devices, ring(): lax.ppermute(x, 'narrow', [(i, (i + by) % count) for i in range(count)])  7.36 us
    pallas_call x1, Pallas kernels, prolong(): pl.pallas_call(prolong_kernel, in_specs=[SMEM] + [VMEM] * 6, out_shape=ja...  4 us
    pallas_call x1, Pallas kernels, residual(): pl.pallas_call(residual_kernel, out_shape=[pltpu.HBM((3, width, 2, height...  3.26 us
  transfers between devices with their start and end apart: 17, of which 9 were waited for; matrix products, arithmetic and copies ran while one was open for 0% of the time, Pallas kernels for 8%

profile of v1, /device:TPU:16, one launch (start us, length us, event | category | flops | bytes accessed | tf_op | source)
XLA Modules:
  0.0 91.2 jit_solution(2124858558815124039)
XLA Ops:
  0.7 1.5 %pack_y.1 = (f32[2,136,128]{2,1,0:T(8,128)S(1)}, f32[2,136,128]{2,1,0:T(8,128)S(1)}) custom-call(f32[3,8,64,256]{3,2,1,0:T(8,128)} %u.3, f32[3,8,64,256]{3,2,1,0:T(8,128)} %u.3, f32[3,8,64,256]{3,2,1,0:T(8,128)} %refs_3_.1, f32[3,8,64,256]{3,2,1,0:T(8,128)} %refs_3_.1, f32[8,64,256]{2,1,0:T(8,128)} %s.4, f32[8,64,256]{2,1,0:T(8,128)} %s.4), custom_call_target="tpu_custom_call" | custom-call | bytes 3690000 | tf_op jit(solution)/shard_map/pack_y/pallas_call | solution.py:175
  2.1 1.4 %collective-permute-start = (f32[2,136,128]{2,1,0:T(8,128)S(1)}, f32[2,136,128]{2,1,0:T(8,128)S(1)}, u32[]{:S(2)}, u32[]{:S(2)}) collective-permute-start(f32[2,136,128]{2,1,0:T(8,128)S(1)} %get-tuple-element.30), channel_id=1, source_target_pairs={{0,1},{1,0},{2,3},{3,2},{4,5},{5,4},{6,7},{7,6},{8,9},{9,8},{10,11... | collective-permute-start | bytes 417800 | tf_op jit(solution)/shard_map/ppermute | solution.py:27
  3.5 0.7 collective-permute-start.1
  4.2 3.3 %residual.1 = (f32[3,8,2,64,128]{4,3,2,1,0:T(8,128)}, f32[10,2,64,128]{3,2,1,0:T(8,128)S(1)}, f32[10,2,64,128]{3,2,1,0:T(8,128)S(1)}) custom-call(f32[3,8,64,256]{3,2,1,0:T(8,128)S(1)} %copy-done, f32[3,8,64,256]{3,2,1,0:T(8,128)S(1)} %copy-done.1, f32[8,64,256]{2,1,0:T(8,128)S(1)} %copy-done.2), custom_call_target="tpu_custom_call" | custom-call | bytes 11070000 | tf_op jit(solution)/shard_map/residual/pallas_call | solution.py:254
  7.6 1.8 %ends.1 = (f32[2,3,8,2,8,128]{5,4,3,2,1,0:T(8,128)}, f32[2,8,2,8,128]{4,3,2,1,0:T(8,128)}, f32[10,2,72,128]{3,2,1,0:T(8,128)S(1)}, f32[10,2,72,128]{3,2,1,0:T(8,128)}) custom-call(f32[3,8,64,256]{3,2,1,0:T(8,128)S(1)} %copy-done, f32[3,8,64,256]{3,2,1,0:T(8,128)S(1)} %copy-done, f32[3,8,64,256]{3,2,1,0:T(8,128)S(1)} %copy-done.1, ...), custom_call_target="tpu_custom_call" | custom-call | bytes 147600000 | tf_op jit(solution)/shard_map/ends/pallas_call | solution.py:371
  9.4 4.7 %collective-permute-start.3 = (f32[10,2,72,128]{3,2,1,0:T(8,128)}, f32[10,2,72,128]{3,2,1,0:T(8,128)}, u32[]{:S(2)}, u32[]{:S(2)}) collective-permute-start(f32[10,2,72,128]{3,2,1,0:T(8,128)} %get-tuple-element.37.sent_far), channel_id=1, source_target_pairs={{8,16},{24,32},{40,48},{56,64},{72,80},{88,96},{104,112},{16,8},{3... | collective-permute-start | bytes 2211848 | tf_op jit(solution)/shard_map/ppermute | solution.py:33
  14.4 11.7 %collective-permute-done.3.got_far = f32[10,2,72,128]{3,2,1,0:T(8,128)} collective-permute-done((f32[10,2,72,128]{3,2,1,0:T(8,128)}, f32[10,2,72,128]{3,2,1,0:T(8,128)}, u32[]{:S(2)}, u32[]{:S(2)}) %collective-permute-start.3) | collective-permute-done | bytes 737312 | tf_op jit(solution)/shard_map/ppermute | solution.py:33
  26.1 10.0 %smoothing.1 = (f32[3,8,64,256]{3,2,1,0:T(8,128)S(1)}, f32[3,6,40,128]{3,2,1,0:T(8,128)S(1)}, f32[18,8,128]{2,1,0:T(8,128)S(1)}, f32[18,8,128]{2,1,0:T(8,128)S(1)}) custom-call(f32[2]{0:T(128)S(1)} %copy-done.6, f32[66,5]{1,0:T(8,128)S(1)} %pad.8.rest_x, f32[3,8,2,64,128]{4,3,2,1,0:T(8,128)} %get-tuple-element.29.r0p, ...), custom_call_target="tpu_custom_call" | custom-call | bytes 36900000 | tf_op jit(solution)/shard_map/smoothing/pallas_call | solution.py:620
  36.1 5.8 %collective-permute-start.4 = (f32[18,8,128]{2,1,0:T(8,128)S(1)}, f32[18,8,128]{2,1,0:T(8,128)S(1)}, u32[]{:S(2)}, u32[]{:S(2)}) collective-permute-start(f32[18,8,128]{2,1,0:T(8,128)S(1)} %get-tuple-element.39), channel_id=1, source_target_pairs={{0,1},{1,0},{2,3},{3,2},{4,5},{5,4},{6,7},{7,6},{8,9},{9,8},{10,11... | collective-permute-start | bytes 221192 | tf_op jit(solution)/shard_map/ppermute | solution.py:27
  41.9 0.7 collective-permute-start.5
  42.6 1.7 %collective-permute-done.4.got_near = f32[18,8,128]{2,1,0:T(8,128)S(1)} collective-permute-done((f32[18,8,128]{2,1,0:T(8,128)S(1)}, f32[18,8,128]{2,1,0:T(8,128)S(1)}, u32[]{:S(2)}, u32[]{:S(2)}) %collective-permute-start.4) | collective-permute-done | bytes 73760 | tf_op jit(solution)/shard_map/ppermute | solution.py:27
  44.4 4.0 %collective-permute-start.7 = (f32[14,40,128]{2,1,0:T(8,128)S(1)}, f32[14,40,128]{2,1,0:T(8,128)S(1)}, u32[]{:S(2)}, u32[]{:S(2)}) collective-permute-start(f32[14,40,128]{2,1,0:T(8,128)S(1)} %get-tuple-element.44), channel_id=1, source_target_pairs={{8,16},{24,32},{40,48},{56,64},{72,80},{88,96},{104,112},{16,8},{3... | collective-permute-start | bytes 860168 | tf_op jit(solution)/shard_map/ppermute | solution.py:33
  48.4 7.7 %collective-permute-done.7.got_far = f32[14,40,128]{2,1,0:T(8,128)S(1)} collective-permute-done((f32[14,40,128]{2,1,0:T(8,128)S(1)}, f32[14,40,128]{2,1,0:T(8,128)S(1)}, u32[]{:S(2)}, u32[]{:S(2)}) %collective-permute-start.7) | collective-permute-done | bytes 286752 | tf_op jit(solution)/shard_map/ppermute | solution.py:33
  56.1 3.1 %coarse_solve.1 = (f32[3,4,40,128]{3,2,1,0:T(8,128)S(1)}, f32[3,4,32,128]{3,2,1,0:T(8,128)S(1)}, f32[3,40,128]{2,1,0:T(8,128)S(1)}, f32[3,40,128]{2,1,0:T(8,128)S(1)}) custom-call(f32[2]{0:T(128)S(1)} %copy-done.5, f32[3,6,40,128]{3,2,1,0:T(8,128)S(1)} %get-tuple-element.41.q, f32[4,40,128]{2,1,0:T(8,128)S(1)} %get-tuple-element.42.s_win, ...), custom_call_target="tpu_custom_call" | custom-call | bytes 11070000 | tf_op jit(solution)/shard_map/coarse_solve/pallas_call | solution.py:841
  59.2 7.0 %collective-permute-start.10 = (f32[3,4,32,128]{3,2,1,0:T(8,128)S(1)}, f32[3,4,32,128]{3,2,1,0:T(8,128)S(1)}, u32[]{:S(2)}, u32[]{:S(2)}) collective-permute-start(f32[3,4,32,128]{3,2,1,0:T(8,128)S(1)} %get-tuple-element.46.refs_0_), channel_id=1, source_target_pairs={{0,6},{1,7},{2,0},{3,1},{4,2},{5,3},{6,4},{7,5},{8,14},{9,15},{10,... | collective-permute-start | bytes 589832 | tf_op jit(solution)/shard_map/ppermute | solution.py:936
  66.5 3.1 %collective-permute-done.10.refs_3_ = f32[3,4,32,128]{3,2,1,0:T(8,128)S(1)} collective-permute-done((f32[3,4,32,128]{3,2,1,0:T(8,128)S(1)}, f32[3,4,32,128]{3,2,1,0:T(8,128)S(1)}, u32[]{:S(2)}, u32[]{:S(2)}) %collective-permute-start.10) | collective-permute-done | bytes 196640 | tf_op jit(solution)/shard_map/ppermute | solution.py:936
  69.6 3.4 %collective-permute-done.9.refs_2_ = f32[3,4,32,128]{3,2,1,0:T(8,128)S(1)} collective-permute-done((f32[3,4,32,128]{3,2,1,0:T(8,128)S(1)}, f32[3,4,32,128]{3,2,1,0:T(8,128)S(1)}, u32[]{:S(2)}, u32[]{:S(2)}) %collective-permute-start.9) | collective-permute-done | bytes 196640 | tf_op jit(solution)/shard_map/ppermute | solution.py:936
  73.0 2.0 %collective-permute-start.11 = (f32[3,4,32,128]{3,2,1,0:T(8,128)S(1)}, f32[3,4,32,128]{3,2,1,0:T(8,128)S(1)}, u32[]{:S(2)}, u32[]{:S(2)}) collective-permute-start(f32[3,4,32,128]{3,2,1,0:T(8,128)S(1)} %collective-permute-done.8.refs_1_), channel_id=1, source_target_pairs={{0,6},{1,7},{2,0},{3,1},{4,2},{5,3},{6,4},{7,5},{8,14},{9,15},{10,... | collective-permute-start | bytes 589832 | tf_op jit(solution)/shard_map/ppermute | solution.py:936
  75.1 1.9 %collective-permute-start.13 = (f32[3,40,128]{2,1,0:T(8,128)S(1)}, f32[3,40,128]{2,1,0:T(8,128)S(1)}, u32[]{:S(2)}, u32[]{:S(2)}) collective-permute-start(f32[3,40,128]{2,1,0:T(8,128)S(1)} %get-tuple-element.49), channel_id=1, source_target_pairs={{8,16},{24,32},{40,48},{56,64},{72,80},{88,96},{104,112},{16,8},{3... | collective-permute-start | bytes 184328 | tf_op jit(solution)/shard_map/ppermute | solution.py:33
  77.7 6.6 %collective-permute-done.13.got_far = f32[3,40,128]{2,1,0:T(8,128)S(1)} collective-permute-done((f32[3,40,128]{2,1,0:T(8,128)S(1)}, f32[3,40,128]{2,1,0:T(8,128)S(1)}, u32[]{:S(2)}, u32[]{:S(2)}) %collective-permute-start.13) | collective-permute-done | bytes 61472 | tf_op jit(solution)/shard_map/ppermute | solution.py:33
  84.2 0.8 collective-permute-start.16
  85.0 4.0 %prolong.1 = f32[3,8,64,256]{3,2,1,0:T(8,128)} custom-call(f32[66,5]{1,0:T(8,128)S(1)} %pad.8.rest_x, f32[3,4,40,128]{3,2,1,0:T(8,128)S(1)} %get-tuple-element.45.corr, f32[3,40,128]{2,1,0:T(8,128)S(1)} %collective-permute-done.12.got_near, f32[3,40,128]{2,1,0:T(8,128)S(1)} %collective-permute-done.13.got_far, ...), custom_call_target="tpu_custom_call" | custom-call | bytes 44280000 | tf_op jit(solution)/shard_map/prolong/pallas_call | solution.py:914
  89.0 0.8 collective-permute-done.15.refs_6_
  89.9 1.3 %assemble.1 = f32[3,4,256,128]{3,2,1,0:T(8,128)} custom-call(f32[3,4,32,128]{3,2,1,0:T(8,128)S(1)} %get-tuple-element.46.refs_0_, f32[3,4,32,128]{3,2,1,0:T(8,128)S(1)} %collective-permute-done.8.refs_1_, f32[3,4,32,128]{3,2,1,0:T(8,128)S(1)} %collective-permute-done.9.refs_2_, f32[3,4,32,128]{3,2,1,0:T(8,128)S(1)} %collective-permute-done.10.refs_3_, ...), custom_call_target="tpu_custom_call" | custom-call | bytes 3690000 | tf_op jit(solution)/shard_map/assemble/pallas_call | solution.py:962
  (40 shorter events, 1.8 us)
Async XLA Ops:
  0.6 3.5 %copy-start.2 = (f32[8,64,256]{2,1,0:T(8,128)S(1)}, f32[8,64,256]{2,1,0:T(8,128)}, u32[]{:S(2)}) copy-start(f32[8,64,256]{2,1,0:T(8,128)} %s.4) | copy-start | bytes 1572868
  2.1 5.5 %collective-permute-start = (f32[2,136,128]{2,1,0:T(8,128)S(1)}, f32[2,136,128]{2,1,0:T(8,128)S(1)}, u32[]{:S(2)}, u32[]{:S(2)}) collective-permute-start(f32[2,136,128]{2,1,0:T(8,128)S(1)} %get-tuple-element.30), channel_id=1, source_target_pairs={{0,1},{1,0},{2,3},{3,2},{4,5},{5,4},{6,7},{7,6},{8,9},{9,8},{10,11... | collective-permute-start | bytes 417800 | tf_op jit(solution)/shard_map/ppermute | solution.py:27
  3.5 4.1 %collective-permute-start.1 = (f32[2,136,128]{2,1,0:T(8,128)S(1)}, f32[2,136,128]{2,1,0:T(8,128)S(1)}, u32[]{:S(2)}, u32[]{:S(2)}) collective-permute-start(f32[2,136,128]{2,1,0:T(8,128)S(1)} %get-tuple-element.31), channel_id=1, source_target_pairs={{1,2},{3,4},{5,6},{2,1},{4,3},{6,5},{9,10},{11,12},{13,14},{10,9},... | collective-permute-start | bytes 417800 | tf_op jit(solution)/shard_map/ppermute | solution.py:33
  7.6 6.5 %copy-start.8 = (f32[64,5]{0,1:T(8,128)S(1)}, f32[64,5]{0,1:T(8,128)}, u32[]{:S(2)}) copy-start(f32[64,5]{0,1:T(8,128)} %param.13) | copy-start | bytes 3844
  7.6 6.6 %copy-start.7 = (f32[256,5]{0,1:T(8,128)S(1)}, f32[256,5]{0,1:T(8,128)}, u32[]{:S(2)}) copy-start(f32[256,5]{0,1:T(8,128)} %param.14) | copy-start | bytes 15364
  7.6 18.5 %copy-start.4 = (f32[128,5]{0,1:T(8,128)S(1)}, f32[128,5]{0,1:T(8,128)}, u32[]{:S(2)}) copy-start(f32[128,5]{0,1:T(8,128)} %param.15) | copy-start | bytes 7684
  7.6 18.5 %copy-start.6 = (f32[2]{0:T(128)S(1)}, f32[2]{0:T(128)}, u32[]{:S(2)}) copy-start(f32[2]{0:T(128)} %bounds.2) | copy-start | bytes 28
  9.4 5.0 %collective-permute-start.2 = (f32[10,2,72,128]{3,2,1,0:T(8,128)S(1)}, f32[10,2,72,128]{3,2,1,0:T(8,128)}, u32[]{:S(2)}, u32[]{:S(2)}) collective-permute-start(f32[10,2,72,128]{3,2,1,0:T(8,128)S(1)} %get-tuple-element.36.sent_near), channel_id=1, source_target_pairs={{0,8},{8,0},{16,24},{24,16},{32,40},{40,32},{48,56},{56,48},{64,72... | collective-permute-start | bytes 2211848 | tf_op jit(solution)/shard_map/ppermute | solution.py:27
  9.4 16.7 %collective-permute-start.3 = (f32[10,2,72,128]{3,2,1,0:T(8,128)}, f32[10,2,72,128]{3,2,1,0:T(8,128)}, u32[]{:S(2)}, u32[]{:S(2)}) collective-permute-start(f32[10,2,72,128]{3,2,1,0:T(8,128)} %get-tuple-element.37.sent_far), channel_id=1, source_target_pairs={{8,16},{24,32},{40,48},{56,64},{72,80},{88,96},{104,112},{16,8},{3... | collective-permute-start | bytes 2211848 | tf_op jit(solution)/shard_map/ppermute | solution.py:33
  26.1 18.1 %copy-start.3 = (f32[4,256,128]{2,1,0:T(8,128)S(1)}, f32[4,256,128]{2,1,0:T(8,128)}, u32[]{:S(2)}) copy-start(f32[4,256,128]{2,1,0:T(8,128)} %s.5) | copy-start | bytes 1572868
  26.1 30.0 %copy-start.5 = (f32[2]{0:T(128)S(1)}, f32[2]{0:T(128)}, u32[]{:S(2)}) copy-start(f32[2]{0:T(128)} %bounds.3) | copy-start | bytes 28
  36.1 8.1 %collective-permute-start.4 = (f32[18,8,128]{2,1,0:T(8,128)S(1)}, f32[18,8,128]{2,1,0:T(8,128)S(1)}, u32[]{:S(2)}, u32[]{:S(2)}) collective-permute-start(f32[18,8,128]{2,1,0:T(8,128)S(1)} %get-tuple-element.39), channel_id=1, source_target_pairs={{0,1},{1,0},{2,3},{3,2},{4,5},{5,4},{6,7},{7,6},{8,9},{9,8},{10,11... | collective-permute-start | bytes 221192 | tf_op jit(solution)/shard_map/ppermute | solution.py:27
  41.9 2.3 %collective-permute-start.5 = (f32[18,8,128]{2,1,0:T(8,128)S(1)}, f32[18,8,128]{2,1,0:T(8,128)S(1)}, u32[]{:S(2)}, u32[]{:S(2)}) collective-permute-start(f32[18,8,128]{2,1,0:T(8,128)S(1)} %get-tuple-element.40), channel_id=1, source_target_pairs={{1,2},{3,4},{5,6},{2,1},{4,3},{6,5},{9,10},{11,12},{13,14},{10,9},... | collective-permute-start | bytes 221192 | tf_op jit(solution)/shard_map/ppermute | solution.py:33
  44.4 4.1 %collective-permute-start.6 = (f32[14,40,128]{2,1,0:T(8,128)S(1)}, f32[14,40,128]{2,1,0:T(8,128)S(1)}, u32[]{:S(2)}, u32[]{:S(2)}) collective-permute-start(f32[14,40,128]{2,1,0:T(8,128)S(1)} %get-tuple-element.43), channel_id=1, source_target_pairs={{0,8},{8,0},{16,24},{24,16},{32,40},{40,32},{48,56},{56,48},{64,72... | collective-permute-start | bytes 860168 | tf_op jit(solution)/shard_map/ppermute | solution.py:27
  44.4 11.7 %collective-permute-start.7 = (f32[14,40,128]{2,1,0:T(8,128)S(1)}, f32[14,40,128]{2,1,0:T(8,128)S(1)}, u32[]{:S(2)}, u32[]{:S(2)}) collective-permute-start(f32[14,40,128]{2,1,0:T(8,128)S(1)} %get-tuple-element.44), channel_id=1, source_target_pairs={{8,16},{24,32},{40,48},{56,64},{72,80},{88,96},{104,112},{16,8},{3... | collective-permute-start | bytes 860168 | tf_op jit(solution)/shard_map/ppermute | solution.py:33
  59.2 10.4 %collective-permute-start.10 = (f32[3,4,32,128]{3,2,1,0:T(8,128)S(1)}, f32[3,4,32,128]{3,2,1,0:T(8,128)S(1)}, u32[]{:S(2)}, u32[]{:S(2)}) collective-permute-start(f32[3,4,32,128]{3,2,1,0:T(8,128)S(1)} %get-tuple-element.46.refs_0_), channel_id=1, source_target_pairs={{0,6},{1,7},{2,0},{3,1},{4,2},{5,3},{6,4},{7,5},{8,14},{9,15},{10,... | collective-permute-start | bytes 589832 | tf_op jit(solution)/shard_map/ppermute | solution.py:936
  66.2 6.9 %collective-permute-start.9 = (f32[3,4,32,128]{3,2,1,0:T(8,128)S(1)}, f32[3,4,32,128]{3,2,1,0:T(8,128)S(1)}, u32[]{:S(2)}, u32[]{:S(2)}) collective-permute-start(f32[3,4,32,128]{3,2,1,0:T(8,128)S(1)} %get-tuple-element.46.refs_0_), channel_id=1, source_target_pairs={{0,2},{1,3},{2,4},{3,5},{4,6},{5,7},{6,0},{7,1},{8,10},{9,11},{10,... | collective-permute-start | bytes 589832 | tf_op jit(solution)/shard_map/ppermute | solution.py:936
  66.2 6.9 %collective-permute-start.8 = (f32[3,4,32,128]{3,2,1,0:T(8,128)S(1)}, f32[3,4,32,128]{3,2,1,0:T(8,128)S(1)}, u32[]{:S(2)}, u32[]{:S(2)}) collective-permute-start(f32[3,4,32,128]{3,2,1,0:T(8,128)S(1)} %get-tuple-element.46.refs_0_), channel_id=1, source_target_pairs={{0,1},{1,0},{2,3},{3,2},{4,5},{5,4},{6,7},{7,6},{8,9},{9,8},{10,11... | collective-permute-start | bytes 589832 | tf_op jit(solution)/shard_map/ppermute | solution.py:27
  73.0 11.2 %collective-permute-start.11 = (f32[3,4,32,128]{3,2,1,0:T(8,128)S(1)}, f32[3,4,32,128]{3,2,1,0:T(8,128)S(1)}, u32[]{:S(2)}, u32[]{:S(2)}) collective-permute-start(f32[3,4,32,128]{3,2,1,0:T(8,128)S(1)} %collective-permute-done.8.refs_1_), channel_id=1, source_target_pairs={{0,6},{1,7},{2,0},{3,1},{4,2},{5,3},{6,4},{7,5},{8,14},{9,15},{10,... | collective-permute-start | bytes 589832 | tf_op jit(solution)/shard_map/ppermute | solution.py:936
  75.1 2.6 %collective-permute-start.12 = (f32[3,40,128]{2,1,0:T(8,128)S(1)}, f32[3,40,128]{2,1,0:T(8,128)S(1)}, u32[]{:S(2)}, u32[]{:S(2)}) collective-permute-start(f32[3,40,128]{2,1,0:T(8,128)S(1)} %get-tuple-element.48), channel_id=1, source_target_pairs={{0,8},{8,0},{16,24},{24,16},{32,40},{40,32},{48,56},{56,48},{64,72... | collective-permute-start | bytes 184328 | tf_op jit(solution)/shard_map/ppermute | solution.py:27
  75.1 9.1 %collective-permute-start.13 = (f32[3,40,128]{2,1,0:T(8,128)S(1)}, f32[3,40,128]{2,1,0:T(8,128)S(1)}, u32[]{:S(2)}, u32[]{:S(2)}) collective-permute-start(f32[3,40,128]{2,1,0:T(8,128)S(1)} %get-tuple-element.49), channel_id=1, source_target_pairs={{8,16},{24,32},{40,48},{56,64},{72,80},{88,96},{104,112},{16,8},{3... | collective-permute-start | bytes 184328 | tf_op jit(solution)/shard_map/ppermute | solution.py:33
  77.0 12.8 %collective-permute-start.14 = (f32[3,4,32,128]{3,2,1,0:T(8,128)S(1)}, f32[3,4,32,128]{3,2,1,0:T(8,128)S(1)}, u32[]{:S(2)}, u32[]{:S(2)}) collective-permute-start(f32[3,4,32,128]{3,2,1,0:T(8,128)S(1)} %collective-permute-done.8.refs_1_), channel_id=1, source_target_pairs={{0,2},{1,3},{2,4},{3,5},{4,6},{5,7},{6,0},{7,1},{8,10},{9,11},{10,... | collective-permute-start | bytes 589832 | tf_op jit(solution)/shard_map/ppermute | solution.py:936
  77.3 12.5 %collective-permute-start.15 = (f32[3,4,32,128]{3,2,1,0:T(8,128)S(1)}, f32[3,4,32,128]{3,2,1,0:T(8,128)S(1)}, u32[]{:S(2)}, u32[]{:S(2)}) collective-permute-start(f32[3,4,32,128]{3,2,1,0:T(8,128)S(1)} %collective-permute-done.9.refs_2_), channel_id=1, source_target_pairs={{0,2},{1,3},{2,4},{3,5},{4,6},{5,7},{6,0},{7,1},{8,10},{9,11},{10,... | collective-permute-start | bytes 589832 | tf_op jit(solution)/shard_map/ppermute | solution.py:936
  84.2 5.7 %collective-permute-start.16 = (f32[3,4,32,128]{3,2,1,0:T(8,128)S(1)}, f32[3,4,32,128]{3,2,1,0:T(8,128)S(1)}, u32[]{:S(2)}, u32[]{:S(2)}) collective-permute-start(f32[3,4,32,128]{3,2,1,0:T(8,128)S(1)} %collective-permute-done.11.refs_5_), channel_id=1, source_target_pairs={{0,6},{1,7},{2,0},{3,1},{4,2},{5,3},{6,4},{7,5},{8,14},{9,15},{10,... | collective-permute-start | bytes 589832 | tf_op jit(solution)/shard_map/ppermute | solution.py:936
  (2 other events, 7.0 us)

commit v2 on v1

--- a/solution.py
+++ b/solution.py
@@ -74,49 +74,52 @@
 
 
 class Plane:
-    def __init__(self, load, edges):
-        first, last = edges
-        v = [load(c, 0) for c in range(3)]
+    def __init__(self, load):
+        self.v = [load(c, 0) for c in range(3)]
         above = [load(c, 1) for c in range(3)]
         below = [load(c, -1) for c in range(3)]
-        dy = [eighth(sub(above[c], below[c])) for c in range(3)]
-        next_0, before_0 = z_next(v[0], last), z_before(v[0], first)
-        next_2, before_2 = z_next(v[2], last), z_before(v[2], first)
-        slope = [
-            add(dy[1], eighth(sub(next_2, before_2))),
-            dy[0],
-            eighth(sub(next_0, before_0)),
-        ]
-        self.v = v
-        self.ahead = [add(v[c], slope[c]) for c in range(3)]
-        self.behind = [sub(v[c], slope[c]) for c in range(3)]
-        self.parts = (above, below, dy, next_0, before_0, edges)
-
-    def inner(self, diagonal):
-        above, below, dy, next_0, before_0, (first, last) = self.parts
-        v = self.v
-        out = []
-        for c in range(3):
-            if c == 0:
-                along_z = add(next_0, before_0)
-            else:
-                other = dy[2] if c == 1 else dy[1]
-                along_z = add(
-                    z_next(sub(v[c], other), last), z_before(add(v[c], other), first)
-                )
-            total = add(add(above[c], below[c]), along_z)
-            out.append(each(lambda d, p, q: d * p - q, diagonal, v[c], total))
-        return out
-
-
-def applied(before, plane, after, diagonal):
-    out = plane.inner(diagonal)
+        self.along_y = [add(above[c], below[c]) for c in range(3)]
+        self.dy = [eighth(sub(above[c], below[c])) for c in range(3)]
+
+
+def applied(before, plane, after, diagonal, edges):
+    first, last = edges
+    v, dy = plane.v, plane.dy
+
+    def difference(pick):
+        if before is None:
+            return pick(after)
+        if after is None:
+            return each(lambda p: -p, pick(before))
+        return sub(pick(after), pick(before))
+
+    slope = [
+        eighth(difference(lambda q: q.v[2])),
+        dy[2],
+        add(eighth(difference(lambda q: q.v[0])), dy[1]),
+    ]
+    cross = [difference(lambda q: q.dy[1]), difference(lambda q: q.dy[0]), None]
+    out = []
     for c in range(3):
-        if after is not None:
-            out[c] = sub(out[c], after.behind[c])
-        if before is not None:
-            out[c] = sub(out[c], before.ahead[c])
+        near = plane.along_y[c]
+        for other in (before, after):
+            if other is not None:
+                near = add(near, other.v[c])
+        total = each(lambda d, p, q: d * p - q, diagonal, v[c], near)
+        if cross[c] is not None:
+            total = add(total, cross[c])
+        total = add(total, z_next(sub(slope[c], v[c]), last))
+        out.append(sub(total, z_before(add(slope[c], v[c]), first)))
     return out
+
+
+def shares(load, edges):
+    first, last = edges
+    plane = Plane(load)
+    v, dy = plane.v, plane.dy
+    along_z = [sub(z_next(v[c], last), z_before(v[c], first)) for c in (0, 2)]
+    slope = [add(dy[1], eighth(along_z[1])), dy[0], eighth(along_z[0])]
+    return [add(v[c], slope[c]) for c in range(3)], [sub(v[c], slope[c]) for c in range(3)]
 
 
 def edge_masks():
@@ -210,22 +213,19 @@
         rows = pl.ds(pl.multiple_of(t * SUB, SUB), SUB)
 
         def plane(x):
-            return Plane(
-                lambda c, dy: [ue[c, x, h, pl.ds(start + dy, SUB), :] for h in range(2)],
-                edges,
-            )
+            return Plane(lambda c, dy: [ue[c, x, h, pl.ds(start + dy, SUB), :] for h in range(2)])
 
         before, here = None, plane(0)
         for x in range(width):
             after = plane(x + 1) if x + 1 < width else None
-            au = applied(before, here, after, [6.0 + s[x, rows, h * LANES : (h + 1) * LANES] for h in range(2)])
+            au = applied(before, here, after, [6.0 + s[x, rows, h * LANES : (h + 1) * LANES] for h in range(2)], edges)
             for c in range(3):
                 for h in range(2):
                     r0[c, x, h, rows, :] = b[c, x, rows, h * LANES : (h + 1) * LANES] - au[c][h]
             before, here = here, after
         return carry
 
-    lax.fori_loop(0, height // SUB, step, 0)
+    lax.fori_loop(0, height // SUB, step, 0, unroll=2)
 
     def pack(out, edge, second):
         for c in range(3):
@@ -305,16 +305,13 @@
         inside = inside_rows(e * own + 2 * RIM * e - SUB * e, own, "narrow")
 
         def plane(x):
-            return Plane(
-                lambda c, dy: [ue[e, c, x, h, pl.ds(PAD + dy, SUB), :] for h in range(2)],
-                edges,
-            )
+            return Plane(lambda c, dy: [ue[e, c, x, h, pl.ds(PAD + dy, SUB), :] for h in range(2)])
 
         before, here = None, plane(0)
         tile = pl.ds(PAD, SUB)
         for x in range(width):
             after = plane(x + 1) if x + 1 < width else None
-            au = applied(before, here, after, [6.0 + se[e, x, h, tile, :] for h in range(2)])
+            au = applied(before, here, after, [6.0 + se[e, x, h, tile, :] for h in range(2)], edges)
             for c in range(3):
                 for h in range(2):
                     r_end[e, c, x, h] = jnp.where(inside, be[e, c, x, h, tile, :] - au[c][h], 0.0)
@@ -323,7 +320,7 @@
             before, here = here, after
         return carry
 
-    lax.fori_loop(0, 2, step, 0)
+    lax.fori_loop(0, 2, step, 0, unroll=2)
 
     def pack(out, main, edge, second):
         for k in range(10):
@@ -424,7 +421,7 @@
     middle = slice(PAD + SUB, PAD + height)
     tile_rows = [slice(PAD, PAD + SUB), slice(PAD + height, PAD + height + SUB)]
     even_x = is_even("wide")
-    zr[...] = z_matrix(rest_zt)
+    zr[0], zr[1] = split(z_matrix(rest_zt))
 
     def place(from_left, from_right, mine_left, mine_right):
         for k in range(10):
@@ -465,37 +462,34 @@
         rows = pl.ds(start, SUB)
         inside = inside_rows(t * SUB, height, "narrow")
 
-        def plane(ref, first):
-            return Plane(
-                lambda c, dy: [ref[first + c, h, pl.ds(start + dy, SUB), :] for h in range(2)],
-                edges,
-            )
-
-        out_left = plane(left, 6)
-        in_left = plane(u_left, 0)
-        in_right = plane(u_right, 0)
-        out_right = plane(right, 6)
+        def of(ref, first):
+            return shares(lambda c, dy: [ref[first + c, h, pl.ds(start + dy, SUB), :] for h in range(2)], edges)
+
+        out_left, _ = of(left, 6)
+        _, in_left = of(u_left, 0)
+        in_right, _ = of(u_right, 0)
+        _, out_right = of(right, 6)
         inside_left = inside & has_left
         inside_right = inside & has_right
         for c in range(3):
             for h in range(2):
                 r0[c, 0, h, rows, :] = left[3 + c, h, rows, :]
                 r0[c, 1, h, rows, :] = jnp.where(
-                    inside_left, left[c, h, rows, :] + in_left.behind[c][h], 0.0
+                    inside_left, left[c, h, rows, :] + in_left[c][h], 0.0
                 )
                 r0[c, 2, h, rows, :] = jnp.where(
-                    inside, r0[c, 2, h, rows, :] + out_left.ahead[c][h], 0.0
+                    inside, r0[c, 2, h, rows, :] + out_left[c][h], 0.0
                 )
                 r0[c, width + 1, h, rows, :] = jnp.where(
-                    inside, r0[c, width + 1, h, rows, :] + out_right.behind[c][h], 0.0
+                    inside, r0[c, width + 1, h, rows, :] + out_right[c][h], 0.0
                 )
                 r0[c, width + 2, h, rows, :] = jnp.where(
-                    inside_right, right[c, h, rows, :] + in_right.ahead[c][h], 0.0
+                    inside_right, right[c, h, rows, :] + in_right[c][h], 0.0
                 )
                 r0[c, width + 3, h, rows, :] = right[3 + c, h, rows, :]
         return carry
 
-    lax.fori_loop(0, tiles, fix, 0)
+    lax.fori_loop(0, tiles, fix, 0, unroll=3)
 
     def first_step(t, carry):
         start = PAD + t * SUB
@@ -503,10 +497,7 @@
         inside = inside_rows(t * SUB, height, "narrow")
 
         def plane(x):
-            return Plane(
-                lambda c, dy: [r0[c, x + 2, h, pl.ds(start + dy, SUB), :] for h in range(2)],
-                edges,
-            )
+            return Plane(lambda c, dy: [r0[c, x + 2, h, pl.ds(start + dy, SUB), :] for h in range(2)])
 
         before, here = plane(-2), plane(-1)
         for x in range(-1, width + 1):
@@ -514,7 +505,7 @@
             keep = inside & has_left if x < 0 else inside & has_right if x == width else inside
             source = left.at[9] if x < 0 else right.at[9] if x == width else s_ext.at[x]
             diagonal = [6.0 + source[h, rows, :] for h in range(2)]
-            ar = applied(before, here, after, diagonal)
+            ar = applied(before, here, after, diagonal, edges)
             for c in range(3):
                 for h in range(2):
                     old = here.v[c][h]
@@ -525,7 +516,7 @@
             before, here = here, after
         return carry
 
-    lax.fori_loop(0, tiles, first_step, 0)
+    lax.fori_loop(0, tiles, first_step, 0, unroll=3)
 
     def second_step(t, carry):
         start = PAD + RIM + t * SUB
@@ -533,16 +524,13 @@
         to = pl.ds(pl.multiple_of(t * SUB, SUB), SUB)
 
         def plane(x):
-            return Plane(
-                lambda c, dy: [d1[c, x + 1, h, pl.ds(start + dy, SUB), :] for h in range(2)],
-                edges,
-            )
+            return Plane(lambda c, dy: [d1[c, x + 1, h, pl.ds(start + dy, SUB), :] for h in range(2)])
 
         before, here = plane(-1), plane(0)
         for x in range(width):
             after = plane(x + 1)
             diagonal = [6.0 + s_ext[x, h, rows, :] for h in range(2)]
-            ad = applied(before, here, after, diagonal)
+            ad = applied(before, here, after, diagonal, edges)
             for c in range(3):
                 for h in range(2):
                     lanes = slice(h * LANES, (h + 1) * LANES)
@@ -552,13 +540,14 @@
             before, here = here, after
         return carry
 
-    lax.fori_loop(0, height // SUB, second_step, 0)
+    lax.fori_loop(0, height // SUB, second_step, 0, unroll=2)
 
     coarse_width = width // 2
     coarse_height = height // 2
     coarse_rows = coarse_height + 2 * RIM
     first_weight = place_x * coarse_width
     lead = 2 * RIM + 2
+    zr_halves = zr[0], zr[1]
     for c in range(3):
         for i in range(-1, coarse_width + 1):
             k = c * (coarse_width + 2) + i + 1
@@ -573,9 +562,7 @@
             joined = jnp.concatenate(halves, axis=1)
             t_pad[k, 0:lead, :] = jnp.zeros((lead, LANES), F32)
             t_pad[k, lead + height :, :] = jnp.zeros((t_pad.shape[1] - lead - height, LANES), F32)
-            t_pad[k, lead : lead + height, :] = jnp.dot(
-                joined, zr[...], precision=lax.Precision.HIGHEST, preferred_element_type=F32
-            )
+            t_pad[k, lead : lead + height, :] = product(joined, zr_halves, 0)
     weights = [y_weights(rest_y, a, coarse_rows, coarse_height) for a in range(5)]
     even_y = is_even("narrow")
     for c in range(3):
@@ -601,6 +588,21 @@
     def _():
         send(near, 0)
         send(far, coarse_rows - SUB)
+
+
+def split(x):
+    high = x.astype(jnp.bfloat16)
+    return high, (x - high.astype(F32)).astype(jnp.bfloat16)
+
+
+def product(x, halves, contract):
+    high, low = split(x)
+    dims = (((1,), (contract,)), ((), ()))
+
+    def dot(p, q):
+        return lax.dot_general(p, q, dims, preferred_element_type=F32)
+
+    return dot(high, halves[0]) + (dot(high, halves[1]) + dot(low, halves[0]))
 
 
 SMEM = pl.BlockSpec(memory_space=pltpu.SMEM)
@@ -637,7 +639,7 @@
             field(3, width),
             pltpu.VMEM((3, width, 2, height, LANES), F32),
             pltpu.VMEM((planes, 2 * coarse_rows + 2 * SUB, LANES), F32),
-            pltpu.VMEM((2 * LANES, LANES), F32),
+            pltpu.VMEM((2, 2 * LANES, LANES), jnp.bfloat16),
         ],
         compiler_params=params(),
         cost_estimate=cost(10),
@@ -770,7 +772,7 @@
                     total[c, i, to, :] = first
         return carry
 
-    lax.fori_loop(0, tiles, start_rows, 0)
+    lax.fori_loop(0, tiles, start_rows, 0, unroll=5)
 
     for k in range(3):
         factor_d, factor_r = factors[k]
@@ -782,20 +784,20 @@
             inside = inside_rows(t * SUB, own, "narrow")
 
             def plane(x):
-                return Plane(lambda c, dy: [d[c, x + reach, pl.ds(start + dy, SUB), :]], edges)
+                return Plane(lambda c, dy: [d[c, x + reach, pl.ds(start + dy, SUB), :]])
 
             before, here = plane(-rim - 1), plane(-rim)
             for x in range(-rim, width + rim):
                 after = plane(x + 1)
                 keep = inside & has_left if x < 0 else inside & has_right if x >= width else inside
-                ad = applied(before, here, after, [6.0 + sc[x + 2, pl.ds(t * SUB, SUB), :]])
+                ad = applied(before, here, after, [6.0 + sc[x + 2, pl.ds(t * SUB, SUB), :]], edges)
                 for c in range(3):
                     new = r[c, x + reach, rows, :] - ad[c][0]
                     r[c, x + reach, rows, :] = jnp.where(keep, new, 0.0)
                 before, here = here, after
             return carry
 
-        lax.fori_loop(0, tiles, residual_step, 0)
+        lax.fori_loop(0, tiles, residual_step, 0, unroll=5)
 
         def direction_step(t, carry, rim=rim, factor_d=factor_d, factor_r=factor_r):
             rows = pl.ds(pl.multiple_of(PAD + t * SUB, SUB), SUB)
@@ -807,7 +809,7 @@
                         total[c, x, rows, :] = total[c, x, rows, :] + new
             return carry
 
-        lax.fori_loop(0, tiles, direction_step, 0)
+        lax.fori_loop(0, tiles, direction_step, 0, unroll=5)
 
     for c in range(3):
         for x in range(width):
@@ -867,7 +869,7 @@
     fine_width = 2 * width
     even_x = is_even("wide")
     first_weight = lax.axis_index("wide") * width
-    zr = z_matrix(rest_zt)
+    zr = split(z_matrix(rest_zt))
     for a in range(5):
         wy[a] = y_weights(rest_y, a, height, own)
 
@@ -902,9 +904,7 @@
             grown[x, pl.ds(0, own, stride=2), :] = at(0, 1) + at(2, 0) + at(4, -1)
             grown[x, pl.ds(1, own, stride=2), :] = at(1, 1) + at(3, 0)
         flat = grown[...].reshape(fine_width * 2 * own, LANES)
-        wide = lax.dot_general(
-            flat, zr, (((1,), (1,)), ((), ())), precision=lax.Precision.HIGHEST, preferred_element_type=F32
-        )
+        wide = product(flat, zr, 1)
         out[c] = smooth[c] + wide.reshape(fine_width, 2 * own, 2 * LANES)
 
 
@@ -928,21 +928,23 @@
     )(rest_x, corr, got_near, got_far, smooth, rest_y, rest_zt)
 
 
-def gather(own, edges):
+def gather(own, edges, prolonged):
     count = lax.axis_size("narrow")
-    n = lax.axis_index("narrow")
 
     def ring(x, by):
         return lax.ppermute(x, "narrow", [(i, (i + by) % count) for i in range(count)])
 
+    after = lax.optimization_barrier
     pair = swap_near(own, "narrow")
     low, high = ring(own, 2), ring(own, -2)
-    pair, low, high = lax.optimization_barrier((pair, low, high))
-    pair_low, pair_high = ring(pair, 2), ring(pair, -2)
-    pair_high, edges = lax.optimization_barrier((pair_high, edges))
-    far_own, far_pair = ring(low, 2), ring(pair_high, -2)
-    blocks = [own, pair, low, high, pair_low, pair_high, far_own, far_pair]
-    return blocks, edges
+    def across(x, by):
+        return lax.ppermute(x, "narrow", [(i, ((i + by) % count) ^ 1) for i in range(count)])
+
+    pair_low, pair_high = across(own, 2), across(own, -2)
+    first, second, edges = after((low, pair_high, edges))
+    far_own, far_pair = ring(first, 2), ring(second, -2)
+    result = prolonged(edges)
+    return [own, pair, low, high, pair_low, pair_high, far_own, far_pair], result
 
 
 def assemble_kernel(*refs):
@@ -995,9 +997,10 @@
     q, s_win, *sent = rows(partial, *got, coarse_reaction)
     got = swap_both(sent, "wide")
     corr, own, *sent = coarse_solve(coarse_bounds, q, s_win, *got)
-    got_near, got_far = swap_both(sent, "wide")
-    blocks, (got_near, got_far) = gather(own, (got_near, got_far))
-    solution_block = prolong(x_weights, corr, got_near, got_far, smooth, y_padded, z_weights)
+    edges = swap_both(sent, "wide")
+    blocks, solution_block = gather(
+        own, edges, lambda edges: prolong(x_weights, corr, *edges, smooth, y_padded, z_weights)
+    )
     return solution_block, assemble(blocks)
 
 

time: 91.4 us -> 81.5 us (0.89)
  waiting for transfers between devices: 35.2 us -> 23.3 us
  starting transfers between devices: 30 us -> 37.4 us
  Pallas kernels: 24.9 us -> 19.5 us
    ppermute x0 -> x2, starting transfers between devices: none -> 7.42 us  [across(): lax.ppermute(x, 'narrow', [(i, (i + by) % count ^ 1) for i in range(count)])]
    ppermute x6 -> x4, waiting for transfers between devices: 7.36 us -> 0.72 us  [ring(): lax.ppermute(x, 'narrow', [(i, (i + by) % count) for i in range(count)])]
    ppermute x5, waiting for transfers between devices: 25.9 us -> 20.2 us  [swap_far(): return lax.ppermute(x, axis, up + [(j, i) for i, j in up])]
    pallas_call x1, Pallas kernels: 9.98 us -> 7.34 us  [smoothing(): pl.pallas_call(smooth_kernel, in_specs=[SMEM, SMEM] + [VMEM] * 11, out_sh...]
    ppermute x6 -> x4, starting transfers between devices: 10.5 us -> 8.12 us  [ring(): lax.ppermute(x, 'narrow', [(i, (i + by) % count) for i in range(count)])]
    pallas_call x1, Pallas kernels: 3.06 us -> 1.61 us  [coarse_solve(): pl.pallas_call(coarse_kernel, in_specs=[SMEM] + [VMEM] * 4, out_shape=[ja...]
    ppermute x6, starting transfers between devices: 7.61 us -> 8.92 us  [swap_near(): return lax.ppermute(x, axis, [(i, i ^ 1) for i in range(count)])]
    ppermute x5, starting transfers between devices: 11.9 us -> 12.9 us  [swap_far(): return lax.ppermute(x, axis, up + [(j, i) for i, j in up])]
  transfers between devices with their start and end apart: 17 -> 17, of which waited for: 9 -> 7; matrix products, arithmetic and copies ran while one was open for 0% -> 0% of each run, Pallas kernels for 8% -> 8%
where the time goes in v2:
time: 81.5 us; the launch traced here: 81.3 us
  starting transfers between devices  37.4 us (46%)
  waiting for transfers between devices  23.3 us (29%)
  Pallas kernels  19.5 us (24%)
  between operations  0.85 us (1%)
    ppermute x5, waiting for transfers between devices, swap_far(): return lax.ppermute(x, axis, up + [(j, i) for i, j in up])  20.2 us
    ppermute x5, starting transfers between devices, swap_far(): return lax.ppermute(x, axis, up + [(j, i) for i, j in up])  12.9 us
    ppermute x6, starting transfers between devices, swap_near(): return lax.ppermute(x, axis, [(i, i ^ 1) for i in range(count)])  8.92 us
    ppermute x4, starting transfers between devices, ring(): lax.ppermute(x, 'narrow', [(i, (i + by) % count) for i in range(count)])  8.12 us
    ppermute x2, starting transfers between devices, across(): lax.ppermute(x, 'narrow', [(i, (i + by) % count ^ 1) for i in range(count)])  7.42 us
    pallas_call x1, Pallas kernels, smoothing(): pl.pallas_call(smooth_kernel, in_specs=[SMEM, SMEM] + [VMEM] * 11, out_sh...  7.34 us
    pallas_call x1, Pallas kernels, prolong(): pl.pallas_call(prolong_kernel, in_specs=[SMEM] + [VMEM] * 6, out_shape=ja...  3.36 us
    pallas_call x1, Pallas kernels, residual(): pl.pallas_call(residual_kernel, out_shape=[pltpu.HBM((3, width, 2, height...  2.75 us
  transfers between devices with their start and end apart: 17, of which 7 were waited for; matrix products, arithmetic and copies ran while one was open for 0% of the time, Pallas kernels for 8%

profile of v2, /device:TPU:16, one launch (start us, length us, event | category | flops | bytes accessed | tf_op | source)
XLA Modules:
  0.0 81.3 jit_solution(1508894151536238146)
XLA Ops:
  0.7 1.5 %pack_y.1 = (f32[2,136,128]{2,1,0:T(8,128)S(1)}, f32[2,136,128]{2,1,0:T(8,128)S(1)}) custom-call(f32[3,8,64,256]{3,2,1,0:T(8,128)} %u.3, f32[3,8,64,256]{3,2,1,0:T(8,128)} %u.3, f32[3,8,64,256]{3,2,1,0:T(8,128)} %refs_3_.1, f32[3,8,64,256]{3,2,1,0:T(8,128)} %refs_3_.1, f32[8,64,256]{2,1,0:T(8,128)} %s.4, f32[8,64,256]{2,1,0:T(8,128)} %s.4), custom_call_target="tpu_custom_call" | custom-call | bytes 3690000 | tf_op jit(solution)/shard_map/pack_y/pallas_call | solution.py:178
  2.1 1.4 %collective-permute-start = (f32[2,136,128]{2,1,0:T(8,128)S(1)}, f32[2,136,128]{2,1,0:T(8,128)S(1)}, u32[]{:S(2)}, u32[]{:S(2)}) collective-permute-start(f32[2,136,128]{2,1,0:T(8,128)S(1)} %get-tuple-element.28), channel_id=1, source_target_pairs={{0,1},{1,0},{2,3},{3,2},{4,5},{5,4},{6,7},{7,6},{8,9},{9,8},{10,11... | collective-permute-start | bytes 417800 | tf_op jit(solution)/shard_map/ppermute | solution.py:27
  4.2 2.8 %residual.1 = (f32[3,8,2,64,128]{4,3,2,1,0:T(8,128)}, f32[10,2,64,128]{3,2,1,0:T(8,128)S(1)}, f32[10,2,64,128]{3,2,1,0:T(8,128)S(1)}) custom-call(f32[3,8,64,256]{3,2,1,0:T(8,128)S(1)} %copy-done, f32[3,8,64,256]{3,2,1,0:T(8,128)S(1)} %copy-done.1, f32[8,64,256]{2,1,0:T(8,128)S(1)} %copy-done.2), custom_call_target="tpu_custom_call" | custom-call | bytes 11070000 | tf_op jit(solution)/shard_map/residual/pallas_call | solution.py:254
  6.9 0.7 collective-permute-done.refs_6_
  7.6 1.6 %ends.1 = (f32[2,3,8,2,8,128]{5,4,3,2,1,0:T(8,128)}, f32[2,8,2,8,128]{4,3,2,1,0:T(8,128)}, f32[10,2,72,128]{3,2,1,0:T(8,128)S(1)}, f32[10,2,72,128]{3,2,1,0:T(8,128)}) custom-call(f32[3,8,64,256]{3,2,1,0:T(8,128)S(1)} %copy-done, f32[3,8,64,256]{3,2,1,0:T(8,128)S(1)} %copy-done, f32[3,8,64,256]{3,2,1,0:T(8,128)S(1)} %copy-done.1, ...), custom_call_target="tpu_custom_call" | custom-call | bytes 147600000 | tf_op jit(solution)/shard_map/ends/pallas_call | solution.py:368
  9.3 4.5 %collective-permute-start.3 = (f32[10,2,72,128]{3,2,1,0:T(8,128)}, f32[10,2,72,128]{3,2,1,0:T(8,128)}, u32[]{:S(2)}, u32[]{:S(2)}) collective-permute-start(f32[10,2,72,128]{3,2,1,0:T(8,128)} %get-tuple-element.35.sent_far), channel_id=1, source_target_pairs={{8,16},{24,32},{40,48},{56,64},{72,80},{88,96},{104,112},{16,8},{3... | collective-permute-start | bytes 2211848 | tf_op jit(solution)/shard_map/ppermute | solution.py:33
  14.1 11.8 %collective-permute-done.3.got_far = f32[10,2,72,128]{3,2,1,0:T(8,128)} collective-permute-done((f32[10,2,72,128]{3,2,1,0:T(8,128)}, f32[10,2,72,128]{3,2,1,0:T(8,128)}, u32[]{:S(2)}, u32[]{:S(2)}) %collective-permute-start.3) | collective-permute-done | bytes 737312 | tf_op jit(solution)/shard_map/ppermute | solution.py:33
  26.0 7.3 %smoothing.1 = (f32[3,8,64,256]{3,2,1,0:T(8,128)S(1)}, f32[3,6,40,128]{3,2,1,0:T(8,128)S(1)}, f32[18,8,128]{2,1,0:T(8,128)S(1)}, f32[18,8,128]{2,1,0:T(8,128)S(1)}) custom-call(f32[2]{0:T(128)S(1)} %copy-done.6, f32[66,5]{1,0:T(8,128)S(1)} %pad.8.rest_x, f32[3,8,2,64,128]{4,3,2,1,0:T(8,128)} %get-tuple-element.27.r0p, ...), custom_call_target="tpu_custom_call" | custom-call | bytes 36900000 | tf_op jit(solution)/shard_map/smoothing/pallas_call | solution.py:622
  33.3 5.8 %collective-permute-start.4 = (f32[18,8,128]{2,1,0:T(8,128)S(1)}, f32[18,8,128]{2,1,0:T(8,128)S(1)}, u32[]{:S(2)}, u32[]{:S(2)}) collective-permute-start(f32[18,8,128]{2,1,0:T(8,128)S(1)} %get-tuple-element.37), channel_id=1, source_target_pairs={{0,1},{1,0},{2,3},{3,2},{4,5},{5,4},{6,7},{7,6},{8,9},{9,8},{10,11... | collective-permute-start | bytes 221192 | tf_op jit(solution)/shard_map/ppermute | solution.py:27
  39.8 1.7 %collective-permute-done.4.got_near = f32[18,8,128]{2,1,0:T(8,128)S(1)} collective-permute-done((f32[18,8,128]{2,1,0:T(8,128)S(1)}, f32[18,8,128]{2,1,0:T(8,128)S(1)}, u32[]{:S(2)}, u32[]{:S(2)}) %collective-permute-start.4) | collective-permute-done | bytes 73760 | tf_op jit(solution)/shard_map/ppermute | solution.py:27
  41.7 4.0 %collective-permute-start.7 = (f32[14,40,128]{2,1,0:T(8,128)S(1)}, f32[14,40,128]{2,1,0:T(8,128)S(1)}, u32[]{:S(2)}, u32[]{:S(2)}) collective-permute-start(f32[14,40,128]{2,1,0:T(8,128)S(1)} %get-tuple-element.42), channel_id=1, source_target_pairs={{8,16},{24,32},{40,48},{56,64},{72,80},{88,96},{104,112},{16,8},{3... | collective-permute-start | bytes 860168 | tf_op jit(solution)/shard_map/ppermute | solution.py:33
  45.7 7.6 %collective-permute-done.7.got_far = f32[14,40,128]{2,1,0:T(8,128)S(1)} collective-permute-done((f32[14,40,128]{2,1,0:T(8,128)S(1)}, f32[14,40,128]{2,1,0:T(8,128)S(1)}, u32[]{:S(2)}, u32[]{:S(2)}) %collective-permute-start.7) | collective-permute-done | bytes 286752 | tf_op jit(solution)/shard_map/ppermute | solution.py:33
  53.2 1.6 %coarse_solve.1 = (f32[3,4,40,128]{3,2,1,0:T(8,128)S(1)}, f32[3,4,32,128]{3,2,1,0:T(8,128)S(1)}, f32[3,40,128]{2,1,0:T(8,128)S(1)}, f32[3,40,128]{2,1,0:T(8,128)S(1)}) custom-call(f32[2]{0:T(128)S(1)} %copy-done.5, f32[3,6,40,128]{3,2,1,0:T(8,128)S(1)} %get-tuple-element.39.q, f32[4,40,128]{2,1,0:T(8,128)S(1)} %get-tuple-element.40.s_win, ...), custom_call_target="tpu_custom_call" | custom-call | bytes 11070000 | tf_op jit(solution)/shard_map/coarse_solve/pallas_call | solution.py:843
  54.9 4.2 %collective-permute-start.9 = (f32[3,4,32,128]{3,2,1,0:T(8,128)S(1)}, f32[3,4,32,128]{3,2,1,0:T(8,128)S(1)}, u32[]{:S(2)}, u32[]{:S(2)}) collective-permute-start(f32[3,4,32,128]{3,2,1,0:T(8,128)S(1)} %get-tuple-element.44.refs_0_), channel_id=1, source_target_pairs={{0,7},{1,6},{2,1},{3,0},{4,3},{5,2},{6,5},{7,4},{8,15},{9,14},{10,... | collective-permute-start | bytes 589832 | tf_op jit(solution)/shard_map/ppermute | solution.py:941
  59.0 2.8 %collective-permute-start.8 = (f32[3,4,32,128]{3,2,1,0:T(8,128)S(1)}, f32[3,4,32,128]{3,2,1,0:T(8,128)S(1)}, u32[]{:S(2)}, u32[]{:S(2)}) collective-permute-start(f32[3,4,32,128]{3,2,1,0:T(8,128)S(1)} %get-tuple-element.44.refs_0_), channel_id=1, source_target_pairs={{0,2},{1,3},{2,4},{3,5},{4,6},{5,7},{6,0},{7,1},{8,10},{9,11},{10,... | collective-permute-start | bytes 589832 | tf_op jit(solution)/shard_map/ppermute | solution.py:935
  61.8 3.1 %collective-permute-start.11 = (f32[3,40,128]{2,1,0:T(8,128)S(1)}, f32[3,40,128]{2,1,0:T(8,128)S(1)}, u32[]{:S(2)}, u32[]{:S(2)}) collective-permute-start(f32[3,40,128]{2,1,0:T(8,128)S(1)} %get-tuple-element.46), channel_id=1, source_target_pairs={{8,16},{24,32},{40,48},{56,64},{72,80},{88,96},{104,112},{16,8},{3... | collective-permute-start | bytes 184328 | tf_op jit(solution)/shard_map/ppermute | solution.py:33
  64.9 3.2 %collective-permute-start.14 = (f32[3,4,32,128]{3,2,1,0:T(8,128)S(1)}, f32[3,4,32,128]{3,2,1,0:T(8,128)S(1)}, u32[]{:S(2)}, u32[]{:S(2)}) collective-permute-start(f32[3,4,32,128]{3,2,1,0:T(8,128)S(1)} %get-tuple-element.44.refs_0_), channel_id=1, source_target_pairs={{0,3},{1,2},{2,5},{3,4},{4,7},{5,6},{6,1},{7,0},{8,11},{9,10},{10,... | collective-permute-start | bytes 589832 | tf_op jit(solution)/shard_map/ppermute | solution.py:941
  68.2 2.0 %collective-permute-start.13 = (f32[3,4,32,128]{3,2,1,0:T(8,128)S(1)}, f32[3,4,32,128]{3,2,1,0:T(8,128)S(1)}, u32[]{:S(2)}, u32[]{:S(2)}) collective-permute-start(f32[3,4,32,128]{3,2,1,0:T(8,128)S(1)} %get-tuple-element.44.refs_0_), channel_id=1, source_target_pairs={{0,6},{1,7},{2,0},{3,1},{4,2},{5,3},{6,4},{7,5},{8,14},{9,15},{10,... | collective-permute-start | bytes 589832 | tf_op jit(solution)/shard_map/ppermute | solution.py:935
  70.2 0.8 collective-permute-done.11.got_far
  71.0 1.7 %collective-permute-start.12 = (f32[3,4,32,128]{3,2,1,0:T(8,128)S(1)}, f32[3,4,32,128]{3,2,1,0:T(8,128)S(1)}, u32[]{:S(2)}, u32[]{:S(2)}) collective-permute-start(f32[3,4,32,128]{3,2,1,0:T(8,128)S(1)} %get-tuple-element.44.refs_0_), channel_id=1, source_target_pairs={{0,1},{1,0},{2,3},{3,2},{4,5},{5,4},{6,7},{7,6},{8,9},{9,8},{10,11... | collective-permute-start | bytes 589832 | tf_op jit(solution)/shard_map/ppermute | solution.py:27
  72.7 1.7 %collective-permute-start.15 = (f32[3,4,32,128]{3,2,1,0:T(8,128)S(1)}, f32[3,4,32,128]{3,2,1,0:T(8,128)S(1)}, u32[]{:S(2)}, u32[]{:S(2)}) collective-permute-start(f32[3,4,32,128]{3,2,1,0:T(8,128)S(1)} %collective-permute-done.8.refs_2_), channel_id=1, source_target_pairs={{0,2},{1,3},{2,4},{3,5},{4,6},{5,7},{6,0},{7,1},{8,10},{9,11},{10,... | collective-permute-start | bytes 589832 | tf_op jit(solution)/shard_map/ppermute | solution.py:935
  74.4 1.6 %collective-permute-start.16 = (f32[3,4,32,128]{3,2,1,0:T(8,128)S(1)}, f32[3,4,32,128]{3,2,1,0:T(8,128)S(1)}, u32[]{:S(2)}, u32[]{:S(2)}) collective-permute-start(f32[3,4,32,128]{3,2,1,0:T(8,128)S(1)} %collective-permute-done.9.refs_5_), channel_id=1, source_target_pairs={{0,6},{1,7},{2,0},{3,1},{4,2},{5,3},{6,4},{7,5},{8,14},{9,15},{10,... | collective-permute-start | bytes 589832 | tf_op jit(solution)/shard_map/ppermute | solution.py:935
  76.0 3.4 %prolong.1 = f32[3,8,64,256]{3,2,1,0:T(8,128)} custom-call(f32[66,5]{1,0:T(8,128)S(1)} %pad.8.rest_x, f32[3,4,40,128]{3,2,1,0:T(8,128)S(1)} %get-tuple-element.43.corr, f32[3,40,128]{2,1,0:T(8,128)S(1)} %collective-permute-done.10.got_near, f32[3,40,128]{2,1,0:T(8,128)S(1)} %collective-permute-done.11.got_far, ...), custom_call_target="tpu_custom_call" | custom-call | bytes 44280000 | tf_op jit(solution)/shard_map/prolong/pallas_call | solution.py:914
  80.0 1.3 %assemble.1 = f32[3,4,256,128]{3,2,1,0:T(8,128)} custom-call(f32[3,4,32,128]{3,2,1,0:T(8,128)S(1)} %get-tuple-element.44.refs_0_, f32[3,4,32,128]{3,2,1,0:T(8,128)S(1)} %collective-permute-done.12.refs_1_, f32[3,4,32,128]{3,2,1,0:T(8,128)S(1)} %collective-permute-done.8.refs_2_, f32[3,4,32,128]{3,2,1,0:T(8,128)S(1)} %collective-permute-done.13.refs_3_, ...), custom_call_target="tpu_custom_call" | custom-call | bytes 3690000 | tf_op jit(solution)/shard_map/assemble/pallas_call | solution.py:964
  (40 shorter events, 2.5 us)
Async XLA Ops:
  0.6 3.5 %copy-start.2 = (f32[8,64,256]{2,1,0:T(8,128)S(1)}, f32[8,64,256]{2,1,0:T(8,128)}, u32[]{:S(2)}) copy-start(f32[8,64,256]{2,1,0:T(8,128)} %s.4) | copy-start | bytes 1572868
  2.1 5.5 %collective-permute-start = (f32[2,136,128]{2,1,0:T(8,128)S(1)}, f32[2,136,128]{2,1,0:T(8,128)S(1)}, u32[]{:S(2)}, u32[]{:S(2)}) collective-permute-start(f32[2,136,128]{2,1,0:T(8,128)S(1)} %get-tuple-element.28), channel_id=1, source_target_pairs={{0,1},{1,0},{2,3},{3,2},{4,5},{5,4},{6,7},{7,6},{8,9},{9,8},{10,11... | collective-permute-start | bytes 417800 | tf_op jit(solution)/shard_map/ppermute | solution.py:27
  3.5 4.1 %collective-permute-start.1 = (f32[2,136,128]{2,1,0:T(8,128)S(1)}, f32[2,136,128]{2,1,0:T(8,128)S(1)}, u32[]{:S(2)}, u32[]{:S(2)}) collective-permute-start(f32[2,136,128]{2,1,0:T(8,128)S(1)} %get-tuple-element.29), channel_id=1, source_target_pairs={{1,2},{3,4},{5,6},{2,1},{4,3},{6,5},{9,10},{11,12},{13,14},{10,9},... | collective-permute-start | bytes 417800 | tf_op jit(solution)/shard_map/ppermute | solution.py:33
  7.6 6.2 %copy-start.8 = (f32[64,5]{0,1:T(8,128)S(1)}, f32[64,5]{0,1:T(8,128)}, u32[]{:S(2)}) copy-start(f32[64,5]{0,1:T(8,128)} %param.13) | copy-start | bytes 3844
  7.6 6.3 %copy-start.7 = (f32[256,5]{0,1:T(8,128)S(1)}, f32[256,5]{0,1:T(8,128)}, u32[]{:S(2)}) copy-start(f32[256,5]{0,1:T(8,128)} %param.14) | copy-start | bytes 15364
  7.6 18.4 %copy-start.4 = (f32[128,5]{0,1:T(8,128)S(1)}, f32[128,5]{0,1:T(8,128)}, u32[]{:S(2)}) copy-start(f32[128,5]{0,1:T(8,128)} %param.15) | copy-start | bytes 7684
  7.6 18.4 %copy-start.6 = (f32[2]{0:T(128)S(1)}, f32[2]{0:T(128)}, u32[]{:S(2)}) copy-start(f32[2]{0:T(128)} %bounds.2) | copy-start | bytes 28
  9.3 4.8 %collective-permute-start.2 = (f32[10,2,72,128]{3,2,1,0:T(8,128)S(1)}, f32[10,2,72,128]{3,2,1,0:T(8,128)}, u32[]{:S(2)}, u32[]{:S(2)}) collective-permute-start(f32[10,2,72,128]{3,2,1,0:T(8,128)S(1)} %get-tuple-element.34.sent_near), channel_id=1, source_target_pairs={{0,8},{8,0},{16,24},{24,16},{32,40},{40,32},{48,56},{56,48},{64,72... | collective-permute-start | bytes 2211848 | tf_op jit(solution)/shard_map/ppermute | solution.py:27
  9.3 16.7 %collective-permute-start.3 = (f32[10,2,72,128]{3,2,1,0:T(8,128)}, f32[10,2,72,128]{3,2,1,0:T(8,128)}, u32[]{:S(2)}, u32[]{:S(2)}) collective-permute-start(f32[10,2,72,128]{3,2,1,0:T(8,128)} %get-tuple-element.35.sent_far), channel_id=1, source_target_pairs={{8,16},{24,32},{40,48},{56,64},{72,80},{88,96},{104,112},{16,8},{3... | collective-permute-start | bytes 2211848 | tf_op jit(solution)/shard_map/ppermute | solution.py:33
  26.0 15.5 %copy-start.3 = (f32[4,256,128]{2,1,0:T(8,128)S(1)}, f32[4,256,128]{2,1,0:T(8,128)}, u32[]{:S(2)}) copy-start(f32[4,256,128]{2,1,0:T(8,128)} %s.5) | copy-start | bytes 1572868
  26.0 27.3 %copy-start.5 = (f32[2]{0:T(128)S(1)}, f32[2]{0:T(128)}, u32[]{:S(2)}) copy-start(f32[2]{0:T(128)} %bounds.3) | copy-start | bytes 28
  33.3 8.1 %collective-permute-start.4 = (f32[18,8,128]{2,1,0:T(8,128)S(1)}, f32[18,8,128]{2,1,0:T(8,128)S(1)}, u32[]{:S(2)}, u32[]{:S(2)}) collective-permute-start(f32[18,8,128]{2,1,0:T(8,128)S(1)} %get-tuple-element.37), channel_id=1, source_target_pairs={{0,1},{1,0},{2,3},{3,2},{4,5},{5,4},{6,7},{7,6},{8,9},{9,8},{10,11... | collective-permute-start | bytes 221192 | tf_op jit(solution)/shard_map/ppermute | solution.py:27
  39.1 2.3 %collective-permute-start.5 = (f32[18,8,128]{2,1,0:T(8,128)S(1)}, f32[18,8,128]{2,1,0:T(8,128)S(1)}, u32[]{:S(2)}, u32[]{:S(2)}) collective-permute-start(f32[18,8,128]{2,1,0:T(8,128)S(1)} %get-tuple-element.38), channel_id=1, source_target_pairs={{1,2},{3,4},{5,6},{2,1},{4,3},{6,5},{9,10},{11,12},{13,14},{10,9},... | collective-permute-start | bytes 221192 | tf_op jit(solution)/shard_map/ppermute | solution.py:33
  41.6 4.1 %collective-permute-start.6 = (f32[14,40,128]{2,1,0:T(8,128)S(1)}, f32[14,40,128]{2,1,0:T(8,128)S(1)}, u32[]{:S(2)}, u32[]{:S(2)}) collective-permute-start(f32[14,40,128]{2,1,0:T(8,128)S(1)} %get-tuple-element.41), channel_id=1, source_target_pairs={{0,8},{8,0},{16,24},{24,16},{32,40},{40,32},{48,56},{56,48},{64,72... | collective-permute-start | bytes 860168 | tf_op jit(solution)/shard_map/ppermute | solution.py:27
  41.7 11.6 %collective-permute-start.7 = (f32[14,40,128]{2,1,0:T(8,128)S(1)}, f32[14,40,128]{2,1,0:T(8,128)S(1)}, u32[]{:S(2)}, u32[]{:S(2)}) collective-permute-start(f32[14,40,128]{2,1,0:T(8,128)S(1)} %get-tuple-element.42), channel_id=1, source_target_pairs={{8,16},{24,32},{40,48},{56,64},{72,80},{88,96},{104,112},{16,8},{3... | collective-permute-start | bytes 860168 | tf_op jit(solution)/shard_map/ppermute | solution.py:33
  54.9 17.8 %collective-permute-start.9 = (f32[3,4,32,128]{3,2,1,0:T(8,128)S(1)}, f32[3,4,32,128]{3,2,1,0:T(8,128)S(1)}, u32[]{:S(2)}, u32[]{:S(2)}) collective-permute-start(f32[3,4,32,128]{3,2,1,0:T(8,128)S(1)} %get-tuple-element.44.refs_0_), channel_id=1, source_target_pairs={{0,7},{1,6},{2,1},{3,0},{4,3},{5,2},{6,5},{7,4},{8,15},{9,14},{10,... | collective-permute-start | bytes 589832 | tf_op jit(solution)/shard_map/ppermute | solution.py:941
  59.0 13.6 %collective-permute-start.8 = (f32[3,4,32,128]{3,2,1,0:T(8,128)S(1)}, f32[3,4,32,128]{3,2,1,0:T(8,128)S(1)}, u32[]{:S(2)}, u32[]{:S(2)}) collective-permute-start(f32[3,4,32,128]{3,2,1,0:T(8,128)S(1)} %get-tuple-element.44.refs_0_), channel_id=1, source_target_pairs={{0,2},{1,3},{2,4},{3,5},{4,6},{5,7},{6,0},{7,1},{8,10},{9,11},{10,... | collective-permute-start | bytes 589832 | tf_op jit(solution)/shard_map/ppermute | solution.py:935
  61.8 6.3 %collective-permute-start.10 = (f32[3,40,128]{2,1,0:T(8,128)S(1)}, f32[3,40,128]{2,1,0:T(8,128)S(1)}, u32[]{:S(2)}, u32[]{:S(2)}) collective-permute-start(f32[3,40,128]{2,1,0:T(8,128)S(1)} %get-tuple-element.45), channel_id=1, source_target_pairs={{0,8},{8,0},{16,24},{24,16},{32,40},{40,32},{48,56},{56,48},{64,72... | collective-permute-start | bytes 184328 | tf_op jit(solution)/shard_map/ppermute | solution.py:27
  61.8 9.1 %collective-permute-start.11 = (f32[3,40,128]{2,1,0:T(8,128)S(1)}, f32[3,40,128]{2,1,0:T(8,128)S(1)}, u32[]{:S(2)}, u32[]{:S(2)}) collective-permute-start(f32[3,40,128]{2,1,0:T(8,128)S(1)} %get-tuple-element.46), channel_id=1, source_target_pairs={{8,16},{24,32},{40,48},{56,64},{72,80},{88,96},{104,112},{16,8},{3... | collective-permute-start | bytes 184328 | tf_op jit(solution)/shard_map/ppermute | solution.py:33
  64.9 14.4 %collective-permute-start.14 = (f32[3,4,32,128]{3,2,1,0:T(8,128)S(1)}, f32[3,4,32,128]{3,2,1,0:T(8,128)S(1)}, u32[]{:S(2)}, u32[]{:S(2)}) collective-permute-start(f32[3,4,32,128]{3,2,1,0:T(8,128)S(1)} %get-tuple-element.44.refs_0_), channel_id=1, source_target_pairs={{0,3},{1,2},{2,5},{3,4},{4,7},{5,6},{6,1},{7,0},{8,11},{9,10},{10,... | collective-permute-start | bytes 589832 | tf_op jit(solution)/shard_map/ppermute | solution.py:941
  68.2 11.2 %collective-permute-start.13 = (f32[3,4,32,128]{3,2,1,0:T(8,128)S(1)}, f32[3,4,32,128]{3,2,1,0:T(8,128)S(1)}, u32[]{:S(2)}, u32[]{:S(2)}) collective-permute-start(f32[3,4,32,128]{3,2,1,0:T(8,128)S(1)} %get-tuple-element.44.refs_0_), channel_id=1, source_target_pairs={{0,6},{1,7},{2,0},{3,1},{4,2},{5,3},{6,4},{7,5},{8,14},{9,15},{10,... | collective-permute-start | bytes 589832 | tf_op jit(solution)/shard_map/ppermute | solution.py:935
  71.0 8.4 %collective-permute-start.12 = (f32[3,4,32,128]{3,2,1,0:T(8,128)S(1)}, f32[3,4,32,128]{3,2,1,0:T(8,128)S(1)}, u32[]{:S(2)}, u32[]{:S(2)}) collective-permute-start(f32[3,4,32,128]{3,2,1,0:T(8,128)S(1)} %get-tuple-element.44.refs_0_), channel_id=1, source_target_pairs={{0,1},{1,0},{2,3},{3,2},{4,5},{5,4},{6,7},{7,6},{8,9},{9,8},{10,11... | collective-permute-start | bytes 589832 | tf_op jit(solution)/shard_map/ppermute | solution.py:27
  72.7 6.9 %collective-permute-start.15 = (f32[3,4,32,128]{3,2,1,0:T(8,128)S(1)}, f32[3,4,32,128]{3,2,1,0:T(8,128)S(1)}, u32[]{:S(2)}, u32[]{:S(2)}) collective-permute-start(f32[3,4,32,128]{3,2,1,0:T(8,128)S(1)} %collective-permute-done.8.refs_2_), channel_id=1, source_target_pairs={{0,2},{1,3},{2,4},{3,5},{4,6},{5,7},{6,0},{7,1},{8,10},{9,11},{10,... | collective-permute-start | bytes 589832 | tf_op jit(solution)/shard_map/ppermute | solution.py:935
  74.4 5.7 %collective-permute-start.16 = (f32[3,4,32,128]{3,2,1,0:T(8,128)S(1)}, f32[3,4,32,128]{3,2,1,0:T(8,128)S(1)}, u32[]{:S(2)}, u32[]{:S(2)}) collective-permute-start(f32[3,4,32,128]{3,2,1,0:T(8,128)S(1)} %collective-permute-done.9.refs_5_), channel_id=1, source_target_pairs={{0,6},{1,7},{2,0},{3,1},{4,2},{5,3},{6,4},{7,5},{8,14},{9,15},{10,... | collective-permute-start | bytes 589832 | tf_op jit(solution)/shard_map/ppermute | solution.py:935
  (2 other events, 7.0 us)

commit v3 on v2

--- a/solution.py
+++ b/solution.py
@@ -187,7 +187,7 @@
     )(u, u, b, b, s, s)
 
 
-def residual_kernel(u, b, s, r0, near, far, ue):
+def residual_kernel(u, b, s, r0, s_out, near, far, ue):
     _, width, height, _ = u.shape
     for h in range(2):
         lanes = slice(h * LANES, (h + 1) * LANES)
@@ -211,6 +211,7 @@
     def step(t, carry):
         start = PAD + t * SUB
         rows = pl.ds(pl.multiple_of(t * SUB, SUB), SUB)
+        to = pl.ds(RIM + t * SUB, SUB)
 
         def plane(x):
             return Plane(lambda c, dy: [ue[c, x, h, pl.ds(start + dy, SUB), :] for h in range(2)])
@@ -221,16 +222,19 @@
             au = applied(before, here, after, [6.0 + s[x, rows, h * LANES : (h + 1) * LANES] for h in range(2)], edges)
             for c in range(3):
                 for h in range(2):
-                    r0[c, x, h, rows, :] = b[c, x, rows, h * LANES : (h + 1) * LANES] - au[c][h]
+                    r0[c, x, h, to, :] = b[c, x, rows, h * LANES : (h + 1) * LANES] - au[c][h]
+            for h in range(2):
+                s_out[x, h, to, :] = s[x, rows, h * LANES : (h + 1) * LANES]
             before, here = here, after
         return carry
 
     lax.fori_loop(0, height // SUB, step, 0, unroll=2)
+    own = slice(RIM, RIM + height)
 
     def pack(out, edge, second):
         for c in range(3):
-            out[c] = r0[c, edge]
-            out[3 + c] = r0[c, second]
+            out[c] = r0[c, edge, :, own, :]
+            out[3 + c] = r0[c, second, :, own, :]
             out[6 + c] = ue[c, edge, :, PAD : PAD + height, :]
         for h in range(2):
             out[9, h] = s[edge, :, h * LANES : (h + 1) * LANES]
@@ -253,7 +257,12 @@
     side = jax.ShapeDtypeStruct((10, 2, height, LANES), F32)
     return pl.pallas_call(
         residual_kernel,
-        out_shape=[pltpu.HBM((3, width, 2, height, LANES), F32), side, side],
+        out_shape=[
+            pltpu.HBM((3, width, 2, height + 2 * RIM, LANES), F32),
+            pltpu.HBM((width, 2, height + 2 * RIM, LANES), F32),
+            side,
+            side,
+        ],
         scratch_shapes=[pltpu.VMEM((3, width, 2, height + 2 * PAD, LANES), F32)],
         compiler_params=params(),
         cost_estimate=cost(3),
@@ -411,16 +420,106 @@
     return jnp.broadcast_to(rest_y[pl.ds(start, rows), a : a + 1], (rows, LANES))
 
 
+def field_shape(height, *lead):
+    return (*lead, 2, height + 2 * (RIM + PAD), LANES)
+
+
+def start_copies(moves, sems):
+    copies = [pltpu.make_async_copy(source, to, sems.at[k]) for k, (source, to) in enumerate(moves)]
+    for copy in copies:
+        copy.start()
+    return copies
+
+
+def inner_kernel(bounds, r0p, s_win, r_end, s_end, r0, s_ext, d1, r1, r2, sems):
+    _, width, _, rows, _ = r0p.shape
+    height = rows - 2 * RIM
+    middle, to_middle = pl.ds(SUB, height - SUB), pl.ds(PAD + SUB, height - SUB)
+    to_tile = [pl.ds(PAD, SUB), pl.ds(PAD + height, SUB)]
+    moves = [
+        (r0p.at[:, :, :, middle, :], r0.at[:, :, :, to_middle, :]),
+        (s_win.at[:, :, middle, :], s_ext.at[:, :, to_middle, :]),
+    ]
+    for e in range(2):
+        moves.append((r_end.at[e], r0.at[:, :, :, to_tile[e], :]))
+        moves.append((s_end.at[e], s_ext.at[:, :, to_tile[e], :]))
+    for copy in start_copies(moves, sems):
+        copy.wait()
+    edges = edge_masks()
+    inverse, factors = chebyshev_numbers(bounds, 2)
+    factor_d = factors[0][0] * inverse
+    factor_r = factors[0][1]
+
+    def first_step(t, carry):
+        start = PAD + t * SUB
+        rows = pl.ds(start, SUB)
+        inside = inside_rows(t * SUB, height, "narrow")
+
+        def plane(x):
+            return Plane(lambda c, dy: [r0[c, x, h, pl.ds(start + dy, SUB), :] for h in range(2)])
+
+        before, here = plane(1), plane(2)
+        for x in range(2, width - 2):
+            after = plane(x + 1)
+            diagonal = [6.0 + s_ext[x, h, rows, :] for h in range(2)]
+            ar = applied(before, here, after, diagonal, edges)
+            for c in range(3):
+                for h in range(2):
+                    old = here.v[c][h]
+                    new = old - inverse * ar[c][h]
+                    d1[c, x - 2, h, rows, :] = jnp.where(inside, factor_d * old + factor_r * new, 0.0)
+                    r1[c, x - 2, h, rows, :] = new
+            before, here = here, after
+        return carry
+
+    lax.fori_loop(0, (height + 2 * RIM) // SUB, first_step, 0, unroll=3)
+
+    def second_step(t, carry):
+        start = PAD + RIM + t * SUB
+        rows = pl.ds(start, SUB)
+        to = pl.ds(pl.multiple_of(t * SUB, SUB), SUB)
+
+        def plane(x):
+            return Plane(lambda c, dy: [d1[c, x - 2, h, pl.ds(start + dy, SUB), :] for h in range(2)])
+
+        before, here = plane(2), plane(3)
+        for x in range(3, width - 3):
+            after = plane(x + 1)
+            ad = applied(before, here, after, [6.0 + s_ext[x, h, rows, :] for h in range(2)], edges)
+            for c in range(3):
+                for h in range(2):
+                    r2[c, x - 3, h, to, :] = r1[c, x - 2, h, rows, :] - ad[c][h]
+            before, here = here, after
+        return carry
+
+    lax.fori_loop(0, height // SUB, second_step, 0, unroll=2)
+
+
+def inner(bounds, r0p, s_win, r_end, s_end):
+    _, width, _, rows, _ = r0p.shape
+    height = rows - 2 * RIM
+    shapes = [field_shape(height, *lead) for lead in ((3, width), (width,), (3, width - 4), (3, width - 4))]
+    shapes.append((3, width - 6, 2, height, LANES))
+    return pl.pallas_call(
+        inner_kernel,
+        in_specs=[SMEM] + [ANY] * 4,
+        out_shape=[jax.ShapeDtypeStruct(shape, F32) for shape in shapes],
+        scratch_shapes=[pltpu.SemaphoreType.DMA((6,))],
+        compiler_params=params(),
+        cost_estimate=cost(5),
+        name="inner",
+    )(bounds, r0p, s_win, r_end, s_end)
+
+
 def smooth_kernel(
-    bounds, rest_x, r0p, r_end, s_end, got_near, got_far, sent_near, sent_far, u, s, rest_y, rest_zt,
-    smooth, partial, near, far, left, right, u_left, u_right, s_ext, r0, d1, r1, r2, t_pad, zr,
+    bounds, rest_x, guess, r0_own, s_ext, d1_own, r1_own, r2_own, got_near, got_far, sent_near, sent_far, rest_y, rest_zt,
+    smooth, partial, near, far, left, right, u_left, u_right, r0_rim, d1_rim, r1_rim, r2_rim, t_pad, zr, u, sems,
 ):
     _, width, height, _ = u.shape
     tiles = (height + 2 * RIM) // SUB
     window = slice(PAD, PAD + height + 2 * RIM)
-    middle = slice(PAD + SUB, PAD + height)
-    tile_rows = [slice(PAD, PAD + SUB), slice(PAD + height, PAD + height + SUB)]
     even_x = is_even("wide")
+    (guess_copy,) = start_copies([(guess, u)], sems)
     zr[0], zr[1] = split(z_matrix(rest_zt))
 
     def place(from_left, from_right, mine_left, mine_right):
@@ -439,15 +538,18 @@
     def _():
         place(got_near, got_far, sent_near, sent_far)
 
-    for x in range(width):
-        for h in range(2):
-            s_ext[x, h, middle, :] = s[x, RIM : height - RIM, h * LANES : (h + 1) * LANES]
-        for e in range(2):
-            s_ext[x, :, tile_rows[e], :] = s_end[e, x]
-            for c in range(3):
-                r0[c, x + 2, :, tile_rows[e], :] = r_end[e, c, x]
-        for c in range(3):
-            r0[c, x + 2, :, middle, :] = r0p[c, x, :, RIM : height - RIM, :]
+    def rim(own_ref, first, last, rim_ref, low):
+        def pick(c, x):
+            if first <= x < last:
+                return own_ref.at[c, x - first]
+            return rim_ref.at[c, x - low if x < first else x - low - (last - first)]
+
+        return pick
+
+    r0 = rim(r0_own.at[:, 1 : width - 1], 1, width - 1, r0_rim, -2)
+    d1 = rim(d1_own, 2, width - 2, d1_rim, -1)
+    r1 = rim(r1_own, 2, width - 2, r1_rim, 0)
+    r2 = rim(r2_own, 3, width - 3, r2_rim, 0)
 
     edges = edge_masks()
     place_x = lax.axis_index("wide")
@@ -473,20 +575,20 @@
         inside_right = inside & has_right
         for c in range(3):
             for h in range(2):
-                r0[c, 0, h, rows, :] = left[3 + c, h, rows, :]
-                r0[c, 1, h, rows, :] = jnp.where(
+                r0(c, -2)[h, rows, :] = left[3 + c, h, rows, :]
+                r0(c, -1)[h, rows, :] = jnp.where(
                     inside_left, left[c, h, rows, :] + in_left[c][h], 0.0
                 )
-                r0[c, 2, h, rows, :] = jnp.where(
-                    inside, r0[c, 2, h, rows, :] + out_left[c][h], 0.0
+                r0(c, 0)[h, rows, :] = jnp.where(
+                    inside, r0_own[c, 0, h, rows, :] + out_left[c][h], 0.0
                 )
-                r0[c, width + 1, h, rows, :] = jnp.where(
-                    inside, r0[c, width + 1, h, rows, :] + out_right[c][h], 0.0
+                r0(c, width - 1)[h, rows, :] = jnp.where(
+                    inside, r0_own[c, width - 1, h, rows, :] + out_right[c][h], 0.0
                 )
-                r0[c, width + 2, h, rows, :] = jnp.where(
+                r0(c, width)[h, rows, :] = jnp.where(
                     inside_right, right[c, h, rows, :] + in_right[c][h], 0.0
                 )
-                r0[c, width + 3, h, rows, :] = right[3 + c, h, rows, :]
+                r0(c, width + 1)[h, rows, :] = right[3 + c, h, rows, :]
         return carry
 
     lax.fori_loop(0, tiles, fix, 0, unroll=3)
@@ -497,23 +599,24 @@
         inside = inside_rows(t * SUB, height, "narrow")
 
         def plane(x):
-            return Plane(lambda c, dy: [r0[c, x + 2, h, pl.ds(start + dy, SUB), :] for h in range(2)])
-
-        before, here = plane(-2), plane(-1)
-        for x in range(-1, width + 1):
-            after = plane(x + 1)
-            keep = inside & has_left if x < 0 else inside & has_right if x == width else inside
-            source = left.at[9] if x < 0 else right.at[9] if x == width else s_ext.at[x]
-            diagonal = [6.0 + source[h, rows, :] for h in range(2)]
-            ar = applied(before, here, after, diagonal, edges)
-            for c in range(3):
-                for h in range(2):
-                    old = here.v[c][h]
-                    new = old - inverse * ar[c][h]
-                    d1[c, x + 1, h, rows, :] = jnp.where(keep, factor_d * old + factor_r * new, 0.0)
-                    if 0 <= x < width:
-                        r1[c, x, h, rows, :] = new
-            before, here = here, after
+            return Plane(lambda c, dy: [r0(c, x)[h, pl.ds(start + dy, SUB), :] for h in range(2)])
+
+        for first in (-1, width - 2):
+            before, here = plane(first - 1), plane(first)
+            for x in range(first, first + 3):
+                after = plane(x + 1)
+                keep = inside & has_left if x < 0 else inside & has_right if x == width else inside
+                source = left.at[9] if x < 0 else right.at[9] if x == width else s_ext.at[x]
+                diagonal = [6.0 + source[h, rows, :] for h in range(2)]
+                ar = applied(before, here, after, diagonal, edges)
+                for c in range(3):
+                    for h in range(2):
+                        old = here.v[c][h]
+                        new = old - inverse * ar[c][h]
+                        d1(c, x)[h, rows, :] = jnp.where(keep, factor_d * old + factor_r * new, 0.0)
+                        if 0 <= x < width:
+                            r1(c, x)[h, rows, :] = new
+                before, here = here, after
         return carry
 
     lax.fori_loop(0, tiles, first_step, 0, unroll=3)
@@ -524,22 +627,27 @@
         to = pl.ds(pl.multiple_of(t * SUB, SUB), SUB)
 
         def plane(x):
-            return Plane(lambda c, dy: [d1[c, x + 1, h, pl.ds(start + dy, SUB), :] for h in range(2)])
-
-        before, here = plane(-1), plane(0)
+            return Plane(lambda c, dy: [d1(c, x)[h, pl.ds(start + dy, SUB), :] for h in range(2)])
+
+        for first in (0, width - 3):
+            before, here = plane(first - 1), plane(first)
+            for x in range(first, first + 3):
+                after = plane(x + 1)
+                diagonal = [6.0 + s_ext[x, h, rows, :] for h in range(2)]
+                ad = applied(before, here, after, diagonal, edges)
+                for c in range(3):
+                    for h in range(2):
+                        r2(c, x)[h, to, :] = r1(c, x)[h, rows, :] - ad[c][h]
+                before, here = here, after
         for x in range(width):
-            after = plane(x + 1)
-            diagonal = [6.0 + s_ext[x, h, rows, :] for h in range(2)]
-            ad = applied(before, here, after, diagonal, edges)
             for c in range(3):
                 for h in range(2):
                     lanes = slice(h * LANES, (h + 1) * LANES)
-                    r2[c, x, h, to, :] = r1[c, x, h, rows, :] - ad[c][h]
-                    step = inverse * r0[c, x + 2, h, rows, :] + here.v[c][h]
+                    step = inverse * r0(c, x)[h, rows, :] + d1(c, x)[h, rows, :]
                     smooth[c, x, to, lanes] = u[c, x, to, lanes] + step
-            before, here = here, after
         return carry
 
+    guess_copy.wait()
     lax.fori_loop(0, height // SUB, second_step, 0, unroll=2)
 
     coarse_width = width // 2
@@ -556,7 +664,7 @@
             for h in range(2):
                 total = None
                 for a, x in terms:
-                    piece = rest_x[first_weight + i + 1, a] * r2[c, x, h]
+                    piece = rest_x[first_weight + i + 1, a] * r2(c, x)[h]
                     total = piece if total is None else total + piece
                 halves.append(total)
             joined = jnp.concatenate(halves, axis=1)
@@ -577,17 +685,18 @@
     def send(out, first):
         for c in range(3):
             for i in range(coarse_width + 2):
-                out[c * (coarse_width + 2) + i] = partial[c, i, first : first + SUB, :]
+                k = 5 * (c * (coarse_width + 2) + i)
+                out[k : k + 5, :] = partial[c, i, first : first + 5, :]
 
     @pl.when(even_y)
     def _():
-        send(near, coarse_rows - SUB)
-        send(far, 0)
+        send(near, coarse_rows - 8)
+        send(far, 3)
 
     @pl.when(jnp.logical_not(even_y))
     def _():
-        send(near, 0)
-        send(far, coarse_rows - SUB)
+        send(near, 3)
+        send(far, coarse_rows - 8)
 
 
 def split(x):
@@ -607,21 +716,21 @@
 
 SMEM = pl.BlockSpec(memory_space=pltpu.SMEM)
 VMEM = pl.BlockSpec(memory_space=pltpu.VMEM)
-
-
-def smoothing(bounds, rest_x, r0p, r_end, s_end, got, sent, u, s, rest_y, rest_zt):
+ANY = pl.BlockSpec(memory_space=pl.ANY)
+
+
+def smoothing(bounds, rest_x, u, own, got, sent, rest_y, rest_zt):
     _, width, height, depth = u.shape
-    padded = height + 2 * (RIM + PAD)
     planes = 3 * (width // 2 + 2)
     coarse_rows = height // 2 + 2 * RIM
-    tile = jax.ShapeDtypeStruct((planes, SUB, LANES), F32)
+    tile = jax.ShapeDtypeStruct((-(-5 * planes // SUB) * SUB, LANES), F32)
 
     def field(*lead):
-        return pltpu.VMEM((*lead, 2, padded, LANES), F32)
+        return pltpu.VMEM(field_shape(height, *lead), F32)
 
     return pl.pallas_call(
         smooth_kernel,
-        in_specs=[SMEM, SMEM] + [VMEM] * 11,
+        in_specs=[SMEM, SMEM, ANY] + [VMEM] * 11,
         out_shape=[
             jax.ShapeDtypeStruct((3, width, height, depth), F32),
             jax.ShapeDtypeStruct((3, width // 2 + 2, coarse_rows, LANES), F32),
@@ -633,18 +742,19 @@
             field(10),
             field(3),
             field(3),
-            field(width),
-            field(3, width + 4),
-            field(3, width + 2),
-            field(3, width),
-            pltpu.VMEM((3, width, 2, height, LANES), F32),
+            field(3, 6),
+            field(3, 6),
+            field(3, 4),
+            pltpu.VMEM((3, 6, 2, height, LANES), F32),
             pltpu.VMEM((planes, 2 * coarse_rows + 2 * SUB, LANES), F32),
             pltpu.VMEM((2, 2 * LANES, LANES), jnp.bfloat16),
+            pltpu.VMEM((3, width, height, depth), F32),
+            pltpu.SemaphoreType.DMA((1,)),
         ],
         compiler_params=params(),
         cost_estimate=cost(10),
         name="smoothing",
-    )(bounds, rest_x, r0p, r_end, s_end, *got, *sent, u, s, rest_y, rest_zt)
+    )(bounds, rest_x, u, *own, *got, *sent, rest_y, rest_zt)
 
 
 def rows_kernel(partial, got_near, got_far, s, q, s_win, near, far):
@@ -653,14 +763,14 @@
     coarse_width = planes - 2
     n = lax.axis_index("narrow")
     even_y = is_even("narrow")
-    q[:, :, SUB : rows - SUB, :] = partial[:, :, SUB : rows - SUB, :]
+    q[...] = partial[...]
 
     def join(low, high):
         for c in range(3):
             for i in range(planes):
-                k = c * planes + i
-                q[c, i, 0:SUB, :] = partial[c, i, 0:SUB, :] + low[k]
-                q[c, i, rows - SUB :, :] = partial[c, i, rows - SUB :, :] + high[k]
+                k = 5 * (c * planes + i)
+                q[c, i, 0:5, :] = partial[c, i, 0:5, :] + low[k : k + 5, :]
+                q[c, i, rows - 5 :, :] = partial[c, i, rows - 5 :, :] + high[k : k + 5, :]
 
     @pl.when(even_y)
     def _():
@@ -863,7 +973,7 @@
     )(bounds, q, s_win, got_near, got_far)
 
 
-def prolong_kernel(rest_x, corr, got_near, got_far, smooth, rest_y, rest_zt, out, left, right, wy, col, grown):
+def prolong_kernel(rest_x, corr, got_far, got_near, smooth, rest_y, rest_zt, out, left, right, wy, col, grown):
     _, width, height, _ = corr.shape
     own = height - 2 * RIM
     fine_width = 2 * width
@@ -941,29 +1051,38 @@
         return lax.ppermute(x, "narrow", [(i, ((i + by) % count) ^ 1) for i in range(count)])
 
     pair_low, pair_high = across(own, 2), across(own, -2)
-    first, second, edges = after((low, pair_high, edges))
+    far_edge, near_edge = edges
+    first, second, near_edge = after((low, pair_high, near_edge))
+    edges = far_edge, near_edge
     far_own, far_pair = ring(first, 2), ring(second, -2)
     result = prolonged(edges)
-    return [own, pair, low, high, pair_low, pair_high, far_own, far_pair], result
+    return [own, pair_low, high, pair, low, pair_high, far_own, far_pair], result
 
 
 def assemble_kernel(*refs):
-    blocks, out = refs[:-1], refs[-1]
+    *blocks, out, sems = refs
     count = len(blocks)
     n = lax.axis_index("narrow")
     m = n + 1 - 2 * lax.rem(n, 2)
     own = blocks[0].shape[2]
-    sources = [n, m, n - 2, n + 2, m - 2, m + 2, n - 4, m + 4]
-    for block, source in zip(blocks, sources):
+    sources = [n, m - 2, n + 2, m, n - 2, m + 2, n - 4, m + 4]
+    copies = []
+    for k, (block, source) in enumerate(zip(blocks, sources)):
         start = pl.multiple_of(lax.rem(source + count, count) * own, SUB)
-        out[:, :, pl.ds(start, own), :] = block[...]
+        copies.append(pltpu.make_async_copy(block, out.at[:, :, pl.ds(start, own), :], sems.at[k]))
+        copies[-1].start()
+    for copy in copies:
+        copy.wait()
 
 
 def assemble(blocks):
     three, width, own, lanes = blocks[0].shape
     return pl.pallas_call(
         assemble_kernel,
+        in_specs=[ANY] * len(blocks),
+        out_specs=ANY,
         out_shape=jax.ShapeDtypeStruct((three, width, own * len(blocks), lanes), F32),
+        scratch_shapes=[pltpu.SemaphoreType.DMA((len(blocks),))],
         compiler_params=params(),
         cost_estimate=cost(1),
         name="assemble",
@@ -986,18 +1105,17 @@
     z_weights = rest_z.T
     from_hbm = [pltpu.with_memory_space_constraint(x, pltpu.HBM) for x in (start_guess, right_side, reaction)]
     got = swap_both(pack_y(*from_hbm), "narrow")
-    r0p, *main = residual(start_guess, right_side, reaction)
+    r0p, s_win, *main = residual(start_guess, right_side, reaction)
     r_end, s_end, *sent = ends(start_guess, right_side, reaction, got, main)
     got = swap_both(sent, "wide")
-    r0p, r_end, s_end = (pltpu.with_memory_space_constraint(x, pltpu.HBM) for x in (r0p, r_end, s_end))
-    smooth, partial, *sent = smoothing(
-        fine_bounds, x_weights, r0p, r_end, s_end, got, sent, start_guess, reaction, y_padded, z_weights
-    )
+    waiting = [pltpu.with_memory_space_constraint(x, pltpu.HBM) for x in (r0p, s_win, r_end, s_end)]
+    own = inner(fine_bounds, *waiting)
+    smooth, partial, *sent = smoothing(fine_bounds, x_weights, start_guess, own, got, sent, y_padded, z_weights)
     got = swap_both(sent, "narrow")
-    q, s_win, *sent = rows(partial, *got, coarse_reaction)
+    q, coarse_win, *sent = rows(partial, *got, coarse_reaction)
     got = swap_both(sent, "wide")
-    corr, own, *sent = coarse_solve(coarse_bounds, q, s_win, *got)
-    edges = swap_both(sent, "wide")
+    corr, own, *sent = coarse_solve(coarse_bounds, q, coarse_win, *got)
+    edges = swap_both(sent, "wide")[::-1]
     blocks, solution_block = gather(
         own, edges, lambda edges: prolong(x_weights, corr, *edges, smooth, y_padded, z_weights)
     )

time: 81.5 us -> 77.8 us (0.955)
  waiting for transfers between devices: 23.3 us -> 18.8 us
  Pallas kernels: 19.5 us -> 21.7 us
  starting transfers between devices: 37.4 us -> 35.6 us
    ppermute x5, waiting for transfers between devices: 20.2 us -> 16 us  [swap_far(): return lax.ppermute(x, axis, up + [(j, i) for i, j in up])]
    pallas_call x2 -> x3, Pallas kernels: 8.61 us -> 10.7 us  [the longest x1 5.96 us: smoothing(): pl.pallas_call(smooth_kernel, in_specs=[SMEM, SMEM, ANY] + [VMEM] * 11, o...]
    ppermute x6, starting transfers between devices: 8.92 us -> 7.61 us  [swap_near(): return lax.ppermute(x, axis, [(i, i ^ 1) for i in range(count)])]
  transfers between devices with their start and end apart: 17 -> 17, of which waited for: 7 -> 6; matrix products, arithmetic and copies ran while one was open for 0% -> 0% of each run, Pallas kernels for 8% -> 13%
where the time goes in v3:
time: 77.8 us; the launch traced here: 77.2 us
  starting transfers between devices  35.6 us (46%)
  Pallas kernels  21.7 us (28%)
  waiting for transfers between devices  18.8 us (24%)
  between operations  0.85 us (1%)
    ppermute x5, waiting for transfers between devices, swap_far(): return lax.ppermute(x, axis, up + [(j, i) for i, j in up])  16 us
    ppermute x5, starting transfers between devices, swap_far(): return lax.ppermute(x, axis, up + [(j, i) for i, j in up])  12.9 us
    ppermute x4, starting transfers between devices, ring(): lax.ppermute(x, 'narrow', [(i, (i + by) % count) for i in range(count)])  7.92 us
    ppermute x6, starting transfers between devices, swap_near(): return lax.ppermute(x, axis, [(i, i ^ 1) for i in range(count)])  7.61 us
    ppermute x2, starting transfers between devices, across(): lax.ppermute(x, 'narrow', [(i, (i + by) % count ^ 1) for i in range(count)])  7.14 us
    pallas_call x1, Pallas kernels, smoothing(): pl.pallas_call(smooth_kernel, in_specs=[SMEM, SMEM, ANY] + [VMEM] * 11, o...  5.96 us
    pallas_call x1, Pallas kernels, inner(): pl.pallas_call(inner_kernel, in_specs=[SMEM] + [ANY] * 4, out_shape=[jax....  3.57 us
    pallas_call x1, Pallas kernels, prolong(): pl.pallas_call(prolong_kernel, in_specs=[SMEM] + [VMEM] * 6, out_shape=ja...  3.36 us
  transfers between devices with their start and end apart: 17, of which 6 were waited for; matrix products, arithmetic and copies ran while one was open for 0% of the time, Pallas kernels for 13%

profile of v3, /device:TPU:16, one launch (start us, length us, event | category | flops | bytes accessed | tf_op | source)
XLA Modules:
  0.0 77.2 jit_solution(3035026733079741376)
XLA Ops:
  0.7 1.5 %pack_y.1 = (f32[2,136,128]{2,1,0:T(8,128)S(1)}, f32[2,136,128]{2,1,0:T(8,128)S(1)}) custom-call(f32[3,8,64,256]{3,2,1,0:T(8,128)} %guess.1, f32[3,8,64,256]{3,2,1,0:T(8,128)} %guess.1, f32[3,8,64,256]{3,2,1,0:T(8,128)} %refs_3_.1, f32[3,8,64,256]{3,2,1,0:T(8,128)} %refs_3_.1, f32[8,64,256]{2,1,0:T(8,128)} %refs_5_.1, f32[8,64,256]{2,1,0:T(8,128)} %refs_5_.1), custom_call_target="tpu_custom_call" | custom-call | bytes 3690000 | tf_op jit(solution)/shard_map/pack_y/pallas_call | solution.py:178
  2.1 1.4 %collective-permute-start = (f32[2,136,128]{2,1,0:T(8,128)S(1)}, f32[2,136,128]{2,1,0:T(8,128)S(1)}, u32[]{:S(2)}, u32[]{:S(2)}) collective-permute-start(f32[2,136,128]{2,1,0:T(8,128)S(1)} %get-tuple-element.34), channel_id=1, source_target_pairs={{0,1},{1,0},{2,3},{3,2},{4,5},{5,4},{6,7},{7,6},{8,9},{9,8},{10,11... | collective-permute-start | bytes 417800 | tf_op jit(solution)/shard_map/ppermute | solution.py:27
  3.5 0.7 collective-permute-start.1
  4.2 3.1 %residual.1 = (f32[3,8,2,72,128]{4,3,2,1,0:T(8,128)}, f32[8,2,72,128]{3,2,1,0:T(8,128)}, f32[10,2,64,128]{3,2,1,0:T(8,128)S(1)}, f32[10,2,64,128]{3,2,1,0:T(8,128)S(1)}) custom-call(f32[3,8,64,256]{3,2,1,0:T(8,128)S(1)} %copy-done, f32[3,8,64,256]{3,2,1,0:T(8,128)S(1)} %copy-done.1, f32[8,64,256]{2,1,0:T(8,128)S(1)} %copy-done.2), custom_call_target="tpu_custom_call" | custom-call | bytes 11070000 | tf_op jit(solution)/shard_map/residual/pallas_call | solution.py:258
  7.6 1.3 %ends.1 = (f32[2,3,8,2,8,128]{5,4,3,2,1,0:T(8,128)}, f32[2,8,2,8,128]{4,3,2,1,0:T(8,128)}, f32[10,2,72,128]{3,2,1,0:T(8,128)S(1)}, f32[10,2,72,128]{3,2,1,0:T(8,128)S(1)}) custom-call(f32[3,8,64,256]{3,2,1,0:T(8,128)S(1)} %copy-done, f32[3,8,64,256]{3,2,1,0:T(8,128)S(1)} %copy-done, f32[3,8,64,256]{3,2,1,0:T(8,128)S(1)} %copy-done.1, ...), custom_call_target="tpu_custom_call" | custom-call | bytes 147600000 | tf_op jit(solution)/shard_map/ends/pallas_call | solution.py:377
  9.0 4.5 %collective-permute-start.3 = (f32[10,2,72,128]{3,2,1,0:T(8,128)S(1)}, f32[10,2,72,128]{3,2,1,0:T(8,128)}, u32[]{:S(2)}, u32[]{:S(2)}) collective-permute-start(f32[10,2,72,128]{3,2,1,0:T(8,128)S(1)} %get-tuple-element.46.sent_far), channel_id=1, source_target_pairs={{8,16},{24,32},{40,48},{56,64},{72,80},{88,96},{104,112},{16,8},{3... | collective-permute-start | bytes 2211848 | tf_op jit(solution)/shard_map/ppermute | solution.py:33
  13.8 3.6 %inner.1 = (f32[3,8,2,88,128]{4,3,2,1,0:T(8,128)S(1)}, f32[8,2,88,128]{3,2,1,0:T(8,128)S(1)}, f32[3,4,2,88,128]{4,3,2,1,0:T(8,128)S(1)}, f32[3,4,2,88,128]{4,3,2,1,0:T(8,128)S(1)}, f32[3,2,2,64,128]{4,3,2,1,0:T(8,128)S(1)}) custom-call(f32[2]{0:T(128)S(1)} %copy-done.5, f32[3,8,2,72,128]{4,3,2,1,0:T(8,128)} %get-tuple-element.32.r0p, ...), custom_call_target="tpu_custom_call" | custom-call | bytes 18450000 | tf_op jit(solution)/shard_map/inner/pallas_call | solution.py:503
  17.4 8.0 %collective-permute-done.3.got_far = f32[10,2,72,128]{3,2,1,0:T(8,128)} collective-permute-done((f32[10,2,72,128]{3,2,1,0:T(8,128)S(1)}, f32[10,2,72,128]{3,2,1,0:T(8,128)}, u32[]{:S(2)}, u32[]{:S(2)}) %collective-permute-start.3) | collective-permute-done | bytes 737312 | tf_op jit(solution)/shard_map/ppermute | solution.py:33
  25.5 6.0 %smoothing.1 = (f32[3,8,64,256]{3,2,1,0:T(8,128)S(1)}, f32[3,6,40,128]{3,2,1,0:T(8,128)S(1)}, f32[96,128]{1,0:T(8,128)S(1)}, f32[96,128]{1,0:T(8,128)S(1)}) custom-call(f32[2]{0:T(128)S(1)} %copy-done.5, f32[66,5]{1,0:T(8,128)S(1)} %pad.8.rest_x, f32[3,8,64,256]{3,2,1,0:T(8,128)S(1)} %copy-done, f32[3,8,2,88,128]{4,3,2,1,0:T(8,128)S(1)} %get-tuple-element.40.r0_own, ...), custom_call_target="tpu_custom_call" | custom-call | bytes 36900000 | tf_op jit(solution)/shard_map/smoothing/pallas_call | solution.py:731
  31.4 5.8 %collective-permute-start.4 = (f32[96,128]{1,0:T(8,128)S(1)}, f32[96,128]{1,0:T(8,128)S(1)}, u32[]{:S(2)}, u32[]{:S(2)}) collective-permute-start(f32[96,128]{1,0:T(8,128)S(1)} %get-tuple-element.48), channel_id=1, source_target_pairs={{0,1},{1,0},{2,3},{3,2},{4,5},{5,4},{6,7},{7,6},{8,9},{9,8},{10,11... | collective-permute-start | bytes 147464 | tf_op jit(solution)/shard_map/ppermute | solution.py:27
  37.2 0.7 collective-permute-start.5
  37.9 1.4 %collective-permute-done.4.got_near = f32[96,128]{1,0:T(8,128)S(1)} collective-permute-done((f32[96,128]{1,0:T(8,128)S(1)}, f32[96,128]{1,0:T(8,128)S(1)}, u32[]{:S(2)}, u32[]{:S(2)}) %collective-permute-start.4) | collective-permute-done | bytes 49184 | tf_op jit(solution)/shard_map/ppermute | solution.py:27
  39.5 4.0 %collective-permute-start.7 = (f32[14,40,128]{2,1,0:T(8,128)S(1)}, f32[14,40,128]{2,1,0:T(8,128)S(1)}, u32[]{:S(2)}, u32[]{:S(2)}) collective-permute-start(f32[14,40,128]{2,1,0:T(8,128)S(1)} %get-tuple-element.53), channel_id=1, source_target_pairs={{8,16},{24,32},{40,48},{56,64},{72,80},{88,96},{104,112},{16,8},{3... | collective-permute-start | bytes 860168 | tf_op jit(solution)/shard_map/ppermute | solution.py:33
  43.5 7.6 %collective-permute-done.7.got_far = f32[14,40,128]{2,1,0:T(8,128)S(1)} collective-permute-done((f32[14,40,128]{2,1,0:T(8,128)S(1)}, f32[14,40,128]{2,1,0:T(8,128)S(1)}, u32[]{:S(2)}, u32[]{:S(2)}) %collective-permute-start.7) | collective-permute-done | bytes 286752 | tf_op jit(solution)/shard_map/ppermute | solution.py:33
  51.1 1.6 %coarse_solve.1 = (f32[3,4,40,128]{3,2,1,0:T(8,128)S(1)}, f32[3,4,32,128]{3,2,1,0:T(8,128)S(1)}, f32[3,40,128]{2,1,0:T(8,128)S(1)}, f32[3,40,128]{2,1,0:T(8,128)S(1)}) custom-call(f32[2]{0:T(128)S(1)} %copy-done.6, f32[3,6,40,128]{3,2,1,0:T(8,128)S(1)} %get-tuple-element.50.q, f32[4,40,128]{2,1,0:T(8,128)S(1)} %get-tuple-element.51.s_win, ...), custom_call_target="tpu_custom_call" | custom-call | bytes 11070000 | tf_op jit(solution)/shard_map/coarse_solve/pallas_call | solution.py:953
  52.7 3.9 %collective-permute-start.10 = (f32[3,4,32,128]{3,2,1,0:T(8,128)S(1)}, f32[3,4,32,128]{3,2,1,0:T(8,128)S(1)}, u32[]{:S(2)}, u32[]{:S(2)}) collective-permute-start(f32[3,4,32,128]{3,2,1,0:T(8,128)S(1)} %get-tuple-element.56.refs_0_), channel_id=1, source_target_pairs={{0,7},{1,6},{2,1},{3,0},{4,3},{5,2},{6,5},{7,4},{8,15},{9,14},{10,... | collective-permute-start | bytes 589832 | tf_op jit(solution)/shard_map/ppermute | solution.py:1051
  56.6 3.0 %collective-permute-start.9 = (f32[3,4,32,128]{3,2,1,0:T(8,128)S(1)}, f32[3,4,32,128]{3,2,1,0:T(8,128)S(1)}, u32[]{:S(2)}, u32[]{:S(2)}) collective-permute-start(f32[3,4,32,128]{3,2,1,0:T(8,128)S(1)} %get-tuple-element.56.refs_0_), channel_id=1, source_target_pairs={{0,2},{1,3},{2,4},{3,5},{4,6},{5,7},{6,0},{7,1},{8,10},{9,11},{10,... | collective-permute-start | bytes 589832 | tf_op jit(solution)/shard_map/ppermute | solution.py:1045
  59.7 3.1 %collective-permute-start.8 = (f32[3,40,128]{2,1,0:T(8,128)S(1)}, f32[3,40,128]{2,1,0:T(8,128)S(1)}, u32[]{:S(2)}, u32[]{:S(2)}) collective-permute-start(f32[3,40,128]{2,1,0:T(8,128)S(1)} %get-tuple-element.55), channel_id=1, source_target_pairs={{8,16},{24,32},{40,48},{56,64},{72,80},{88,96},{104,112},{16,8},{3... | collective-permute-start | bytes 184328 | tf_op jit(solution)/shard_map/ppermute | solution.py:33
  62.8 3.2 %collective-permute-start.12 = (f32[3,4,32,128]{3,2,1,0:T(8,128)S(1)}, f32[3,4,32,128]{3,2,1,0:T(8,128)S(1)}, u32[]{:S(2)}, u32[]{:S(2)}) collective-permute-start(f32[3,4,32,128]{3,2,1,0:T(8,128)S(1)} %get-tuple-element.56.refs_0_), channel_id=1, source_target_pairs={{0,3},{1,2},{2,5},{3,4},{4,7},{5,6},{6,1},{7,0},{8,11},{9,10},{10,... | collective-permute-start | bytes 589832 | tf_op jit(solution)/shard_map/ppermute | solution.py:1051
  66.0 2.0 %collective-permute-start.13 = (f32[3,4,32,128]{3,2,1,0:T(8,128)S(1)}, f32[3,4,32,128]{3,2,1,0:T(8,128)S(1)}, u32[]{:S(2)}, u32[]{:S(2)}) collective-permute-start(f32[3,4,32,128]{3,2,1,0:T(8,128)S(1)} %get-tuple-element.56.refs_0_), channel_id=1, source_target_pairs={{0,6},{1,7},{2,0},{3,1},{4,2},{5,3},{6,4},{7,5},{8,14},{9,15},{10,... | collective-permute-start | bytes 589832 | tf_op jit(solution)/shard_map/ppermute | solution.py:1045
  68.8 2.8 %collective-permute-start.16 = (f32[3,4,32,128]{3,2,1,0:T(8,128)S(1)}, f32[3,4,32,128]{3,2,1,0:T(8,128)S(1)}, u32[]{:S(2)}, u32[]{:S(2)}) collective-permute-start(f32[3,4,32,128]{3,2,1,0:T(8,128)S(1)} %collective-permute-done.10.refs_5_), channel_id=1, source_target_pairs={{0,6},{1,7},{2,0},{3,1},{4,2},{5,3},{6,4},{7,5},{8,14},{9,15},{10,... | collective-permute-start | bytes 589832 | tf_op jit(solution)/shard_map/ppermute | solution.py:1045
  71.7 3.4 %prolong.1 = f32[3,8,64,256]{3,2,1,0:T(8,128)} custom-call(f32[66,5]{1,0:T(8,128)S(1)} %pad.8.rest_x, f32[3,4,40,128]{3,2,1,0:T(8,128)S(1)} %get-tuple-element.54.corr, f32[3,40,128]{2,1,0:T(8,128)S(1)} %collective-permute-done.8.got_far, f32[3,40,128]{2,1,0:T(8,128)S(1)} %collective-permute-done.11.got_near, ...), custom_call_target="tpu_custom_call" | custom-call | bytes 44280000 | tf_op jit(solution)/shard_map/prolong/pallas_call | solution.py:1024
  75.0 1.0 %collective-permute-done.15.refs_6_ = f32[3,4,32,128]{3,2,1,0:T(8,128)S(1)} collective-permute-done((f32[3,4,32,128]{3,2,1,0:T(8,128)S(1)}, f32[3,4,32,128]{3,2,1,0:T(8,128)S(1)}, u32[]{:S(2)}, u32[]{:S(2)}) %collective-permute-start.15) | collective-permute-done | bytes 196640 | tf_op jit(solution)/shard_map/ppermute | solution.py:1045
  76.0 1.2 %assemble.1 = f32[3,4,256,128]{3,2,1,0:T(8,128)} custom-call(f32[3,4,32,128]{3,2,1,0:T(8,128)S(1)} %get-tuple-element.56.refs_0_, f32[3,4,32,128]{3,2,1,0:T(8,128)S(1)} %collective-permute-done.12.refs_1_, f32[3,4,32,128]{3,2,1,0:T(8,128)S(1)} %collective-permute-done.13.refs_2_, f32[3,4,32,128]{3,2,1,0:T(8,128)S(1)} %collective-permute-done.14.refs_3_, ...), custom_call_target="tpu_custom_call" | custom-call | bytes 3690000 | tf_op jit(solution)/shard_map/assemble/pallas_call | solution.py:1080
  (41 shorter events, 1.7 us)
Async XLA Ops:
  0.6 3.5 %copy-start = (f32[3,8,64,256]{3,2,1,0:T(8,128)S(1)}, f32[3,8,64,256]{3,2,1,0:T(8,128)}, u32[]{:S(2)}) copy-start(f32[3,8,64,256]{3,2,1,0:T(8,128)} %guess.1) | copy-start | bytes 4718596
  2.1 5.5 %collective-permute-start = (f32[2,136,128]{2,1,0:T(8,128)S(1)}, f32[2,136,128]{2,1,0:T(8,128)S(1)}, u32[]{:S(2)}, u32[]{:S(2)}) collective-permute-start(f32[2,136,128]{2,1,0:T(8,128)S(1)} %get-tuple-element.34), channel_id=1, source_target_pairs={{0,1},{1,0},{2,3},{3,2},{4,5},{5,4},{6,7},{7,6},{8,9},{9,8},{10,11... | collective-permute-start | bytes 417800 | tf_op jit(solution)/shard_map/ppermute | solution.py:27
  3.5 4.1 %collective-permute-start.1 = (f32[2,136,128]{2,1,0:T(8,128)S(1)}, f32[2,136,128]{2,1,0:T(8,128)S(1)}, u32[]{:S(2)}, u32[]{:S(2)}) collective-permute-start(f32[2,136,128]{2,1,0:T(8,128)S(1)} %get-tuple-element.35), channel_id=1, source_target_pairs={{1,2},{3,4},{5,6},{2,1},{4,3},{6,5},{9,10},{11,12},{13,14},{10,9},... | collective-permute-start | bytes 417800 | tf_op jit(solution)/shard_map/ppermute | solution.py:33
  7.6 5.9 %copy-start.7 = (f32[256,5]{0,1:T(8,128)S(1)}, f32[256,5]{0,1:T(8,128)}, u32[]{:S(2)}) copy-start(f32[256,5]{0,1:T(8,128)} %param.14) | copy-start | bytes 15364
  7.6 6.1 %copy-start.8 = (f32[64,5]{0,1:T(8,128)S(1)}, f32[64,5]{0,1:T(8,128)}, u32[]{:S(2)}) copy-start(f32[64,5]{0,1:T(8,128)} %param.13) | copy-start | bytes 3844
  7.6 6.2 %copy-start.5 = (f32[2]{0:T(128)S(1)}, f32[2]{0:T(128)}, u32[]{:S(2)}) copy-start(f32[2]{0:T(128)} %bounds.4) | copy-start | bytes 28
  9.0 8.4 %collective-permute-start.2 = (f32[10,2,72,128]{3,2,1,0:T(8,128)S(1)}, f32[10,2,72,128]{3,2,1,0:T(8,128)}, u32[]{:S(2)}, u32[]{:S(2)}) collective-permute-start(f32[10,2,72,128]{3,2,1,0:T(8,128)S(1)} %get-tuple-element.45.sent_near), channel_id=1, source_target_pairs={{0,8},{8,0},{16,24},{24,16},{32,40},{40,32},{48,56},{56,48},{64,72... | collective-permute-start | bytes 2211848 | tf_op jit(solution)/shard_map/ppermute | solution.py:27
  9.0 16.5 %collective-permute-start.3 = (f32[10,2,72,128]{3,2,1,0:T(8,128)S(1)}, f32[10,2,72,128]{3,2,1,0:T(8,128)}, u32[]{:S(2)}, u32[]{:S(2)}) collective-permute-start(f32[10,2,72,128]{3,2,1,0:T(8,128)S(1)} %get-tuple-element.46.sent_far), channel_id=1, source_target_pairs={{8,16},{24,32},{40,48},{56,64},{72,80},{88,96},{104,112},{16,8},{3... | collective-permute-start | bytes 2211848 | tf_op jit(solution)/shard_map/ppermute | solution.py:33
  13.8 11.7 %copy-start.4 = (f32[128,5]{0,1:T(8,128)S(1)}, f32[128,5]{0,1:T(8,128)}, u32[]{:S(2)}) copy-start(f32[128,5]{0,1:T(8,128)} %param.15) | copy-start | bytes 7684
  25.5 13.8 %copy-start.3 = (f32[4,256,128]{2,1,0:T(8,128)S(1)}, f32[4,256,128]{2,1,0:T(8,128)}, u32[]{:S(2)}) copy-start(f32[4,256,128]{2,1,0:T(8,128)} %s.3) | copy-start | bytes 1572868
  25.5 25.6 %copy-start.6 = (f32[2]{0:T(128)S(1)}, f32[2]{0:T(128)}, u32[]{:S(2)}) copy-start(f32[2]{0:T(128)} %bounds.5) | copy-start | bytes 28
  31.4 7.9 %collective-permute-start.4 = (f32[96,128]{1,0:T(8,128)S(1)}, f32[96,128]{1,0:T(8,128)S(1)}, u32[]{:S(2)}, u32[]{:S(2)}) collective-permute-start(f32[96,128]{1,0:T(8,128)S(1)} %get-tuple-element.48), channel_id=1, source_target_pairs={{0,1},{1,0},{2,3},{3,2},{4,5},{5,4},{6,7},{7,6},{8,9},{9,8},{10,11... | collective-permute-start | bytes 147464 | tf_op jit(solution)/shard_map/ppermute | solution.py:27
  37.2 2.1 %collective-permute-start.5 = (f32[96,128]{1,0:T(8,128)S(1)}, f32[96,128]{1,0:T(8,128)S(1)}, u32[]{:S(2)}, u32[]{:S(2)}) collective-permute-start(f32[96,128]{1,0:T(8,128)S(1)} %get-tuple-element.49), channel_id=1, source_target_pairs={{1,2},{3,4},{5,6},{2,1},{4,3},{6,5},{9,10},{11,12},{13,14},{10,9},... | collective-permute-start | bytes 147464 | tf_op jit(solution)/shard_map/ppermute | solution.py:33
  39.4 4.1 %collective-permute-start.6 = (f32[14,40,128]{2,1,0:T(8,128)S(1)}, f32[14,40,128]{2,1,0:T(8,128)S(1)}, u32[]{:S(2)}, u32[]{:S(2)}) collective-permute-start(f32[14,40,128]{2,1,0:T(8,128)S(1)} %get-tuple-element.52), channel_id=1, source_target_pairs={{0,8},{8,0},{16,24},{24,16},{32,40},{40,32},{48,56},{56,48},{64,72... | collective-permute-start | bytes 860168 | tf_op jit(solution)/shard_map/ppermute | solution.py:27
  39.5 11.6 %collective-permute-start.7 = (f32[14,40,128]{2,1,0:T(8,128)S(1)}, f32[14,40,128]{2,1,0:T(8,128)S(1)}, u32[]{:S(2)}, u32[]{:S(2)}) collective-permute-start(f32[14,40,128]{2,1,0:T(8,128)S(1)} %get-tuple-element.53), channel_id=1, source_target_pairs={{8,16},{24,32},{40,48},{56,64},{72,80},{88,96},{104,112},{16,8},{3... | collective-permute-start | bytes 860168 | tf_op jit(solution)/shard_map/ppermute | solution.py:33
  52.7 15.3 %collective-permute-start.10 = (f32[3,4,32,128]{3,2,1,0:T(8,128)S(1)}, f32[3,4,32,128]{3,2,1,0:T(8,128)S(1)}, u32[]{:S(2)}, u32[]{:S(2)}) collective-permute-start(f32[3,4,32,128]{3,2,1,0:T(8,128)S(1)} %get-tuple-element.56.refs_0_), channel_id=1, source_target_pairs={{0,7},{1,6},{2,1},{3,0},{4,3},{5,2},{6,5},{7,4},{8,15},{9,14},{10,... | collective-permute-start | bytes 589832 | tf_op jit(solution)/shard_map/ppermute | solution.py:1051
  56.6 11.8 %collective-permute-start.9 = (f32[3,4,32,128]{3,2,1,0:T(8,128)S(1)}, f32[3,4,32,128]{3,2,1,0:T(8,128)S(1)}, u32[]{:S(2)}, u32[]{:S(2)}) collective-permute-start(f32[3,4,32,128]{3,2,1,0:T(8,128)S(1)} %get-tuple-element.56.refs_0_), channel_id=1, source_target_pairs={{0,2},{1,3},{2,4},{3,5},{4,6},{5,7},{6,0},{7,1},{8,10},{9,11},{10,... | collective-permute-start | bytes 589832 | tf_op jit(solution)/shard_map/ppermute | solution.py:1045
  59.7 6.3 %collective-permute-start.11 = (f32[3,40,128]{2,1,0:T(8,128)S(1)}, f32[3,40,128]{2,1,0:T(8,128)S(1)}, u32[]{:S(2)}, u32[]{:S(2)}) collective-permute-start(f32[3,40,128]{2,1,0:T(8,128)S(1)} %get-tuple-element.57), channel_id=1, source_target_pairs={{0,8},{8,0},{16,24},{24,16},{32,40},{40,32},{48,56},{56,48},{64,72... | collective-permute-start | bytes 184328 | tf_op jit(solution)/shard_map/ppermute | solution.py:27
  59.7 9.1 %collective-permute-start.8 = (f32[3,40,128]{2,1,0:T(8,128)S(1)}, f32[3,40,128]{2,1,0:T(8,128)S(1)}, u32[]{:S(2)}, u32[]{:S(2)}) collective-permute-start(f32[3,40,128]{2,1,0:T(8,128)S(1)} %get-tuple-element.55), channel_id=1, source_target_pairs={{8,16},{24,32},{40,48},{56,64},{72,80},{88,96},{104,112},{16,8},{3... | collective-permute-start | bytes 184328 | tf_op jit(solution)/shard_map/ppermute | solution.py:33
  62.8 12.3 %collective-permute-start.12 = (f32[3,4,32,128]{3,2,1,0:T(8,128)S(1)}, f32[3,4,32,128]{3,2,1,0:T(8,128)S(1)}, u32[]{:S(2)}, u32[]{:S(2)}) collective-permute-start(f32[3,4,32,128]{3,2,1,0:T(8,128)S(1)} %get-tuple-element.56.refs_0_), channel_id=1, source_target_pairs={{0,3},{1,2},{2,5},{3,4},{4,7},{5,6},{6,1},{7,0},{8,11},{9,10},{10,... | collective-permute-start | bytes 589832 | tf_op jit(solution)/shard_map/ppermute | solution.py:1051
  66.0 9.0 %collective-permute-start.13 = (f32[3,4,32,128]{3,2,1,0:T(8,128)S(1)}, f32[3,4,32,128]{3,2,1,0:T(8,128)S(1)}, u32[]{:S(2)}, u32[]{:S(2)}) collective-permute-start(f32[3,4,32,128]{3,2,1,0:T(8,128)S(1)} %get-tuple-element.56.refs_0_), channel_id=1, source_target_pairs={{0,6},{1,7},{2,0},{3,1},{4,2},{5,3},{6,4},{7,5},{8,14},{9,15},{10,... | collective-permute-start | bytes 589832 | tf_op jit(solution)/shard_map/ppermute | solution.py:1045
  68.1 7.0 %collective-permute-start.14 = (f32[3,4,32,128]{3,2,1,0:T(8,128)S(1)}, f32[3,4,32,128]{3,2,1,0:T(8,128)S(1)}, u32[]{:S(2)}, u32[]{:S(2)}) collective-permute-start(f32[3,4,32,128]{3,2,1,0:T(8,128)S(1)} %get-tuple-element.56.refs_0_), channel_id=1, source_target_pairs={{0,1},{1,0},{2,3},{3,2},{4,5},{5,4},{6,7},{7,6},{8,9},{9,8},{10,11... | collective-permute-start | bytes 589832 | tf_op jit(solution)/shard_map/ppermute | solution.py:27
  68.4 7.6 %collective-permute-start.15 = (f32[3,4,32,128]{3,2,1,0:T(8,128)S(1)}, f32[3,4,32,128]{3,2,1,0:T(8,128)S(1)}, u32[]{:S(2)}, u32[]{:S(2)}) collective-permute-start(f32[3,4,32,128]{3,2,1,0:T(8,128)S(1)} %collective-permute-done.9.refs_4_), channel_id=1, source_target_pairs={{0,2},{1,3},{2,4},{3,5},{4,6},{5,7},{6,0},{7,1},{8,10},{9,11},{10,... | collective-permute-start | bytes 589832 | tf_op jit(solution)/shard_map/ppermute | solution.py:1045
  68.8 7.2 %collective-permute-start.16 = (f32[3,4,32,128]{3,2,1,0:T(8,128)S(1)}, f32[3,4,32,128]{3,2,1,0:T(8,128)S(1)}, u32[]{:S(2)}, u32[]{:S(2)}) collective-permute-start(f32[3,4,32,128]{3,2,1,0:T(8,128)S(1)} %collective-permute-done.10.refs_5_), channel_id=1, source_target_pairs={{0,6},{1,7},{2,0},{3,1},{4,2},{5,3},{6,4},{7,5},{8,14},{9,15},{10,... | collective-permute-start | bytes 589832 | tf_op jit(solution)/shard_map/ppermute | solution.py:1045
  (2 other events, 7.0 us)

commit v4 on v3

--- a/solution.py
+++ b/solution.py
@@ -149,8 +149,7 @@
                     out[h, 3 * k : 3 * k + 3, :] = u[c, x, u_rows, lanes]
                     base = 9 * width + 2 * k
                     out[h, base : base + 2, :] = b[c, x, two, lanes]
-                base = 15 * width + 2 * x
-                out[h, base : base + 2, :] = s[x, two, lanes]
+            out[h, 15 * width :, :] = jnp.concatenate([s[x, two, lanes] for x in range(width)], axis=0)
 
     even = is_even("narrow")
 
@@ -284,6 +283,7 @@
         two = slice(at - 2, at) if low else slice(at + SUB, at + SUB + 2)
         for h in range(2):
             lanes = slice(h * LANES, (h + 1) * LANES)
+            coefficient = halo[h, 15 * width :, :]
             for x in range(width):
                 for c in range(3):
                     k = c * width + x
@@ -293,8 +293,7 @@
                     base = 9 * width + 2 * k
                     be[e, c, x, h, two, :] = halo[h, base : base + 2, :]
                 se[e, x, h, at : at + SUB, :] = s[x, :, lanes]
-                base = 15 * width + 2 * x
-                se[e, x, h, two, :] = halo[h, base : base + 2, :]
+                se[e, x, h, two, :] = coefficient[2 * x : 2 * x + 2, :]
 
     even = is_even("narrow")
 
@@ -472,7 +471,7 @@
             before, here = here, after
         return carry
 
-    lax.fori_loop(0, (height + 2 * RIM) // SUB, first_step, 0, unroll=3)
+    lax.fori_loop(0, (height + 2 * RIM) // SUB, first_step, 0, unroll=9)
 
     def second_step(t, carry):
         start = PAD + RIM + t * SUB
@@ -492,7 +491,7 @@
             before, here = here, after
         return carry
 
-    lax.fori_loop(0, height // SUB, second_step, 0, unroll=2)
+    lax.fori_loop(0, height // SUB, second_step, 0, unroll=4)
 
 
 def inner(bounds, r0p, s_win, r_end, s_end):
@@ -591,7 +590,7 @@
                 r0(c, width + 1)[h, rows, :] = right[3 + c, h, rows, :]
         return carry
 
-    lax.fori_loop(0, tiles, fix, 0, unroll=3)
+    lax.fori_loop(0, tiles, fix, 0, unroll=9)
 
     def first_step(t, carry):
         start = PAD + t * SUB
@@ -619,7 +618,7 @@
                 before, here = here, after
         return carry
 
-    lax.fori_loop(0, tiles, first_step, 0, unroll=3)
+    lax.fori_loop(0, tiles, first_step, 0, unroll=9)
 
     def second_step(t, carry):
         start = PAD + RIM + t * SUB
@@ -648,7 +647,7 @@
         return carry
 
     guess_copy.wait()
-    lax.fori_loop(0, height // SUB, second_step, 0, unroll=2)
+    lax.fori_loop(0, height // SUB, second_step, 0, unroll=4)
 
     coarse_width = width // 2
     coarse_height = height // 2
@@ -766,11 +765,14 @@
     q[...] = partial[...]
 
     def join(low, high):
+        spare = jnp.zeros((SUB - 5, LANES), F32)
         for c in range(3):
             for i in range(planes):
                 k = 5 * (c * planes + i)
-                q[c, i, 0:5, :] = partial[c, i, 0:5, :] + low[k : k + 5, :]
-                q[c, i, rows - 5 :, :] = partial[c, i, rows - 5 :, :] + high[k : k + 5, :]
+                q[c, i, 0:SUB, :] = partial[c, i, 0:SUB, :] + jnp.concatenate([low[k : k + 5, :], spare], axis=0)
+                q[c, i, rows - SUB :, :] = partial[c, i, rows - SUB :, :] + jnp.concatenate(
+                    [spare, high[k : k + 5, :]], axis=0
+                )
 
     @pl.when(even_y)
     def _():
@@ -785,9 +787,14 @@
     before = pl.multiple_of(jnp.maximum(start - SUB, 0), SUB)
     after = pl.multiple_of(jnp.minimum(start + own, total - SUB), SUB)
     for x in range(coarse_width):
-        s_win[x, RIM : RIM + own, :] = s[x, pl.ds(start, own), :]
-        s_win[x, 0:RIM, :] = s[x, pl.ds(before, SUB), :][SUB - RIM :, :]
-        s_win[x, RIM + own :, :] = s[x, pl.ds(after, SUB), :][0:RIM, :]
+        s_win[x] = jnp.concatenate(
+            [
+                s[x, pl.ds(before, SUB), :][SUB - RIM :, :],
+                s[x, pl.ds(start, own), :],
+                s[x, pl.ds(after, SUB), :][0:RIM, :],
+            ],
+            axis=0,
+        )
 
     def pack(out, to_left):
         first = 0 if to_left else 2

time: 77.8 us -> 77.5 us (level)
  no operation moved by 1% of the time
where the time goes in v4:
time: 77.5 us; the launch traced here: 76.9 us
  starting transfers between devices  35.6 us (46%)
  Pallas kernels  21.1 us (27%)
  waiting for transfers between devices  19.1 us (25%)
  between operations  0.85 us (1%)
    ppermute x5, waiting for transfers between devices, swap_far(): return lax.ppermute(x, axis, up + [(j, i) for i, j in up])  16.3 us
    ppermute x5, starting transfers between devices, swap_far(): return lax.ppermute(x, axis, up + [(j, i) for i, j in up])  12.9 us
    ppermute x4, starting transfers between devices, ring(): lax.ppermute(x, 'narrow', [(i, (i + by) % count) for i in range(count)])  7.92 us
    ppermute x6, starting transfers between devices, swap_near(): return lax.ppermute(x, axis, [(i, i ^ 1) for i in range(count)])  7.61 us
    ppermute x2, starting transfers between devices, across(): lax.ppermute(x, 'narrow', [(i, (i + by) % count ^ 1) for i in range(count)])  7.14 us
    pallas_call x1, Pallas kernels, smoothing(): pl.pallas_call(smooth_kernel, in_specs=[SMEM, SMEM, ANY] + [VMEM] * 11, o...  5.61 us
    pallas_call x1, Pallas kernels, prolong(): pl.pallas_call(prolong_kernel, in_specs=[SMEM] + [VMEM] * 6, out_shape=ja...  3.36 us
    pallas_call x1, Pallas kernels, inner(): pl.pallas_call(inner_kernel, in_specs=[SMEM] + [ANY] * 4, out_shape=[jax....  3.33 us
  transfers between devices with their start and end apart: 17, of which 6 were waited for; matrix products, arithmetic and copies ran while one was open for 0% of the time, Pallas kernels for 13%

profile of v4, /device:TPU:16, one launch (start us, length us, event | category | flops | bytes accessed | tf_op | source)
XLA Modules:
  0.0 76.9 jit_solution(1273585008871929243)
XLA Ops:
  0.7 1.5 %pack_y.1 = (f32[2,136,128]{2,1,0:T(8,128)S(1)}, f32[2,136,128]{2,1,0:T(8,128)S(1)}) custom-call(f32[3,8,64,256]{3,2,1,0:T(8,128)} %guess.1, f32[3,8,64,256]{3,2,1,0:T(8,128)} %guess.1, f32[3,8,64,256]{3,2,1,0:T(8,128)} %refs_3_.1, f32[3,8,64,256]{3,2,1,0:T(8,128)} %refs_3_.1, f32[8,64,256]{2,1,0:T(8,128)} %refs_5_.1, f32[8,64,256]{2,1,0:T(8,128)} %refs_5_.1), custom_call_target="tpu_custom_call" | custom-call | bytes 3690000 | tf_op jit(solution)/shard_map/pack_y/pallas_call | solution.py:177
  2.1 1.4 %collective-permute-start = (f32[2,136,128]{2,1,0:T(8,128)S(1)}, f32[2,136,128]{2,1,0:T(8,128)S(1)}, u32[]{:S(2)}, u32[]{:S(2)}) collective-permute-start(f32[2,136,128]{2,1,0:T(8,128)S(1)} %get-tuple-element.34), channel_id=1, source_target_pairs={{0,1},{1,0},{2,3},{3,2},{4,5},{5,4},{6,7},{7,6},{8,9},{9,8},{10,11... | collective-permute-start | bytes 417800 | tf_op jit(solution)/shard_map/ppermute | solution.py:27
  3.5 0.7 collective-permute-start.1
  4.2 3.1 %residual.1 = (f32[3,8,2,72,128]{4,3,2,1,0:T(8,128)}, f32[8,2,72,128]{3,2,1,0:T(8,128)}, f32[10,2,64,128]{3,2,1,0:T(8,128)S(1)}, f32[10,2,64,128]{3,2,1,0:T(8,128)S(1)}) custom-call(f32[3,8,64,256]{3,2,1,0:T(8,128)S(1)} %copy-done, f32[3,8,64,256]{3,2,1,0:T(8,128)S(1)} %copy-done.1, f32[8,64,256]{2,1,0:T(8,128)S(1)} %copy-done.2), custom_call_target="tpu_custom_call" | custom-call | bytes 11070000 | tf_op jit(solution)/shard_map/residual/pallas_call | solution.py:257
  7.6 1.3 %ends.1 = (f32[2,3,8,2,8,128]{5,4,3,2,1,0:T(8,128)}, f32[2,8,2,8,128]{4,3,2,1,0:T(8,128)}, f32[10,2,72,128]{3,2,1,0:T(8,128)S(1)}, f32[10,2,72,128]{3,2,1,0:T(8,128)S(1)}) custom-call(f32[3,8,64,256]{3,2,1,0:T(8,128)S(1)} %copy-done, f32[3,8,64,256]{3,2,1,0:T(8,128)S(1)} %copy-done, f32[3,8,64,256]{3,2,1,0:T(8,128)S(1)} %copy-done.1, ...), custom_call_target="tpu_custom_call" | custom-call | bytes 147600000 | tf_op jit(solution)/shard_map/ends/pallas_call | solution.py:376
  9.0 4.5 %collective-permute-start.3 = (f32[10,2,72,128]{3,2,1,0:T(8,128)S(1)}, f32[10,2,72,128]{3,2,1,0:T(8,128)}, u32[]{:S(2)}, u32[]{:S(2)}) collective-permute-start(f32[10,2,72,128]{3,2,1,0:T(8,128)S(1)} %get-tuple-element.46.sent_far), channel_id=1, source_target_pairs={{8,16},{24,32},{40,48},{56,64},{72,80},{88,96},{104,112},{16,8},{3... | collective-permute-start | bytes 2211848 | tf_op jit(solution)/shard_map/ppermute | solution.py:33
  13.8 3.3 %inner.1 = (f32[3,8,2,88,128]{4,3,2,1,0:T(8,128)S(1)}, f32[8,2,88,128]{3,2,1,0:T(8,128)S(1)}, f32[3,4,2,88,128]{4,3,2,1,0:T(8,128)S(1)}, f32[3,4,2,88,128]{4,3,2,1,0:T(8,128)S(1)}, f32[3,2,2,64,128]{4,3,2,1,0:T(8,128)S(1)}) custom-call(f32[2]{0:T(128)S(1)} %copy-done.5, f32[3,8,2,72,128]{4,3,2,1,0:T(8,128)} %get-tuple-element.32.r0p, ...), custom_call_target="tpu_custom_call" | custom-call | bytes 18450000 | tf_op jit(solution)/shard_map/inner/pallas_call | solution.py:502
  17.2 8.3 %collective-permute-done.3.got_far = f32[10,2,72,128]{3,2,1,0:T(8,128)} collective-permute-done((f32[10,2,72,128]{3,2,1,0:T(8,128)S(1)}, f32[10,2,72,128]{3,2,1,0:T(8,128)}, u32[]{:S(2)}, u32[]{:S(2)}) %collective-permute-start.3) | collective-permute-done | bytes 737312 | tf_op jit(solution)/shard_map/ppermute | solution.py:33
  25.5 5.6 %smoothing.1 = (f32[3,8,64,256]{3,2,1,0:T(8,128)S(1)}, f32[3,6,40,128]{3,2,1,0:T(8,128)S(1)}, f32[96,128]{1,0:T(8,128)S(1)}, f32[96,128]{1,0:T(8,128)S(1)}) custom-call(f32[2]{0:T(128)S(1)} %copy-done.5, f32[66,5]{1,0:T(8,128)S(1)} %pad.8.rest_x, f32[3,8,64,256]{3,2,1,0:T(8,128)S(1)} %copy-done, f32[3,8,2,88,128]{4,3,2,1,0:T(8,128)S(1)} %get-tuple-element.40.r0_own, ...), custom_call_target="tpu_custom_call" | custom-call | bytes 36900000 | tf_op jit(solution)/shard_map/smoothing/pallas_call | solution.py:730
  31.1 5.8 %collective-permute-start.4 = (f32[96,128]{1,0:T(8,128)S(1)}, f32[96,128]{1,0:T(8,128)S(1)}, u32[]{:S(2)}, u32[]{:S(2)}) collective-permute-start(f32[96,128]{1,0:T(8,128)S(1)} %get-tuple-element.48), channel_id=1, source_target_pairs={{0,1},{1,0},{2,3},{3,2},{4,5},{5,4},{6,7},{7,6},{8,9},{9,8},{10,11... | collective-permute-start | bytes 147464 | tf_op jit(solution)/shard_map/ppermute | solution.py:27
  36.9 0.7 collective-permute-start.5
  37.5 1.4 %collective-permute-done.4.got_near = f32[96,128]{1,0:T(8,128)S(1)} collective-permute-done((f32[96,128]{1,0:T(8,128)S(1)}, f32[96,128]{1,0:T(8,128)S(1)}, u32[]{:S(2)}, u32[]{:S(2)}) %collective-permute-start.4) | collective-permute-done | bytes 49184 | tf_op jit(solution)/shard_map/ppermute | solution.py:27
  39.2 4.0 %collective-permute-start.7 = (f32[14,40,128]{2,1,0:T(8,128)S(1)}, f32[14,40,128]{2,1,0:T(8,128)S(1)}, u32[]{:S(2)}, u32[]{:S(2)}) collective-permute-start(f32[14,40,128]{2,1,0:T(8,128)S(1)} %get-tuple-element.53), channel_id=1, source_target_pairs={{8,16},{24,32},{40,48},{56,64},{72,80},{88,96},{104,112},{16,8},{3... | collective-permute-start | bytes 860168 | tf_op jit(solution)/shard_map/ppermute | solution.py:33
  43.2 7.6 %collective-permute-done.7.got_far = f32[14,40,128]{2,1,0:T(8,128)S(1)} collective-permute-done((f32[14,40,128]{2,1,0:T(8,128)S(1)}, f32[14,40,128]{2,1,0:T(8,128)S(1)}, u32[]{:S(2)}, u32[]{:S(2)}) %collective-permute-start.7) | collective-permute-done | bytes 286752 | tf_op jit(solution)/shard_map/ppermute | solution.py:33
  50.8 1.6 %coarse_solve.1 = (f32[3,4,40,128]{3,2,1,0:T(8,128)S(1)}, f32[3,4,32,128]{3,2,1,0:T(8,128)S(1)}, f32[3,40,128]{2,1,0:T(8,128)S(1)}, f32[3,40,128]{2,1,0:T(8,128)S(1)}) custom-call(f32[2]{0:T(128)S(1)} %copy-done.6, f32[3,6,40,128]{3,2,1,0:T(8,128)S(1)} %get-tuple-element.50.q, f32[4,40,128]{2,1,0:T(8,128)S(1)} %get-tuple-element.51.s_win, ...), custom_call_target="tpu_custom_call" | custom-call | bytes 11070000 | tf_op jit(solution)/shard_map/coarse_solve/pallas_call | solution.py:960
  52.4 3.9 %collective-permute-start.10 = (f32[3,4,32,128]{3,2,1,0:T(8,128)S(1)}, f32[3,4,32,128]{3,2,1,0:T(8,128)S(1)}, u32[]{:S(2)}, u32[]{:S(2)}) collective-permute-start(f32[3,4,32,128]{3,2,1,0:T(8,128)S(1)} %get-tuple-element.56.refs_0_), channel_id=1, source_target_pairs={{0,7},{1,6},{2,1},{3,0},{4,3},{5,2},{6,5},{7,4},{8,15},{9,14},{10,... | collective-permute-start | bytes 589832 | tf_op jit(solution)/shard_map/ppermute | solution.py:1058
  56.3 3.0 %collective-permute-start.9 = (f32[3,4,32,128]{3,2,1,0:T(8,128)S(1)}, f32[3,4,32,128]{3,2,1,0:T(8,128)S(1)}, u32[]{:S(2)}, u32[]{:S(2)}) collective-permute-start(f32[3,4,32,128]{3,2,1,0:T(8,128)S(1)} %get-tuple-element.56.refs_0_), channel_id=1, source_target_pairs={{0,2},{1,3},{2,4},{3,5},{4,6},{5,7},{6,0},{7,1},{8,10},{9,11},{10,... | collective-permute-start | bytes 589832 | tf_op jit(solution)/shard_map/ppermute | solution.py:1052
  59.3 3.1 %collective-permute-start.8 = (f32[3,40,128]{2,1,0:T(8,128)S(1)}, f32[3,40,128]{2,1,0:T(8,128)S(1)}, u32[]{:S(2)}, u32[]{:S(2)}) collective-permute-start(f32[3,40,128]{2,1,0:T(8,128)S(1)} %get-tuple-element.55), channel_id=1, source_target_pairs={{8,16},{24,32},{40,48},{56,64},{72,80},{88,96},{104,112},{16,8},{3... | collective-permute-start | bytes 184328 | tf_op jit(solution)/shard_map/ppermute | solution.py:33
  62.4 3.2 %collective-permute-start.12 = (f32[3,4,32,128]{3,2,1,0:T(8,128)S(1)}, f32[3,4,32,128]{3,2,1,0:T(8,128)S(1)}, u32[]{:S(2)}, u32[]{:S(2)}) collective-permute-start(f32[3,4,32,128]{3,2,1,0:T(8,128)S(1)} %get-tuple-element.56.refs_0_), channel_id=1, source_target_pairs={{0,3},{1,2},{2,5},{3,4},{4,7},{5,6},{6,1},{7,0},{8,11},{9,10},{10,... | collective-permute-start | bytes 589832 | tf_op jit(solution)/shard_map/ppermute | solution.py:1058
  65.7 2.0 %collective-permute-start.13 = (f32[3,4,32,128]{3,2,1,0:T(8,128)S(1)}, f32[3,4,32,128]{3,2,1,0:T(8,128)S(1)}, u32[]{:S(2)}, u32[]{:S(2)}) collective-permute-start(f32[3,4,32,128]{3,2,1,0:T(8,128)S(1)} %get-tuple-element.56.refs_0_), channel_id=1, source_target_pairs={{0,6},{1,7},{2,0},{3,1},{4,2},{5,3},{6,4},{7,5},{8,14},{9,15},{10,... | collective-permute-start | bytes 589832 | tf_op jit(solution)/shard_map/ppermute | solution.py:1052
  68.5 2.9 %collective-permute-start.16 = (f32[3,4,32,128]{3,2,1,0:T(8,128)S(1)}, f32[3,4,32,128]{3,2,1,0:T(8,128)S(1)}, u32[]{:S(2)}, u32[]{:S(2)}) collective-permute-start(f32[3,4,32,128]{3,2,1,0:T(8,128)S(1)} %collective-permute-done.10.refs_5_), channel_id=1, source_target_pairs={{0,6},{1,7},{2,0},{3,1},{4,2},{5,3},{6,4},{7,5},{8,14},{9,15},{10,... | collective-permute-start | bytes 589832 | tf_op jit(solution)/shard_map/ppermute | solution.py:1052
  71.3 3.4 %prolong.1 = f32[3,8,64,256]{3,2,1,0:T(8,128)} custom-call(f32[66,5]{1,0:T(8,128)S(1)} %pad.8.rest_x, f32[3,4,40,128]{3,2,1,0:T(8,128)S(1)} %get-tuple-element.54.corr, f32[3,40,128]{2,1,0:T(8,128)S(1)} %collective-permute-done.8.got_far, f32[3,40,128]{2,1,0:T(8,128)S(1)} %collective-permute-done.11.got_near, ...), custom_call_target="tpu_custom_call" | custom-call | bytes 44280000 | tf_op jit(solution)/shard_map/prolong/pallas_call | solution.py:1031
  74.7 1.0 %collective-permute-done.15.refs_6_ = f32[3,4,32,128]{3,2,1,0:T(8,128)S(1)} collective-permute-done((f32[3,4,32,128]{3,2,1,0:T(8,128)S(1)}, f32[3,4,32,128]{3,2,1,0:T(8,128)S(1)}, u32[]{:S(2)}, u32[]{:S(2)}) %collective-permute-start.15) | collective-permute-done | bytes 196640 | tf_op jit(solution)/shard_map/ppermute | solution.py:1052
  75.7 1.2 %assemble.1 = f32[3,4,256,128]{3,2,1,0:T(8,128)} custom-call(f32[3,4,32,128]{3,2,1,0:T(8,128)S(1)} %get-tuple-element.56.refs_0_, f32[3,4,32,128]{3,2,1,0:T(8,128)S(1)} %collective-permute-done.12.refs_1_, f32[3,4,32,128]{3,2,1,0:T(8,128)S(1)} %collective-permute-done.13.refs_2_, f32[3,4,32,128]{3,2,1,0:T(8,128)S(1)} %collective-permute-done.14.refs_3_, ...), custom_call_target="tpu_custom_call" | custom-call | bytes 3690000 | tf_op jit(solution)/shard_map/assemble/pallas_call | solution.py:1087
  (41 shorter events, 1.6 us)
Async XLA Ops:
  0.6 3.5 %copy-start = (f32[3,8,64,256]{3,2,1,0:T(8,128)S(1)}, f32[3,8,64,256]{3,2,1,0:T(8,128)}, u32[]{:S(2)}) copy-start(f32[3,8,64,256]{3,2,1,0:T(8,128)} %guess.1) | copy-start | bytes 4718596
  2.1 5.5 %collective-permute-start = (f32[2,136,128]{2,1,0:T(8,128)S(1)}, f32[2,136,128]{2,1,0:T(8,128)S(1)}, u32[]{:S(2)}, u32[]{:S(2)}) collective-permute-start(f32[2,136,128]{2,1,0:T(8,128)S(1)} %get-tuple-element.34), channel_id=1, source_target_pairs={{0,1},{1,0},{2,3},{3,2},{4,5},{5,4},{6,7},{7,6},{8,9},{9,8},{10,11... | collective-permute-start | bytes 417800 | tf_op jit(solution)/shard_map/ppermute | solution.py:27
  3.5 4.1 %collective-permute-start.1 = (f32[2,136,128]{2,1,0:T(8,128)S(1)}, f32[2,136,128]{2,1,0:T(8,128)S(1)}, u32[]{:S(2)}, u32[]{:S(2)}) collective-permute-start(f32[2,136,128]{2,1,0:T(8,128)S(1)} %get-tuple-element.35), channel_id=1, source_target_pairs={{1,2},{3,4},{5,6},{2,1},{4,3},{6,5},{9,10},{11,12},{13,14},{10,9},... | collective-permute-start | bytes 417800 | tf_op jit(solution)/shard_map/ppermute | solution.py:33
  7.6 5.9 %copy-start.7 = (f32[256,5]{0,1:T(8,128)S(1)}, f32[256,5]{0,1:T(8,128)}, u32[]{:S(2)}) copy-start(f32[256,5]{0,1:T(8,128)} %param.14) | copy-start | bytes 15364
  7.6 6.1 %copy-start.8 = (f32[64,5]{0,1:T(8,128)S(1)}, f32[64,5]{0,1:T(8,128)}, u32[]{:S(2)}) copy-start(f32[64,5]{0,1:T(8,128)} %param.13) | copy-start | bytes 3844
  7.6 6.2 %copy-start.5 = (f32[2]{0:T(128)S(1)}, f32[2]{0:T(128)}, u32[]{:S(2)}) copy-start(f32[2]{0:T(128)} %bounds.4) | copy-start | bytes 28
  9.0 8.2 %collective-permute-start.2 = (f32[10,2,72,128]{3,2,1,0:T(8,128)S(1)}, f32[10,2,72,128]{3,2,1,0:T(8,128)}, u32[]{:S(2)}, u32[]{:S(2)}) collective-permute-start(f32[10,2,72,128]{3,2,1,0:T(8,128)S(1)} %get-tuple-element.45.sent_near), channel_id=1, source_target_pairs={{0,8},{8,0},{16,24},{24,16},{32,40},{40,32},{48,56},{56,48},{64,72... | collective-permute-start | bytes 2211848 | tf_op jit(solution)/shard_map/ppermute | solution.py:27
  9.0 16.5 %collective-permute-start.3 = (f32[10,2,72,128]{3,2,1,0:T(8,128)S(1)}, f32[10,2,72,128]{3,2,1,0:T(8,128)}, u32[]{:S(2)}, u32[]{:S(2)}) collective-permute-start(f32[10,2,72,128]{3,2,1,0:T(8,128)S(1)} %get-tuple-element.46.sent_far), channel_id=1, source_target_pairs={{8,16},{24,32},{40,48},{56,64},{72,80},{88,96},{104,112},{16,8},{3... | collective-permute-start | bytes 2211848 | tf_op jit(solution)/shard_map/ppermute | solution.py:33
  13.8 11.7 %copy-start.4 = (f32[128,5]{0,1:T(8,128)S(1)}, f32[128,5]{0,1:T(8,128)}, u32[]{:S(2)}) copy-start(f32[128,5]{0,1:T(8,128)} %param.15) | copy-start | bytes 7684
  25.5 13.5 %copy-start.3 = (f32[4,256,128]{2,1,0:T(8,128)S(1)}, f32[4,256,128]{2,1,0:T(8,128)}, u32[]{:S(2)}) copy-start(f32[4,256,128]{2,1,0:T(8,128)} %s.3) | copy-start | bytes 1572868
  25.5 25.3 %copy-start.6 = (f32[2]{0:T(128)S(1)}, f32[2]{0:T(128)}, u32[]{:S(2)}) copy-start(f32[2]{0:T(128)} %bounds.5) | copy-start | bytes 28
  31.1 7.9 %collective-permute-start.4 = (f32[96,128]{1,0:T(8,128)S(1)}, f32[96,128]{1,0:T(8,128)S(1)}, u32[]{:S(2)}, u32[]{:S(2)}) collective-permute-start(f32[96,128]{1,0:T(8,128)S(1)} %get-tuple-element.48), channel_id=1, source_target_pairs={{0,1},{1,0},{2,3},{3,2},{4,5},{5,4},{6,7},{7,6},{8,9},{9,8},{10,11... | collective-permute-start | bytes 147464 | tf_op jit(solution)/shard_map/ppermute | solution.py:27
  36.9 2.1 %collective-permute-start.5 = (f32[96,128]{1,0:T(8,128)S(1)}, f32[96,128]{1,0:T(8,128)S(1)}, u32[]{:S(2)}, u32[]{:S(2)}) collective-permute-start(f32[96,128]{1,0:T(8,128)S(1)} %get-tuple-element.49), channel_id=1, source_target_pairs={{1,2},{3,4},{5,6},{2,1},{4,3},{6,5},{9,10},{11,12},{13,14},{10,9},... | collective-permute-start | bytes 147464 | tf_op jit(solution)/shard_map/ppermute | solution.py:33
  39.1 4.1 %collective-permute-start.6 = (f32[14,40,128]{2,1,0:T(8,128)S(1)}, f32[14,40,128]{2,1,0:T(8,128)S(1)}, u32[]{:S(2)}, u32[]{:S(2)}) collective-permute-start(f32[14,40,128]{2,1,0:T(8,128)S(1)} %get-tuple-element.52), channel_id=1, source_target_pairs={{0,8},{8,0},{16,24},{24,16},{32,40},{40,32},{48,56},{56,48},{64,72... | collective-permute-start | bytes 860168 | tf_op jit(solution)/shard_map/ppermute | solution.py:27
  39.2 11.6 %collective-permute-start.7 = (f32[14,40,128]{2,1,0:T(8,128)S(1)}, f32[14,40,128]{2,1,0:T(8,128)S(1)}, u32[]{:S(2)}, u32[]{:S(2)}) collective-permute-start(f32[14,40,128]{2,1,0:T(8,128)S(1)} %get-tuple-element.53), channel_id=1, source_target_pairs={{8,16},{24,32},{40,48},{56,64},{72,80},{88,96},{104,112},{16,8},{3... | collective-permute-start | bytes 860168 | tf_op jit(solution)/shard_map/ppermute | solution.py:33
  52.4 15.3 %collective-permute-start.10 = (f32[3,4,32,128]{3,2,1,0:T(8,128)S(1)}, f32[3,4,32,128]{3,2,1,0:T(8,128)S(1)}, u32[]{:S(2)}, u32[]{:S(2)}) collective-permute-start(f32[3,4,32,128]{3,2,1,0:T(8,128)S(1)} %get-tuple-element.56.refs_0_), channel_id=1, source_target_pairs={{0,7},{1,6},{2,1},{3,0},{4,3},{5,2},{6,5},{7,4},{8,15},{9,14},{10,... | collective-permute-start | bytes 589832 | tf_op jit(solution)/shard_map/ppermute | solution.py:1058
  56.3 11.8 %collective-permute-start.9 = (f32[3,4,32,128]{3,2,1,0:T(8,128)S(1)}, f32[3,4,32,128]{3,2,1,0:T(8,128)S(1)}, u32[]{:S(2)}, u32[]{:S(2)}) collective-permute-start(f32[3,4,32,128]{3,2,1,0:T(8,128)S(1)} %get-tuple-element.56.refs_0_), channel_id=1, source_target_pairs={{0,2},{1,3},{2,4},{3,5},{4,6},{5,7},{6,0},{7,1},{8,10},{9,11},{10,... | collective-permute-start | bytes 589832 | tf_op jit(solution)/shard_map/ppermute | solution.py:1052
  59.3 6.3 %collective-permute-start.11 = (f32[3,40,128]{2,1,0:T(8,128)S(1)}, f32[3,40,128]{2,1,0:T(8,128)S(1)}, u32[]{:S(2)}, u32[]{:S(2)}) collective-permute-start(f32[3,40,128]{2,1,0:T(8,128)S(1)} %get-tuple-element.57), channel_id=1, source_target_pairs={{0,8},{8,0},{16,24},{24,16},{32,40},{40,32},{48,56},{56,48},{64,72... | collective-permute-start | bytes 184328 | tf_op jit(solution)/shard_map/ppermute | solution.py:27
  59.3 9.1 %collective-permute-start.8 = (f32[3,40,128]{2,1,0:T(8,128)S(1)}, f32[3,40,128]{2,1,0:T(8,128)S(1)}, u32[]{:S(2)}, u32[]{:S(2)}) collective-permute-start(f32[3,40,128]{2,1,0:T(8,128)S(1)} %get-tuple-element.55), channel_id=1, source_target_pairs={{8,16},{24,32},{40,48},{56,64},{72,80},{88,96},{104,112},{16,8},{3... | collective-permute-start | bytes 184328 | tf_op jit(solution)/shard_map/ppermute | solution.py:33
  62.4 12.3 %collective-permute-start.12 = (f32[3,4,32,128]{3,2,1,0:T(8,128)S(1)}, f32[3,4,32,128]{3,2,1,0:T(8,128)S(1)}, u32[]{:S(2)}, u32[]{:S(2)}) collective-permute-start(f32[3,4,32,128]{3,2,1,0:T(8,128)S(1)} %get-tuple-element.56.refs_0_), channel_id=1, source_target_pairs={{0,3},{1,2},{2,5},{3,4},{4,7},{5,6},{6,1},{7,0},{8,11},{9,10},{10,... | collective-permute-start | bytes 589832 | tf_op jit(solution)/shard_map/ppermute | solution.py:1058
  65.7 9.0 %collective-permute-start.13 = (f32[3,4,32,128]{3,2,1,0:T(8,128)S(1)}, f32[3,4,32,128]{3,2,1,0:T(8,128)S(1)}, u32[]{:S(2)}, u32[]{:S(2)}) collective-permute-start(f32[3,4,32,128]{3,2,1,0:T(8,128)S(1)} %get-tuple-element.56.refs_0_), channel_id=1, source_target_pairs={{0,6},{1,7},{2,0},{3,1},{4,2},{5,3},{6,4},{7,5},{8,14},{9,15},{10,... | collective-permute-start | bytes 589832 | tf_op jit(solution)/shard_map/ppermute | solution.py:1052
  67.7 7.0 %collective-permute-start.14 = (f32[3,4,32,128]{3,2,1,0:T(8,128)S(1)}, f32[3,4,32,128]{3,2,1,0:T(8,128)S(1)}, u32[]{:S(2)}, u32[]{:S(2)}) collective-permute-start(f32[3,4,32,128]{3,2,1,0:T(8,128)S(1)} %get-tuple-element.56.refs_0_), channel_id=1, source_target_pairs={{0,1},{1,0},{2,3},{3,2},{4,5},{5,4},{6,7},{7,6},{8,9},{9,8},{10,11... | collective-permute-start | bytes 589832 | tf_op jit(solution)/shard_map/ppermute | solution.py:27
  68.1 7.6 %collective-permute-start.15 = (f32[3,4,32,128]{3,2,1,0:T(8,128)S(1)}, f32[3,4,32,128]{3,2,1,0:T(8,128)S(1)}, u32[]{:S(2)}, u32[]{:S(2)}) collective-permute-start(f32[3,4,32,128]{3,2,1,0:T(8,128)S(1)} %collective-permute-done.9.refs_4_), channel_id=1, source_target_pairs={{0,2},{1,3},{2,4},{3,5},{4,6},{5,7},{6,0},{7,1},{8,10},{9,11},{10,... | collective-permute-start | bytes 589832 | tf_op jit(solution)/shard_map/ppermute | solution.py:1052
  68.5 7.2 %collective-permute-start.16 = (f32[3,4,32,128]{3,2,1,0:T(8,128)S(1)}, f32[3,4,32,128]{3,2,1,0:T(8,128)S(1)}, u32[]{:S(2)}, u32[]{:S(2)}) collective-permute-start(f32[3,4,32,128]{3,2,1,0:T(8,128)S(1)} %collective-permute-done.10.refs_5_), channel_id=1, source_target_pairs={{0,6},{1,7},{2,0},{3,1},{4,2},{5,3},{6,4},{7,5},{8,14},{9,15},{10,... | collective-permute-start | bytes 589832 | tf_op jit(solution)/shard_map/ppermute | solution.py:1052
  (2 other events, 7.0 us)
